TPU v7x, 32 devices: a whole 2x2x4 slice. The times are simulated.
32 devices in a mesh: kgrp: 2 (over y), orb: 16 (over z, x, core).
Axes of the slice: x: 2, y: 2, z: 4, core: 2. Of those that a mesh axis runs over, the one named last changes fastest.
Arguments:
- hopping_tiles: bfloat16 [32, 12, 96, 128], P('orb'), may hold values from -0.109375 to 0.109375
- tile_strip: int32 [32, 12, 1], replicated, may hold values from 0 to 15; in each aligned block of 24 rows (0 to 23, 24 to 47, ..., all dimensions but the last counted through in order) at most 2 rows name the same one
- tile_column_slot: int32 [32, 12], replicated, may hold values from 0 to 1
- lattice: int32 [32, 3], replicated, may hold values from -6 to 6
- kpoints: float32 [4, 3], P('kgrp'), parts along dimension 0, may hold values from 0 to 1
- start_block: bfloat16 [1536, 8192], P('orb'), may hold values from -6 to 6
Outputs:
- filtered: bfloat16 [4, 2, 1536, 8192], P('kgrp', None, 'orb'), parts along dimension 0
There are 2 independent parts, one for each index of `kgrp`. A program takes and returns all parts, laid end to end along the dimension named above; an argument that names none is the same for every part. Nothing has to cross between parts.
Inputs may be any that keep to these rules, and one draw needn't show every extreme that they name: `tile_strip`: among the 24 tiles of the lattice vectors r with the same r // 2 (one owner), no strip is named more than 2 times, and in every draw some strip is named exactly 2 times.
All inputs are finite; a program needn't handle non-finite values.
Results may differ from a plain program's by a relative error of at most 0.0065.
Values may be sent and summed in bfloat16 or wider, within the bound.
No kernel may reach another device: no remote copies, remote signals or barrier semaphores. Data moves between devices by JAX's collectives and lax.ppermute only.
A program may use at most 128 MiB of HBM per device.

v0:
```python
import jax
import jax.numpy as jnp
from jax import lax
from jax.sharding import PartitionSpec as P

HALO = 80
CAP = 2


def passed_along(value, axis, steps):
    count = lax.axis_size(axis)
    leading, last = (max(0, -steps), min(count, count - steps))
    return lax.ppermute(value, axis, [(source, source + steps) for source in range(leading, last)])


def phase_table(lattice, kpoints):
    cell_float = lattice.astype(jnp.float32)
    fraction = (
        kpoints[None, :, 0] * cell_float[:, None, 0]
        + kpoints[None, :, 1] * cell_float[:, None, 1]
        + kpoints[None, :, 2] * cell_float[:, None, 2]
    )
    radians = 6.283185307179586 * fraction
    return jnp.stack([jnp.cos(radians), jnp.sin(radians)], axis=-1).astype(jnp.bfloat16)


def send_order(own_dest, owners, slot_cap):
    tile_total = own_dest.shape[0]
    matched = (own_dest[:, None] == jnp.arange(owners, dtype=jnp.int32)[None, :]).astype(jnp.int32)
    earlier = jnp.cumsum(matched, axis=0) - matched
    order_rank = jnp.sum(earlier * matched, axis=1)
    position = own_dest * slot_cap + order_rank
    slot_ids = jnp.arange(owners * slot_cap, dtype=jnp.int32)
    placed = position[None, :] == slot_ids[:, None]
    source = jnp.sum(jnp.where(placed, jnp.arange(tile_total, dtype=jnp.int32)[None, :], 0), axis=1)
    filled = jnp.any(placed, axis=1)
    return (source, filled)


def receive_weights(dest_all, slot_all, phase_all, device, slot_cap, slot_count):
    owners = dest_all.shape[0]
    matched = (dest_all == device).astype(jnp.int32)
    order_rank = jnp.cumsum(matched, axis=1) - matched
    picked = (matched[:, None, :] == 1) & (
        order_rank[:, None, :] == jnp.arange(slot_cap, dtype=jnp.int32)[None, :, None]
    )
    column = (
        slot_all[:, :, None] == jnp.arange(slot_count, dtype=jnp.int32)[None, None, :]
    ).astype(jnp.float32)
    weights = jnp.einsum(
        "ocm,omkp,omj->ockpj",
        picked.astype(jnp.float32),
        phase_all,
        column,
        precision=lax.Precision.HIGHEST,
    )
    return weights.reshape(owners * slot_cap, -1).astype(jnp.bfloat16)


def pack_tiles(tile_block, own_dest, owners):
    source, filled = send_order(own_dest, owners, CAP)
    chosen = tile_block[source]
    return jnp.where(filled[:, None, None], chosen, jnp.zeros_like(chosen))


def local(hopping_tiles, tile_strip, tile_column_slot, lattice, kpoints, start_block):
    owners = lax.axis_size("orb")
    device = lax.axis_index("orb")
    step_count, tile_count, row_count, col_width = hopping_tiles.shape
    slot_count = (row_count + 2 * HALO) // col_width
    band_width = slot_count * col_width
    k_count = kpoints.shape[0]
    phases = lax.optimization_barrier(phase_table(lattice, kpoints)).astype(jnp.float32)
    dest_all = tile_strip[:, :, 0].reshape(owners, step_count, tile_count)
    slot_all = tile_column_slot.reshape(owners, step_count, tile_count)
    phase_all = jnp.broadcast_to(
        phases.reshape(owners, step_count, 1, k_count, 2),
        (owners, step_count, tile_count, k_count, 2),
    )
    own_dest = lax.dynamic_index_in_dim(dest_all, device, 0, keepdims=False)
    totals = jnp.zeros((k_count * 2 * slot_count, row_count * col_width), jnp.float32)
    for step_index in range(step_count):
        outgoing = pack_tiles(hopping_tiles[step_index], own_dest[step_index], owners)
        incoming = lax.all_to_all(outgoing, "orb", split_axis=0, concat_axis=0, tiled=True)
        weights = receive_weights(
            dest_all[:, step_index],
            slot_all[:, step_index],
            phase_all[:, step_index],
            device,
            CAP,
            slot_count,
        )
        totals = totals + jnp.dot(
            weights.T,
            incoming.reshape(owners * CAP, row_count * col_width),
            preferred_element_type=jnp.float32,
        )
    banded_hamiltonian = totals.reshape(k_count, 2, slot_count, row_count, col_width).transpose(
        0, 1, 3, 2, 4
    )
    banded_hamiltonian = banded_hamiltonian.reshape(k_count, 2, row_count, band_width).astype(
        jnp.bfloat16
    )
    shifted = {}
    for distance in (2, 1, -1, -2):
        shifted[distance] = passed_along(start_block, "orb", distance)
    rows_all = jnp.concatenate(
        [shifted[2], shifted[1], start_block, shifted[-1], shifted[-2]], axis=0
    )
    bands = {0: banded_hamiltonian}
    for distance in (1, -1):
        bands[distance] = passed_along(banded_hamiltonian, "orb", distance)

    def first_of(band, offset):
        window = lax.slice_in_dim(rows_all, offset, offset + band_width, axis=0)
        return jnp.einsum("kprb,bv->kprv", band, window, preferred_element_type=jnp.float32).astype(
            jnp.bfloat16
        )

    left_first = first_of(bands[1], row_count - HALO)
    own_first = first_of(bands[0], 2 * row_count - HALO)
    right_first = first_of(bands[-1], 3 * row_count - HALO)
    first_wide = jnp.concatenate(
        [left_first[:, :, row_count - HALO :], own_first, right_first[:, :, :HALO]], axis=2
    )
    product = jnp.einsum(
        "kprb,kqbv->kpqrv", banded_hamiltonian, first_wide, preferred_element_type=jnp.float32
    )
    real_part = 2.0 * (product[:, 0, 0] - product[:, 1, 1]) - start_block.astype(jnp.float32)[None]
    imag_part = 2.0 * (product[:, 0, 1] + product[:, 1, 0])
    return jnp.stack([real_part, imag_part], axis=1).astype(jnp.bfloat16)


def solution(mesh):
    return jax.shard_map(
        local,
        mesh=mesh,
        in_specs=(P("orb", None, None, None), P(), P(), P(), P("kgrp", None), P("orb", None)),
        out_specs=P("kgrp", None, "orb", None),
        check_vma=False,
    )
```

profile of v0, /device:TPU:11, one launch (start us, length us, event | category | flops | bytes accessed | tf_op | source)
XLA Modules:
  0.0 198.6 jit_solution(1716810783012256904)
XLA Ops:
  0.0 2.6 %collective-permute-start.3 = (bf16[96,8192]{1,0:T(8,128)(2,1)}, bf16[96,8192]{1,0:T(8,128)(2,1)}, u32[]{:S(2)}, u32[]{:S(2)}) collective-permute-start(bf16[96,8192]{1,0:T(8,128)(2,1)} %param.11), channel_id=1, source_target_pairs={{1,0},{2,1},{3,2},{4,3},{5,4},{6,5},{7,6},{8,7},{9,8},{10,9},{11,1... | collective-permute-start | bytes 4718600 | tf_op jit(solution)/shard_map/ppermute | solution.py:13
  2.6 2.2 %collective-permute-start.5 = (bf16[96,8192]{1,0:T(8,128)(2,1)}, bf16[96,8192]{1,0:T(8,128)(2,1)}, u32[]{:S(2)}, u32[]{:S(2)}) collective-permute-start(bf16[96,8192]{1,0:T(8,128)(2,1)} %param.11), channel_id=1, source_target_pairs={{2,0},{3,1},{4,2},{5,3},{6,4},{7,5},{8,6},{9,7},{10,8},{11,9},{12,... | collective-permute-start | bytes 4718600 | tf_op jit(solution)/shard_map/ppermute | solution.py:13
  4.8 4.2 %collective-permute-start.2 = (bf16[96,8192]{1,0:T(8,128)(2,1)}, bf16[96,8192]{1,0:T(8,128)(2,1)}, u32[]{:S(2)}, u32[]{:S(2)}) collective-permute-start(bf16[96,8192]{1,0:T(8,128)(2,1)} %param.11), channel_id=1, source_target_pairs={{0,1},{1,2},{2,3},{3,4},{4,5},{5,6},{6,7},{7,8},{8,9},{9,10},{10,1... | collective-permute-start | bytes 4718600 | tf_op jit(solution)/shard_map/ppermute | solution.py:13
  9.0 3.1 %collective-permute-start.1 = (bf16[96,8192]{1,0:T(8,128)(2,1)}, bf16[96,8192]{1,0:T(8,128)(2,1)}, u32[]{:S(2)}, u32[]{:S(2)}) collective-permute-start(bf16[96,8192]{1,0:T(8,128)(2,1)} %param.11), channel_id=1, source_target_pairs={{0,2},{1,3},{2,4},{3,5},{4,6},{5,7},{6,8},{7,9},{8,10},{9,11},{10,... | collective-permute-start | bytes 4718600 | tf_op jit(solution)/shard_map/ppermute | solution.py:13
  12.1 0.8 copy.44
  12.8 0.1 fusion.52
  12.9 0.1 fusion.50
  13.1 0.2 select_reduce_fusion.1
  13.3 0.1 select_reduce_fusion.2
  13.3 0.1 fusion.51
  13.5 1.1 slice_bitcast_fusion.2
  14.5 0.7 gather_fusion
  15.3 1.0 broadcast_select_fusion.1
  16.3 6.1 %all-to-all-start = ((bf16[32,96,128]{2,1,0:T(8,128)(2,1)}), bf16[32,96,128]{2,1,0:T(8,128)(2,1)S(1)}, u32[]{:S(2)}, u32[]{:S(2)}) async-start(bf16[32,96,128]{2,1,0:T(8,128)(2,1)} %broadcast_select_fusion.1), calls=%async_computation | async-start | bytes 1572864 | tf_op jit(solution)/shard_map/all_to_all | solution.py:84
  22.4 0.7 convert_element_type.71
  23.1 1.0 slice_reduce_fusion.2
  24.1 0.1 cosine_convert_fusion
  24.2 0.1 select_reduce_fusion
  24.4 0.1 reshape.450
  24.4 0.8 copy.43
  25.2 0.7 gather_fusion.1
  25.9 0.1 fusion.49
  26.1 0.1 fusion.59
  26.2 1.0 broadcast_select_fusion
  27.2 88.4 %all-to-all-done = bf16[32,96,128]{2,1,0:T(8,128)(2,1)S(1)} async-done(((bf16[32,96,128]{2,1,0:T(8,128)(2,1)}), bf16[32,96,128]{2,1,0:T(8,128)(2,1)S(1)}, u32[]{:S(2)}, u32[]{:S(2)}) %all-to-all-start) | async-done | bytes 786464 | tf_op jit(solution)/shard_map/all_to_all | solution.py:84
  115.5 5.0 %all-to-all-start.1 = ((bf16[32,96,128]{2,1,0:T(8,128)(2,1)}), bf16[32,96,128]{2,1,0:T(8,128)(2,1)}, u32[]{:S(2)}, u32[]{:S(2)}) async-start(bf16[32,96,128]{2,1,0:T(8,128)(2,1)} %broadcast_select_fusion), calls=%async_computation.1 | async-start | bytes 1572864 | tf_op jit(solution)/shard_map/all_to_all | solution.py:84
  120.6 0.0 copy-done
  120.6 1.7 convert_element_type.88
  122.3 2.9 %reduce_window_sum.34 = s32[16,1,12]{2,1,0:T(1,128)S(1)} reduce-window(s32[16,1,12]{2,1,0:T(1,128)S(1)} %get-tuple-element.21, s32[]{:T(128)} %constant.15.clone.1), window={size=1x1x12 pad=0_0x0_0x11_0}, to_apply=%region_0.1 | reduce-window | flops 2112 | bytes 1540 | tf_op jit(solution)/shard_map/jit(cumsum)/reduce_window_sum | solution.py:43
  125.2 0.3 copy.64
  125.5 1.9 fusion.27
  127.4 0.5 copy.47
  128.0 0.1 convert_element_type.74
  128.1 2.9 %reduce_window_sum.36 = s32[16,1,12]{2,1,0:T(1,128)S(1)} reduce-window(s32[16,1,12]{2,1,0:T(1,128)S(1)} %get-tuple-element.9, s32[]{:T(128)} %constant.15.clone.1), window={size=1x1x12 pad=0_0x0_0x11_0}, to_apply=%region_5.6 | reduce-window | flops 2112 | bytes 1540 | tf_op jit(solution)/shard_map/jit(cumsum)/reduce_window_sum | solution.py:43
  131.0 0.3 copy.65
  131.3 1.9 fusion.28
  133.2 0.5 copy.49
  133.8 0.1 convert_element_type.79
  133.9 1.5 fusion.31
  135.3 4.6 %all-to-all-done.1 = bf16[32,96,128]{2,1,0:T(8,128)(2,1)} async-done(((bf16[32,96,128]{2,1,0:T(8,128)(2,1)}), bf16[32,96,128]{2,1,0:T(8,128)(2,1)}, u32[]{:S(2)}, u32[]{:S(2)}) %all-to-all-start.1) | async-done | bytes 786464 | tf_op jit(solution)/shard_map/all_to_all | solution.py:84
  139.9 1.5 fusion.26
  141.4 0.7 copy.86
  142.1 2.1 %collective-permute-start.4 = (bf16[2,2,96,256]{3,2,1,0:T(8,128)(2,1)}, bf16[2,2,96,256]{3,2,1,0:T(8,128)(2,1)}, u32[]{:S(2)}, u32[]{:S(2)}) collective-permute-start(bf16[2,2,96,256]{3,2,1,0:T(8,128)(2,1)} %bitcast.150), channel_id=1, source_target_pairs={{1,0},{2,1},{3,2},{4,3},{5,4},{6,5},{7,6},{8,7},{9,8},{10,9},{11,1... | collective-permute-start | bytes 589832 | tf_op jit(solution)/shard_map/ppermute | solution.py:13
  144.2 0.2 copy.50
  144.4 0.8 reshape.475
  145.2 0.0 collective-permute-done.3
  145.2 4.6 %collective-permute-start = (bf16[2,2,96,256]{3,2,1,0:T(8,128)(2,1)}, bf16[2,2,96,256]{3,2,1,0:T(8,128)(2,1)S(1)}, u32[]{:S(2)}, u32[]{:S(2)}) collective-permute-start(bf16[2,2,96,256]{3,2,1,0:T(8,128)(2,1)} %bitcast.150), channel_id=1, source_target_pairs={{0,1},{1,2},{2,3},{3,4},{4,5},{5,6},{6,7},{7,8},{8,9},{9,10},{10,1... | collective-permute-start | bytes 589832 | tf_op jit(solution)/shard_map/ppermute | solution.py:13
  149.8 0.0 collective-permute-done.2
  149.8 6.7 %convolution_convert_fusion = bf16[2,2,96,8192]{3,2,1,0:T(8,128)(2,1)} fusion(bf16[96,8192]{1,0:T(8,128)(2,1)} %collective-permute-done.3, bf16[96,8192]{1,0:T(8,128)(2,1)} %param.11, bf16[96,8192]{1,0:T(8,128)(2,1)} %collective-permute-done.2, bf16[2,2,2,12,8,128]{5,4,3,2,1,0:T(8,128)(2,1)S(1)} %bitcast.154), kind=kOutput, calls=%fused_computation.11 | convolution fusion | flops 1626341376 | bytes 11206656 | tf_op jit(solution)/shard_map/kprb,bv->kprv/dot_general | solution.py:116
  156.5 0.0 collective-permute-done.5
  156.5 0.0 collective-permute-done.4
  156.6 0.0 copy-done.1
  156.6 3.7 %fusion.15 = bf16[2,2,96,8192]{3,2,1,0:T(8,128)(2,1)S(1)} fusion(bf16[2,2,96,256]{3,2,1,0:T(8,128)(2,1)} %collective-permute-done.4, bf16[96,8192]{1,0:T(8,128)(2,1)} %collective-permute-done.5, bf16[96,8192]{1,0:T(8,128)(2,1)} %collective-permute-done.3, bf16[96,8192]{1,0:T(8,128)(2,1)S(1)} %copy-done.1), kind=kOutput, calls=%fused_computation.27 | convolution fusion | flops 1623195648 | bytes 11206656 | tf_op jit(solution)/shard_map/kprb,bv->kprv/dot_general | solution.py:116
  160.3 2.7 %slice.174 = bf16[2,2,80,8192]{3,2,1,0:T(8,128)(2,1)} slice(bf16[2,2,96,8192]{3,2,1,0:T(8,128)(2,1)S(1)} %fusion.15), slice={[0:2], [0:2], [0:80], [0:8192]} | slice | bytes 10485760 | tf_op jit(solution)/shard_map/slice | solution.py:124
  163.0 0.0 collective-permute-done.1
  163.0 0.0 collective-permute-done
  163.0 3.6 %fusion.22 = bf16[2,2,96,8192]{3,2,1,0:T(8,128)(2,1)S(1)} fusion(bf16[2,2,96,256]{3,2,1,0:T(8,128)(2,1)S(1)} %collective-permute-done, bf16[96,8192]{1,0:T(8,128)(2,1)S(1)} %copy-done.1, bf16[96,8192]{1,0:T(8,128)(2,1)} %collective-permute-done.2, bf16[96,8192]{1,0:T(8,128)(2,1)} %collective-permute-done.1), kind=kOutput, calls=%fused_computation.36 | convolution fusion | flops 1623195648 | bytes 11206656 | tf_op jit(solution)/shard_map/kprb,bv->kprv/dot_general | solution.py:116
  166.6 0.0 copy-start.2
  166.6 2.6 %slice.175 = bf16[2,2,80,8192]{3,2,1,0:T(8,128)(2,1)} slice(bf16[2,2,96,8192]{3,2,1,0:T(8,128)(2,1)S(1)} %fusion.22), slice={[0:2], [0:2], [16:96], [0:8192]} | slice | bytes 10485760 | tf_op jit(solution)/shard_map/slice | solution.py:124
  169.3 14.8 %fusion.5 = f32[2,2,2,96,8192]{4,3,1,2,0:T(8,128)} fusion(bf16[2,2,80,8192]{3,2,1,0:T(8,128)(2,1)} %slice.174, bf16[2,2,96,8192]{3,2,1,0:T(8,128)(2,1)} %convolution_convert_fusion, bf16[2,2,80,8192]{3,2,1,0:T(8,128)(2,1)} %slice.175, bf16[2,2,96,256,1]{3,2,1,0,4:T(8,128)(2,1)S(1)} %copy-done.2), kind=kOutput, calls=%fused_computation.8 | convolution fusion | flops 3271557120 | bytes 42139648 | tf_op jit(solution)/shard_map/kprb,kqbv->kpqrv/dot_general | solution.py:126
  184.1 5.7 %fusion.25 = bf16[2,1,96,8192]{3,2,0,1:T(8,128)(2,1)S(1)} fusion(f32[2,2,2,96,8192]{4,3,1,2,0:T(8,128)} %fusion.5), kind=kLoop, calls=%fused_computation.39 | loop fusion | flops 4718592 | bytes 15728640 | tf_op jit(solution)/shard_map/mul | solution.py:130
  189.8 5.1 %fusion.13 = bf16[2,1,96,8192]{3,2,0,1:T(8,128)(2,1)S(1)} fusion(f32[2,2,2,96,8192]{4,3,1,2,0:T(8,128)} %fusion.5, f32[96,8192]{1,0:T(8,128)S(1)} %convert_element_type.88), kind=kLoop, calls=%fused_computation.22 | loop fusion | flops 6291456 | bytes 18874368 | tf_op jit(solution)/shard_map/convert.9
  195.0 0.6 pad_maximum_fusion
  195.5 3.1 %copy.54 = bf16[2,2,96,8192]{3,2,1,0:T(8,128)(2,1)} copy(bf16[2,2,96,8192]{3,2,0,1:T(8,128)(2,1)S(1)} %pad_maximum_fusion) | data formatting | bytes 12582912 | tf_op jit(solution)/shard_map/stack | solution.py:131
  (26 shorter events, 0.3 us)
Async XLA Ops:
  0.0 145.2 %collective-permute-start.3 = (bf16[96,8192]{1,0:T(8,128)(2,1)}, bf16[96,8192]{1,0:T(8,128)(2,1)}, u32[]{:S(2)}, u32[]{:S(2)}) collective-permute-start(bf16[96,8192]{1,0:T(8,128)(2,1)} %param.11), channel_id=1, source_target_pairs={{1,0},{2,1},{3,2},{4,3},{5,4},{6,5},{7,6},{8,7},{9,8},{10,9},{11,1... | collective-permute-start | bytes 4718600 | tf_op jit(solution)/shard_map/ppermute | solution.py:13
  2.6 154.0 %collective-permute-start.5 = (bf16[96,8192]{1,0:T(8,128)(2,1)}, bf16[96,8192]{1,0:T(8,128)(2,1)}, u32[]{:S(2)}, u32[]{:S(2)}) collective-permute-start(bf16[96,8192]{1,0:T(8,128)(2,1)} %param.11), channel_id=1, source_target_pairs={{2,0},{3,1},{4,2},{5,3},{6,4},{7,5},{8,6},{9,7},{10,8},{11,9},{12,... | collective-permute-start | bytes 4718600 | tf_op jit(solution)/shard_map/ppermute | solution.py:13
  4.8 145.1 %collective-permute-start.2 = (bf16[96,8192]{1,0:T(8,128)(2,1)}, bf16[96,8192]{1,0:T(8,128)(2,1)}, u32[]{:S(2)}, u32[]{:S(2)}) collective-permute-start(bf16[96,8192]{1,0:T(8,128)(2,1)} %param.11), channel_id=1, source_target_pairs={{0,1},{1,2},{2,3},{3,4},{4,5},{5,6},{6,7},{7,8},{8,9},{9,10},{10,1... | collective-permute-start | bytes 4718600 | tf_op jit(solution)/shard_map/ppermute | solution.py:13
  9.0 154.1 %collective-permute-start.1 = (bf16[96,8192]{1,0:T(8,128)(2,1)}, bf16[96,8192]{1,0:T(8,128)(2,1)}, u32[]{:S(2)}, u32[]{:S(2)}) collective-permute-start(bf16[96,8192]{1,0:T(8,128)(2,1)} %param.11), channel_id=1, source_target_pairs={{0,2},{1,3},{2,4},{3,5},{4,6},{5,7},{6,8},{7,9},{8,10},{9,11},{10,... | collective-permute-start | bytes 4718600 | tf_op jit(solution)/shard_map/ppermute | solution.py:13
  16.3 99.3 %all-to-all-start = ((bf16[32,96,128]{2,1,0:T(8,128)(2,1)}), bf16[32,96,128]{2,1,0:T(8,128)(2,1)S(1)}, u32[]{:S(2)}, u32[]{:S(2)}) async-start(bf16[32,96,128]{2,1,0:T(8,128)(2,1)} %broadcast_select_fusion.1), calls=%async_computation | async-start | bytes 1572864 | tf_op jit(solution)/shard_map/all_to_all | solution.py:84
  115.5 5.0 %copy-start = (bf16[32,96,128]{2,1,0:T(8,128)(2,1)}, bf16[32,96,128]{2,1,0:T(8,128)(2,1)S(1)}, u32[]{:S(2)}) copy-start(bf16[32,96,128]{2,1,0:T(8,128)(2,1)S(1)} %all-to-all-done) | copy-start | bytes 2359300
  115.5 24.4 %all-to-all-start.1 = ((bf16[32,96,128]{2,1,0:T(8,128)(2,1)}), bf16[32,96,128]{2,1,0:T(8,128)(2,1)}, u32[]{:S(2)}, u32[]{:S(2)}) async-start(bf16[32,96,128]{2,1,0:T(8,128)(2,1)} %broadcast_select_fusion), calls=%async_computation.1 | async-start | bytes 1572864 | tf_op jit(solution)/shard_map/all_to_all | solution.py:84
  142.1 14.5 %collective-permute-start.4 = (bf16[2,2,96,256]{3,2,1,0:T(8,128)(2,1)}, bf16[2,2,96,256]{3,2,1,0:T(8,128)(2,1)}, u32[]{:S(2)}, u32[]{:S(2)}) collective-permute-start(bf16[2,2,96,256]{3,2,1,0:T(8,128)(2,1)} %bitcast.150), channel_id=1, source_target_pairs={{1,0},{2,1},{3,2},{4,3},{5,4},{6,5},{7,6},{8,7},{9,8},{10,9},{11,1... | collective-permute-start | bytes 589832 | tf_op jit(solution)/shard_map/ppermute | solution.py:13
  145.2 11.4 %copy-start.1 = (bf16[96,8192]{1,0:T(8,128)(2,1)S(1)}, bf16[96,8192]{1,0:T(8,128)(2,1)}, u32[]{:S(2)}) copy-start(bf16[96,8192]{1,0:T(8,128)(2,1)} %param.11) | copy-start | bytes 4718596
  145.2 17.8 %collective-permute-start = (bf16[2,2,96,256]{3,2,1,0:T(8,128)(2,1)}, bf16[2,2,96,256]{3,2,1,0:T(8,128)(2,1)S(1)}, u32[]{:S(2)}, u32[]{:S(2)}) collective-permute-start(bf16[2,2,96,256]{3,2,1,0:T(8,128)(2,1)} %bitcast.150), channel_id=1, source_target_pairs={{0,1},{1,2},{2,3},{3,4},{4,5},{5,6},{6,7},{7,8},{8,9},{9,10},{10,1... | collective-permute-start | bytes 589832 | tf_op jit(solution)/shard_map/ppermute | solution.py:13
  166.6 2.6 %copy-start.2 = (bf16[2,2,96,256,1]{3,2,1,0,4:T(8,128)(2,1)S(1)}, bf16[2,2,96,256,1]{3,2,1,0,4:T(8,128)(2,1)}, u32[]{:S(2)}) copy-start(bf16[2,2,96,256,1]{3,2,1,0,4:T(8,128)(2,1)} %reshape.475) | copy-start | bytes 589828
where the time goes:
time: 199 us
  waiting for transfers between devices  92.9 us (47%)
  matrix products  35.6 us (18%)
  starting transfers between devices  29.9 us (15%)
  other arithmetic  22.6 us (11%)
  local copies, waits for them, and re-layouts  17.3 us (9%)
    all_to_all x2, waiting for transfers between devices, local(): lax.all_to_all(outgoing, 'orb', split_axis=0, concat_axis=0, tiled=True)  92.9 us
    ppermute x6, starting transfers between devices, passed_along(): lax.ppermute(value, axis, [(source, source + steps) for source in range(l...  18.8 us
    dot_general x1, matrix products, local(): jnp.einsum('kprb,kqbv->kpqrv', banded_hamiltonian, first_wide, preferred_...  14.8 us
    dot_general x3, matrix products, first_of(): jnp.einsum('kprb,bv->kprv', band, window, preferred_element_type=jnp.floa...  14 us
    all_to_all x2, starting transfers between devices, local(): lax.all_to_all(outgoing, 'orb', split_axis=0, concat_axis=0, tiled=True)  11.1 us
    another operation x2, other arithmetic, receive_weights(): order_rank = jnp.cumsum(matched, axis=1) - matched  5.79 us
    mul x1, other arithmetic, local(): imag_part = 2.0 * (product[:, 0, 1] + product[:, 1, 0])  5.73 us
    another operation x7, other arithmetic  5.33 us
  transfers between devices with their start and end apart: 8, of which 2 were waited for; matrix products, arithmetic and copies ran while one was open for 20% of the time, Pallas kernels for 0%

commit v1 on v0

v1 whole, which is shorter than its diff:
```python
import functools

import jax
import jax.numpy as jnp
from jax import lax
from jax.experimental import pallas as pl
from jax.experimental.pallas import tpu as pltpu
from jax.sharding import PartitionSpec as P

HALO = 80
CAP = 2
PIECES = 2
BLOCK = 1024


def routed(value, route):
    groups, owners = lax.axis_size("kgrp"), lax.axis_size("orb")
    pairs = []
    for group in range(groups):
        for owner in range(owners):
            to_group, to_owner = route(group, owner)
            if 0 <= to_owner < owners:
                pairs.append((group * owners + owner, to_group * owners + to_owner))
    return lax.ppermute(value, ("kgrp", "orb"), pairs)


def to_sibling(value):
    return routed(value, lambda group, owner: (group, owner ^ 1))


def to_pair_chip(value):
    return routed(value, lambda group, owner: (group, owner ^ 2))


def onward(value):
    return routed(value, lambda group, owner: (group, owner + (4 if owner & 2 == 0 else -4)))


def to_other_group(value):
    return routed(value, lambda group, owner: (1 - group, owner))


def shifted(value, steps):
    return routed(value, lambda group, owner: (group, owner + steps))


def phase_table(lattice, kpoints):
    cell_float = lattice.astype(jnp.float32)
    fraction = (
        kpoints[None, :, 0] * cell_float[:, None, 0]
        + kpoints[None, :, 1] * cell_float[:, None, 1]
        + kpoints[None, :, 2] * cell_float[:, None, 2]
    )
    radians = 6.283185307179586 * fraction
    return jnp.stack([jnp.cos(radians), jnp.sin(radians)], axis=-1).astype(jnp.bfloat16)


def pack_kernel(tile_count, dest_ref, tiles_ref, packed_ref, source, placed, sems):
    slots = packed_ref.shape[0]

    def clear(slot, carry):
        source[slot] = 0
        return carry

    def forget(owner, carry):
        placed[owner] = 0
        return carry

    def place(tile, carry):
        dest = dest_ref[tile]
        rank = placed[dest]
        placed[dest] = rank + 1
        source[dest * CAP + rank] = tile
        return carry

    lax.fori_loop(0, slots, clear, 0)
    lax.fori_loop(0, slots // CAP, forget, 0)
    lax.fori_loop(0, tile_count, place, 0)

    def copy(slot):
        return pltpu.make_async_copy(tiles_ref.at[source[slot]], packed_ref.at[slot], sems.at[slot])

    def start(slot, carry):
        copy(slot).start()
        return carry

    def wait(slot, carry):
        copy(slot).wait()
        return carry

    lax.fori_loop(0, slots, start, 0)
    lax.fori_loop(0, slots, wait, 0)


def pack_tiles(tiles, own_dest, owners):
    tile_count = tiles.shape[0]
    slots = owners * CAP
    return pl.pallas_call(
        functools.partial(pack_kernel, tile_count),
        out_shape=jax.ShapeDtypeStruct((slots,) + tiles.shape[1:], tiles.dtype),
        grid_spec=pltpu.PrefetchScalarGridSpec(
            num_scalar_prefetch=1,
            grid=(1,),
            in_specs=[pl.BlockSpec(memory_space=pl.ANY)],
            out_specs=pl.BlockSpec(memory_space=pl.ANY),
            scratch_shapes=[
                pltpu.SMEM((slots,), jnp.int32),
                pltpu.SMEM((owners,), jnp.int32),
                pltpu.SemaphoreType.DMA((slots,)),
            ],
        ),
        name="pack_tiles",
    )(own_dest, tiles)


def receive_weights(dest_all, slot_all, phases, device, slot_count):
    owners, step_count, tile_count = dest_all.shape
    k_count = phases.shape[1]
    total = step_count * tile_count
    mine = dest_all.reshape(owners, total) == device
    before = jnp.tril(jnp.ones((total, total), jnp.int32), -1)
    rank = jnp.sum(mine.astype(jnp.int32)[:, None, :] * before[None], axis=-1)
    column = slot_all.reshape(owners, total)
    phase_all = jnp.broadcast_to(
        phases.reshape(owners, step_count, 1, k_count * 2), (owners, step_count, tile_count, k_count * 2)
    ).reshape(owners, total, k_count * 2)
    chosen = (
        mine[None, None, :, :]
        & (rank[None, None] == jnp.arange(CAP, dtype=jnp.int32)[:, None, None, None])
        & (column[None, None] == jnp.arange(slot_count, dtype=jnp.int32)[None, :, None, None])
    )
    weights = jnp.sum(
        jnp.where(chosen[None], phase_all.transpose(2, 0, 1)[:, None, None], 0.0), axis=-1
    )
    return weights.transpose(0, 2, 3, 1).reshape(k_count * 2 * slot_count, owners * CAP)


def band_kernel(k_count, slot_count, weight_ref, tiles_ref, pair_ref, tail_ref, head_ref):
    slots, rows, width = tiles_ref.shape
    part = rows // 2
    band = slot_count * width
    kinds = k_count * 2 * slot_count
    for low in (0, part):

        def add(slot, totals):
            tile = tiles_ref[slot, low : low + part, :].astype(jnp.float32)
            return tuple(total + weight_ref[kind, slot] * tile for kind, total in enumerate(totals))

        totals = lax.fori_loop(
            0, slots, add, tuple(jnp.zeros((part, width), jnp.float32) for _ in range(kinds)), unroll=2
        )
        for k in range(k_count):
            for p in range(2):
                for j in range(slot_count):
                    value = totals[(k * 2 + p) * slot_count + j].astype(jnp.bfloat16)
                    columns = slice(j * width, (j + 1) * width)
                    later = slice(band + j * width, band + (j + 1) * width)
                    if p == 0:
                        pair_ref[k, low : low + part, columns] = value
                        pair_ref[k, rows + low : rows + low + part, later] = value
                    else:
                        pair_ref[k, rows + low : rows + low + part, columns] = value
                        pair_ref[k, low : low + part, later] = -value
    for k in range(k_count):
        for p in range(2):
            tail_ref[k, p] = pair_ref[k, (p + 1) * rows - HALO : (p + 1) * rows, 0:band]
            head_ref[k, p] = pair_ref[k, p * rows : p * rows + HALO, 0:band]


def make_bands(weights, tiles, k_count, slot_count):
    rows, width = tiles.shape[1:]
    band = slot_count * width
    vmem = pl.BlockSpec(memory_space=pltpu.VMEM)
    edge = jax.ShapeDtypeStruct((k_count, 2, HALO, band), jnp.bfloat16)
    return pl.pallas_call(
        functools.partial(band_kernel, k_count, slot_count),
        out_shape=[jax.ShapeDtypeStruct((k_count, 2 * rows, 2 * band), jnp.bfloat16), edge, edge],
        in_specs=[pl.BlockSpec(memory_space=pltpu.SMEM), vmem],
        out_specs=[vmem, vmem, vmem],
        compiler_params=pltpu.CompilerParams(vmem_limit_bytes=40 * 1024 * 1024),
        name="make_bands",
    )(weights, tiles)


def filter_kernel(
    steps,
    where_ref,
    pair_ref,
    left_ref,
    right_ref,
    own_ref,
    sibling_ref,
    near_ref,
    chip_ref,
    onward_ref,
    *rest,
):
    out_ref, window, sems = rest[-3:]
    k_count, double_rows, _ = pair_ref.shape
    rows = double_rows // 2
    band = left_ref.shape[-1]
    block = out_ref.shape[-1]
    step = pl.program_id(0)
    odd_chip, odd_core, first_block = where_ref[0], where_ref[1], where_ref[2]
    starts = [0, HALO, HALO + rows, HALO + 2 * rows, HALO + 3 * rows]

    def copies(number, slot):
        whole = pl.ds(pl.multiple_of((first_block + number) * block, block), block)
        piece = pl.ds(pl.multiple_of(number * block, block), block)

        def one(source, part, count, index):
            return pltpu.make_async_copy(
                source, window.at[slot, starts[part] : starts[part] + count, :], sems.at[slot, index]
            )

        own = one(own_ref.at[:, whole], 2, rows, 2)
        core = (
            [one(near_ref.at[:, piece], 1, rows, 1), one(sibling_ref.at[:, whole], 3, rows, 3)],
            [one(sibling_ref.at[:, whole], 1, rows, 1), one(near_ref.at[:, piece], 3, rows, 3)],
        )
        last = slice(rows - HALO, rows)
        chip = (
            [one(onward_ref.at[last, piece], 0, HALO, 0), one(chip_ref.at[0:HALO, piece], 4, HALO, 4)],
            [one(chip_ref.at[last, piece], 0, HALO, 0), one(onward_ref.at[0:HALO, piece], 4, HALO, 4)],
        )
        return own, core, chip

    def begin(number, slot):
        own, core, chip = copies(number, slot)
        own.start()
        for odd in (0, 1):

            @pl.when(odd_core == odd)
            def _():
                core[odd][0].start()
                core[odd][1].start()

            @pl.when(odd_chip == odd)
            def _():
                chip[odd][0].start()
                chip[odd][1].start()

    @pl.when(step == 0)
    def _():
        begin(0, 0)

    slot = lax.rem(step, 2)

    @pl.when(step + 1 < steps)
    def _():
        begin(step + 1, 1 - slot)

    own, core, chip = copies(step, slot)
    own.wait()
    for copy in core[0] + chip[0]:
        copy.wait()

    def product(left, right):
        return jnp.dot(left, right, preferred_element_type=jnp.float32)

    for k in range(k_count):
        pair = pair_ref[k]
        lower = window[slot, 0:band, :]
        middle = window[slot, rows : rows + band, :]
        upper = window[slot, 2 * rows : 2 * rows + band, :]
        own_first = product(pair[:, 0:band], middle).astype(jnp.bfloat16)
        left_first = product(left_ref[k].reshape(2 * HALO, band), lower).astype(jnp.bfloat16)
        right_first = product(right_ref[k].reshape(2 * HALO, band), upper).astype(jnp.bfloat16)
        wide = jnp.concatenate(
            [
                piece
                for p in range(2)
                for piece in (
                    left_first[p * HALO : (p + 1) * HALO],
                    own_first[p * rows : (p + 1) * rows],
                    right_first[p * HALO : (p + 1) * HALO],
                )
            ],
            axis=0,
        )
        both = 2.0 * product(pair, wide)
        center = window[slot, HALO + rows : HALO + 2 * rows, :].astype(jnp.float32)
        out_ref[k, 0] = (both[0:rows] - center).astype(jnp.bfloat16)
        out_ref[k, 1] = both[rows:].astype(jnp.bfloat16)


def filter_columns(where, pair, left, right, own, sibling, near, chip, onward_rows, so_far):
    k_count, double_rows, _ = pair.shape
    rows = double_rows // 2
    columns = own.shape[1]
    block = min(BLOCK, near.shape[1])
    steps = near.shape[1] // block
    vmem = pl.BlockSpec(memory_space=pltpu.VMEM)
    hbm = pl.BlockSpec(memory_space=pl.ANY)
    operands = [where, pair, left, right, own, sibling, near, chip, onward_rows]
    specs = [vmem] * 3 + [hbm] * 5
    aliases = {}
    if so_far is not None:
        aliases = {len(operands): 0}
        operands.append(so_far)
        specs.append(hbm)
    return pl.pallas_call(
        functools.partial(filter_kernel, steps),
        out_shape=jax.ShapeDtypeStruct((k_count, 2, rows, columns), jnp.bfloat16),
        grid_spec=pltpu.PrefetchScalarGridSpec(
            num_scalar_prefetch=1,
            grid=(steps,),
            in_specs=specs,
            out_specs=pl.BlockSpec((k_count, 2, rows, block), lambda i, where: (0, 0, 0, where[2] + i)),
            scratch_shapes=[
                pltpu.VMEM((2, 3 * rows + 2 * HALO, block), jnp.bfloat16),
                pltpu.SemaphoreType.DMA((2, 5)),
            ],
        ),
        input_output_aliases=aliases,
        compiler_params=pltpu.CompilerParams(
            vmem_limit_bytes=40 * 1024 * 1024, dimension_semantics=("arbitrary",)
        ),
        cost_estimate=pl.CostEstimate(
            flops=2 * near.shape[1] * k_count * (4 * 256 * 256 + 2 * 192 * 256),
            bytes_accessed=near.shape[1] * 2 * (448 + 384),
            transcendentals=0,
        ),
        name="filter_columns",
    )(*operands)


def local(hopping_tiles, tile_strip, tile_column_slot, lattice, kpoints, start_block):
    owners = lax.axis_size("orb")
    device = lax.axis_index("orb")
    group = lax.axis_index("kgrp")
    odd_core = device & 1
    odd_chip = (device >> 1) & 1
    step_count, tile_count, row_count, col_width = hopping_tiles.shape
    slot_count = (row_count + 2 * HALO) // col_width
    k_count = kpoints.shape[0]
    half = start_block.shape[1] // 2
    piece = half // PIECES
    block = min(BLOCK, piece)

    dest_all = tile_strip[:, :, 0].reshape(owners, step_count, tile_count)
    own_dest = lax.dynamic_index_in_dim(dest_all, device, 0, keepdims=False).reshape(-1)
    tiles = hopping_tiles.reshape(step_count * tile_count, row_count, col_width)
    outgoing = pack_tiles(tiles, own_dest, owners)
    incoming = lax.all_to_all(outgoing, "orb", split_axis=0, concat_axis=0, tiled=True)
    phases = lax.optimization_barrier(phase_table(lattice, kpoints)).astype(jnp.float32)
    slot_all = tile_column_slot.reshape(owners, step_count, tile_count)
    weights = receive_weights(dest_all, slot_all, phases, device, slot_count)
    pair, tail, head = make_bands(weights, incoming, k_count, slot_count)
    left = shifted(tail, 1)
    right = shifted(head, -1)

    sibling = to_sibling(start_block)
    passes = odd_chip == odd_core
    result = None
    work = []
    for number in range(PIECES):
        begin = group * half + number * piece
        chip = to_pair_chip(lax.dynamic_slice_in_dim(start_block, begin, piece, axis=1))
        beyond = onward(chip)
        near = to_sibling(jnp.where(passes, chip, beyond))
        work.append((begin, near, chip, beyond))
        chip, beyond = to_other_group(chip), to_other_group(beyond)
        near = to_sibling(jnp.where(passes, chip, beyond))
        work.append(((1 - group) * half + number * piece, near, chip, beyond))
    for begin, near, chip, beyond in work:
        where = jnp.stack([odd_chip, odd_core, begin // block]).astype(jnp.int32)
        result = filter_columns(where, pair, left, right, start_block, sibling, near, chip, beyond, result)
    return result


def solution(mesh):
    return jax.shard_map(
        local,
        mesh=mesh,
        in_specs=(P("orb", None, None, None), P(), P(), P(), P("kgrp", None), P("orb", None)),
        out_specs=P("kgrp", None, "orb", None),
        check_vma=False,
    )
```

time: 199 us -> 135 us (0.68)
  waiting for transfers between devices: 92.9 us -> 20.9 us
  Pallas kernels: 0 us -> 50.1 us
  matrix products: 35.6 us -> 0 us
  other arithmetic: 22.6 us -> 15.5 us
  starting transfers between devices: 29.9 us -> 27.5 us
    all_to_all x2 -> x1, waiting for transfers between devices: 92.9 us -> 0.01 us  [local(): lax.all_to_all(outgoing, 'orb', split_axis=0, concat_axis=0, tiled=True)]
    pallas_call x0 -> x6, Pallas kernels: none -> 50.1 us  [the longest x1 26.5 us: pack_tiles(): pl.pallas_call(functools.partial(pack_kernel, tile_count), out_shape=jax....]
    dot_general x8 -> x0, matrix products: 35.6 us -> none  [the longest x1 14.8 us: local(): jnp.einsum('kprb,kqbv->kpqrv', banded_hamiltonian, first_wide, preferred_...]
    ppermute x6 -> x15, waiting for transfers between devices: 0.02 us -> 20.9 us  [routed(): return lax.ppermute(value, ('kgrp', 'orb'), pairs)]
    another operation x12 -> x4, other arithmetic: 11.8 us -> 2.58 us  [the longest x2 5.79 us: receive_weights(): order_rank = jnp.cumsum(matched, axis=1) - matched]
    mul x1 -> x0, other arithmetic: 5.73 us -> none  [local(): imag_part = 2.0 * (product[:, 0, 1] + product[:, 1, 0])]
    slice x4 -> x0, local copies, waits for them, and re-layouts: 5.44 us -> none  [the longest x1 2.72 us: local(): right_first[:, :, :HALO]]
    all_to_all x2 -> x1, starting transfers between devices: 11.1 us -> 6.35 us  [local(): lax.all_to_all(outgoing, 'orb', split_axis=0, concat_axis=0, tiled=True)]
  transfers between devices with their start and end apart: 8 -> 16, of which waited for: 2 -> 3; matrix products, arithmetic and copies ran while one was open for 20% -> 25% of each run, Pallas kernels for 0% -> 34%
where the time goes in v1:
time: 135 us; the launch traced here: 133 us
  Pallas kernels  50.1 us (37%)
  starting transfers between devices  27.5 us (20%)
  waiting for transfers between devices  20.9 us (15%)
  local copies, waits for them, and re-layouts  19.2 us (14%)
  other arithmetic  15.5 us (11%)
    pallas_call x1, Pallas kernels, pack_tiles(): pl.pallas_call(functools.partial(pack_kernel, tile_count), out_shape=jax....  26.5 us
    ppermute x15, starting transfers between devices, routed(): return lax.ppermute(value, ('kgrp', 'orb'), pairs)  21.2 us
    pallas_call x4, Pallas kernels, filter_columns(): pl.pallas_call(functools.partial(filter_kernel, steps), out_shape=jax.Sha...  21.1 us
    ppermute x15, waiting for transfers between devices, routed(): return lax.ppermute(value, ('kgrp', 'orb'), pairs)  20.9 us
    all_to_all x1, starting transfers between devices, local(): lax.all_to_all(outgoing, 'orb', split_axis=0, concat_axis=0, tiled=True)  6.35 us
    select_n x4, other arithmetic, local(): near = to_sibling(jnp.where(passes, chip, beyond))  4.52 us
    unnamed x14, local copies, waits for them, and re-layouts  3.56 us
  transfers between devices with their start and end apart: 16, of which 3 were waited for; matrix products, arithmetic and copies ran while one was open for 25% of the time, Pallas kernels for 34%

profile of v1, /device:TPU:11, one launch (start us, length us, event | category | flops | bytes accessed | tf_op | source)
XLA Modules:
  0.0 133.5 jit_solution(17329479411708402635)
XLA Ops:
  0.0 0.7 collective-permute-start.2
  0.7 2.1 %constant_dynamic-slice_fusion = (bf16[96,2048]{1,0:T(8,128)(2,1)}, bf16[96,2048]{1,0:T(8,128)(2,1)}) fusion(bf16[96,8192]{1,0:T(8,128)(2,1)} %own_ref.7, s32[]{:T(128)S(6)} %select_n.66, s32[]{:T(128)S(6)} %select_n.61), kind=kLoop, calls=%fused_computation.20 | loop fusion | bytes 1572872 | tf_op jit(solution)/shard_map/dynamic_slice | solution.py:359
  2.8 0.3 collective-permute-start.9
  3.0 0.8 copy.28
  3.8 0.6 constant_dynamic-slice_fusion.2
  4.4 1.3 reshape.381.dest_ref
  5.7 26.5 %pack_tiles.1 = bf16[32,96,128]{2,1,0:T(8,128)(2,1)} custom-call(s32[24]{0:T(128)} %reshape.381.dest_ref, bf16[24,96,128]{2,1,0:T(8,128)(2,1)} %bitcast.24), custom_call_target="tpu_custom_call" | custom-call | tf_op jit(solution)/shard_map/pack_tiles/pallas_call | solution.py:98
  32.2 6.4 %all-to-all-start = ((bf16[32,96,128]{2,1,0:T(8,128)(2,1)}), bf16[32,96,128]{2,1,0:T(8,128)(2,1)}, u32[]{:S(2)}, u32[]{:S(2)}) async-start(bf16[32,96,128]{2,1,0:T(8,128)(2,1)} %pack_tiles.1), calls=%async_computation | async-start | bytes 1572864 | tf_op jit(solution)/shard_map/all_to_all | solution.py:345
  38.5 0.3 collective-permute-start.3
  38.8 1.3 broadcast_compare_fusion
  40.1 0.7 fusion.1
  40.8 0.7 convert_element_type.13
  41.5 0.6 slice_bitcast_fusion.2
  42.0 1.6 %slice_reduce_fusion.2 = (f32[2]{0:T(128)S(1)}, f32[2]{0:T(128)}, f32[2]{0:T(128)}) fusion(f32[2,3]{1,0:T(2,128)} %param.10), kind=kLoop, calls=%fused_computation.19 | loop fusion | bytes 48 | tf_op jit(solution)/shard_map/slice | solution.py:50
  43.6 0.6 pad_add_fusion.4
  44.2 0.1 pad_add_fusion.3
  44.3 1.3 cosine_convert_fusion
  45.6 0.6 sine_convert_fusion
  46.2 1.4 %copy.22 = pred[32,12,1]{1,0,2:T(8,128)(4,1)} copy(pred[32,12,1]{0,2,1:T(4,128)(4,1)} %broadcast_compare_fusion) | data formatting | bytes 768 | tf_op jit(solution)/shard_map/eq | solution.py:120
  47.6 0.8 eq.60
  48.3 0.6 convert_element_type.12
  48.9 1.4 %copy.23 = s32[32,12]{1,0:T(8,128)} copy(s32[32,12]{0,1:T(8,128)} %param.8) | data formatting | bytes 3072 | tf_op args[2]
  50.3 1.4 %eq.64 = s32[16,24]{1,0:T(8,128)} reshape(s32[32,12]{1,0:T(8,128)} %copy.23) | data formatting | bytes 3072 | tf_op jit(solution)/shard_map/eq | solution.py:130
  51.7 1.1 multiply_reduce_fusion
  52.8 1.3 iota_compare_fusion
  54.1 2.0 %collective-permute-start.11 = (bf16[96,2048]{1,0:T(8,128)(2,1)S(1)}, bf16[96,2048]{1,0:T(8,128)(2,1)}, u32[]{:S(2)}, u32[]{:S(2)}) collective-permute-start(bf16[96,2048]{1,0:T(8,128)(2,1)S(1)} %collective-permute-done.9.chip_ref), channel_id=1, source_target_pairs={{0,4},{1,5},{4,8},{5,9},{6,2},{7,3},{8,12},{9,13},{10,6},{11,7},{1... | collective-permute-start | bytes 1179656 | tf_op jit(solution)/shard_map/ppermute | solution.py:24
  56.0 0.7 pad_maximum_fusion
  56.7 0.7 reshape.383
  57.4 0.9 copy.25
  58.3 0.6 broadcast_in_dim.50
  58.9 1.5 %copy.26 = f32[4,16,24]{2,1,0:T(8,128)} copy(f32[4,16,24]{1,0,2:T(4,128)} %bitcast.25) | data formatting | bytes 12288 | tf_op jit(solution)/shard_map/transpose | solution.py:133
  60.4 0.7 broadcast_and_fusion
  61.1 1.5 %select_reduce_fusion = f32[4,2,2,16]{3,2,1,0:T(2,128)} fusion(f32[4,16,24]{2,1,0:T(8,128)} %copy.26, pred[2,2,16,24]{3,2,1,0:T(8,128)(4,1)S(1)} %broadcast_and_fusion), kind=kLoop, calls=%fused_computation.5 | loop fusion | flops 12032 | bytes 8704 | tf_op jit(solution)/shard_map/reduce_sum | solution.py:132
  62.6 1.4 %copy.27 = f32[4,2,16,2]{3,2,1,0:T(8,128)} copy(f32[4,2,16,2]{2,1,3,0:T(2,128)} %bitcast.26) | data formatting | bytes 2048 | tf_op jit(solution)/shard_map/transpose | solution.py:135
  64.0 0.9 reshape.380.weight_ref
  64.9 1.3 collective-permute-start.10
  66.2 1.9 %collective-permute-start.5 = (bf16[96,2048]{1,0:T(8,128)(2,1)}, bf16[96,2048]{1,0:T(8,128)(2,1)}, u32[]{:S(2)}, u32[]{:S(2)}) collective-permute-start(bf16[96,2048]{1,0:T(8,128)(2,1)} %collective-permute-done.3.chip_ref), channel_id=1, source_target_pairs={{0,4},{1,5},{4,8},{5,9},{6,2},{7,3},{8,12},{9,13},{10,6},{11,7},{1... | collective-permute-start | bytes 1179656 | tf_op jit(solution)/shard_map/ppermute | solution.py:24
  68.1 0.3 collective-permute-start.4
  68.4 0.0 collective-permute-done.11.onward_ref
  68.4 0.8 broadcast_select_fusion
  69.2 2.3 %collective-permute-start.14 = (bf16[96,2048]{1,0:T(8,128)(2,1)}, bf16[96,2048]{1,0:T(8,128)(2,1)}, u32[]{:S(2)}, u32[]{:S(2)}) collective-permute-start(bf16[96,2048]{1,0:T(8,128)(2,1)} %broadcast_select_fusion), channel_id=1, source_target_pairs={{0,1},{1,0},{2,3},{3,2},{4,5},{5,4},{6,7},{7,6},{8,9},{9,8},{10,11... | collective-permute-start | bytes 1179656 | tf_op jit(solution)/shard_map/ppermute | solution.py:24
  71.6 6.4 %collective-permute-done.5.onward_ref = bf16[96,2048]{1,0:T(8,128)(2,1)} collective-permute-done((bf16[96,2048]{1,0:T(8,128)(2,1)}, bf16[96,2048]{1,0:T(8,128)(2,1)}, u32[]{:S(2)}, u32[]{:S(2)}) %collective-permute-start.5) | collective-permute-done | bytes 393248 | tf_op jit(solution)/shard_map/ppermute | solution.py:24
  78.0 0.2 collective-permute-start.12
  78.2 1.8 %broadcast_select_fusion.2 = bf16[96,2048]{1,0:T(8,128)(2,1)} fusion(bf16[96,2048]{1,0:T(8,128)(2,1)} %collective-permute-done.3.chip_ref, bf16[96,2048]{1,0:T(8,128)(2,1)} %collective-permute-done.5.onward_ref, pred[]{:T(512)S(6)} %eq.68), kind=kLoop, calls=%fused_computation.2 | loop fusion | flops 196608 | bytes 1179649 | tf_op jit(solution)/shard_map/jit(_where)/select_n | solution.py:361
  80.0 0.0 collective-permute-done.10.chip_ref
  80.0 1.2 collective-permute-start.6
  81.3 10.4 %collective-permute-done.12.onward_ref = bf16[96,2048]{1,0:T(8,128)(2,1)S(1)} collective-permute-done((bf16[96,2048]{1,0:T(8,128)(2,1)}, bf16[96,2048]{1,0:T(8,128)(2,1)S(1)}, u32[]{:S(2)}, u32[]{:S(2)}) %collective-permute-start.12) | collective-permute-done | bytes 393248 | tf_op jit(solution)/shard_map/ppermute | solution.py:24
  91.7 0.9 broadcast_select_fusion.1
  92.6 0.0 copy-done.3
  92.6 0.8 copy-done.1
  93.4 2.9 %collective-permute-start.13 = (bf16[96,2048]{1,0:T(8,128)(2,1)}, bf16[96,2048]{1,0:T(8,128)(2,1)}, u32[]{:S(2)}, u32[]{:S(2)}) collective-permute-start(bf16[96,2048]{1,0:T(8,128)(2,1)} %broadcast_select_fusion.1), channel_id=1, source_target_pairs={{0,1},{1,0},{2,3},{3,2},{4,5},{5,4},{6,7},{7,6},{8,9},{9,8},{10,11... | collective-permute-start | bytes 1179656 | tf_op jit(solution)/shard_map/ppermute | solution.py:24
  96.3 0.0 all-to-all-done.tiles_ref
  96.3 2.5 %make_bands.1 = (bf16[2,192,512]{2,1,0:T(8,128)(2,1)S(1)}, bf16[2,2,80,256]{3,2,1,0:T(8,128)(2,1)S(1)}, bf16[2,2,80,256]{3,2,1,0:T(8,128)(2,1)S(1)}) custom-call(f32[8,32]{1,0:T(8,128)S(1)} %reshape.380.weight_ref, bf16[32,96,128]{2,1,0:T(8,128)(2,1)} %all-to-all-done.tiles_ref), custom_call_target="tpu_custom_call" | custom-call | tf_op jit(solution)/shard_map/make_bands/pallas_call | solution.py:175
  98.9 5.3 %collective-permute-start = (bf16[2,2,80,256]{3,2,1,0:T(8,128)(2,1)S(1)}, bf16[2,2,80,256]{3,2,1,0:T(8,128)(2,1)S(1)}, u32[]{:S(2)}, u32[]{:S(2)}) collective-permute-start(bf16[2,2,80,256]{3,2,1,0:T(8,128)(2,1)S(1)} %get-tuple-element.9), channel_id=1, source_target_pairs={{0,1},{1,2},{2,3},{3,4},{4,5},{5,6},{6,7},{7,8},{8,9},{9,10},{10,1... | collective-permute-start | bytes 491528 | tf_op jit(solution)/shard_map/ppermute | solution.py:24
  104.2 1.9 %collective-permute-start.1 = (bf16[2,2,80,256]{3,2,1,0:T(8,128)(2,1)S(1)}, bf16[2,2,80,256]{3,2,1,0:T(8,128)(2,1)S(1)}, u32[]{:S(2)}, u32[]{:S(2)}) collective-permute-start(bf16[2,2,80,256]{3,2,1,0:T(8,128)(2,1)S(1)} %get-tuple-element.10), channel_id=1, source_target_pairs={{1,0},{2,1},{3,2},{4,3},{5,4},{6,5},{7,6},{8,7},{9,8},{10,9},{11,1... | collective-permute-start | bytes 491528 | tf_op jit(solution)/shard_map/ppermute | solution.py:24
  106.1 1.1 broadcast_select_fusion.3
  107.2 0.1 collective-permute-start.8
  107.3 0.5 collective-permute-start.7
  107.8 4.0 %collective-permute-done.1.right_ref = bf16[2,2,80,256]{3,2,1,0:T(8,128)(2,1)S(1)} collective-permute-done((bf16[2,2,80,256]{3,2,1,0:T(8,128)(2,1)S(1)}, bf16[2,2,80,256]{3,2,1,0:T(8,128)(2,1)S(1)}, u32[]{:S(2)}, u32[]{:S(2)}) %collective-permute-start.1) | collective-permute-done | bytes 163872 | tf_op jit(solution)/shard_map/ppermute | solution.py:24
  111.7 0.6 copy-done.5
  112.3 5.3 %filter_columns.4.rest_0_ = bf16[2,2,96,8192]{3,2,1,0:T(8,128)(2,1)} custom-call(s32[3]{0:T(128)S(1)} %copy-done.5, bf16[2,192,512]{2,1,0:T(8,128)(2,1)S(1)} %get-tuple-element.8.pair_ref, bf16[2,2,80,256]{3,2,1,0:T(8,128)(2,1)S(1)} %collective-permute-done.left_ref, bf16[2,2,80,256]{3,2,1,0:T(8,128)(2,1)S(1)} %collective-permute-done.1.right_ref, ...), custom_call_target="tpu_custom_call" | custom-call | flops 2952790016 | bytes 3407872 | tf_op jit(solution)/shard_map/filter_columns/pallas_call | solution.py:302
  117.6 5.2 %filter_columns.5.rest_0_ = bf16[2,2,96,8192]{3,2,1,0:T(8,128)(2,1)} custom-call(s32[3]{0:T(128)S(1)} %get-tuple-element.23.where_ref, bf16[2,192,512]{2,1,0:T(8,128)(2,1)S(1)} %get-tuple-element.8.pair_ref, bf16[2,2,80,256]{3,2,1,0:T(8,128)(2,1)S(1)} %collective-permute-done.left_ref, ...), custom_call_target="tpu_custom_call", output_to_operand_aliasing={{}: (9, {})} | custom-call | flops 2952790016 | bytes 3407872 | tf_op jit(solution)/shard_map/filter_columns/pallas_call | solution.py:302
  122.9 5.3 %filter_columns.6.rest_0_ = bf16[2,2,96,8192]{3,2,1,0:T(8,128)(2,1)} custom-call(s32[3]{0:T(128)S(1)} %get-tuple-element.24.where_ref, bf16[2,192,512]{2,1,0:T(8,128)(2,1)S(1)} %get-tuple-element.8.pair_ref, bf16[2,2,80,256]{3,2,1,0:T(8,128)(2,1)S(1)} %collective-permute-done.left_ref, ...), custom_call_target="tpu_custom_call", output_to_operand_aliasing={{}: (9, {})} | custom-call | flops 2952790016 | bytes 3407872 | tf_op jit(solution)/shard_map/filter_columns/pallas_call | solution.py:302
  128.2 5.3 %filter_columns.7 = bf16[2,2,96,8192]{3,2,1,0:T(8,128)(2,1)} custom-call(s32[3]{0:T(128)S(1)} %get-tuple-element.25.where_ref, bf16[2,192,512]{2,1,0:T(8,128)(2,1)S(1)} %get-tuple-element.8.pair_ref, bf16[2,2,80,256]{3,2,1,0:T(8,128)(2,1)S(1)} %collective-permute-done.left_ref, ...), custom_call_target="tpu_custom_call", output_to_operand_aliasing={{}: (9, {})} | custom-call | flops 2952790016 | bytes 3407872 | tf_op jit(solution)/shard_map/filter_columns/pallas_call | solution.py:302
  (21 shorter events, 0.1 us)
Async XLA Ops:
  0.0 111.7 %copy-start = (bf16[96,8192]{1,0:T(8,128)(2,1)S(1)}, bf16[96,8192]{1,0:T(8,128)(2,1)}, u32[]{:S(2)}) copy-start(bf16[96,8192]{1,0:T(8,128)(2,1)} %own_ref.7) | copy-start | bytes 4718596
  0.0 107.2 %collective-permute-start.2 = (bf16[96,8192]{1,0:T(8,128)(2,1)}, bf16[96,8192]{1,0:T(8,128)(2,1)S(1)}, u32[]{:S(2)}, u32[]{:S(2)}) collective-permute-start(bf16[96,8192]{1,0:T(8,128)(2,1)} %own_ref.7), channel_id=1, source_target_pairs={{0,1},{1,0},{2,3},{3,2},{4,5},{5,4},{6,7},{7,6},{8,9},{9,8},{10,11... | collective-permute-start | bytes 4718600 | tf_op jit(solution)/shard_map/ppermute | solution.py:24
  2.8 51.3 %collective-permute-start.9 = (bf16[96,2048]{1,0:T(8,128)(2,1)}, bf16[96,2048]{1,0:T(8,128)(2,1)S(1)}, u32[]{:S(2)}, u32[]{:S(2)}) collective-permute-start(bf16[96,2048]{1,0:T(8,128)(2,1)} %get-tuple-element.18), channel_id=1, source_target_pairs={{0,2},{1,3},{2,0},{3,1},{4,6},{5,7},{6,4},{7,5},{8,10},{9,11},{10,... | collective-permute-start | bytes 1179656 | tf_op jit(solution)/shard_map/ppermute | solution.py:24
  32.2 64.1 %all-to-all-start = ((bf16[32,96,128]{2,1,0:T(8,128)(2,1)}), bf16[32,96,128]{2,1,0:T(8,128)(2,1)}, u32[]{:S(2)}, u32[]{:S(2)}) async-start(bf16[32,96,128]{2,1,0:T(8,128)(2,1)} %pack_tiles.1), calls=%async_computation | async-start | bytes 1572864 | tf_op jit(solution)/shard_map/all_to_all | solution.py:345
  38.5 27.7 %collective-permute-start.3 = (bf16[96,2048]{1,0:T(8,128)(2,1)}, bf16[96,2048]{1,0:T(8,128)(2,1)}, u32[]{:S(2)}, u32[]{:S(2)}) collective-permute-start(bf16[96,2048]{1,0:T(8,128)(2,1)} %get-tuple-element.19), channel_id=1, source_target_pairs={{0,2},{1,3},{2,0},{3,1},{4,6},{5,7},{6,4},{7,5},{8,10},{9,11},{10,... | collective-permute-start | bytes 1179656 | tf_op jit(solution)/shard_map/ppermute | solution.py:24
  54.1 14.4 %collective-permute-start.11 = (bf16[96,2048]{1,0:T(8,128)(2,1)S(1)}, bf16[96,2048]{1,0:T(8,128)(2,1)}, u32[]{:S(2)}, u32[]{:S(2)}) collective-permute-start(bf16[96,2048]{1,0:T(8,128)(2,1)S(1)} %collective-permute-done.9.chip_ref), channel_id=1, source_target_pairs={{0,4},{1,5},{4,8},{5,9},{6,2},{7,3},{8,12},{9,13},{10,6},{11,7},{1... | collective-permute-start | bytes 1179656 | tf_op jit(solution)/shard_map/ppermute | solution.py:24
  64.9 15.1 %collective-permute-start.10 = (bf16[96,2048]{1,0:T(8,128)(2,1)S(1)}, bf16[96,2048]{1,0:T(8,128)(2,1)S(1)}, u32[]{:S(2)}, u32[]{:S(2)}) collective-permute-start(bf16[96,2048]{1,0:T(8,128)(2,1)S(1)} %collective-permute-done.9.chip_ref), channel_id=1, source_target_pairs={{0,16},{1,17},{2,18},{3,19},{4,20},{5,21},{6,22},{7,23},{8,24},{9,... | collective-permute-start | bytes 1179656 | tf_op jit(solution)/shard_map/ppermute | solution.py:24
  66.2 11.8 %collective-permute-start.5 = (bf16[96,2048]{1,0:T(8,128)(2,1)}, bf16[96,2048]{1,0:T(8,128)(2,1)}, u32[]{:S(2)}, u32[]{:S(2)}) collective-permute-start(bf16[96,2048]{1,0:T(8,128)(2,1)} %collective-permute-done.3.chip_ref), channel_id=1, source_target_pairs={{0,4},{1,5},{4,8},{5,9},{6,2},{7,3},{8,12},{9,13},{10,6},{11,7},{1... | collective-permute-start | bytes 1179656 | tf_op jit(solution)/shard_map/ppermute | solution.py:24
  68.1 30.7 %collective-permute-start.4 = (bf16[96,2048]{1,0:T(8,128)(2,1)}, bf16[96,2048]{1,0:T(8,128)(2,1)}, u32[]{:S(2)}, u32[]{:S(2)}) collective-permute-start(bf16[96,2048]{1,0:T(8,128)(2,1)} %collective-permute-done.3.chip_ref), channel_id=1, source_target_pairs={{0,16},{1,17},{2,18},{3,19},{4,20},{5,21},{6,22},{7,23},{8,24},{9,... | collective-permute-start | bytes 1179656 | tf_op jit(solution)/shard_map/ppermute | solution.py:24
  69.2 37.9 %collective-permute-start.14 = (bf16[96,2048]{1,0:T(8,128)(2,1)}, bf16[96,2048]{1,0:T(8,128)(2,1)}, u32[]{:S(2)}, u32[]{:S(2)}) collective-permute-start(bf16[96,2048]{1,0:T(8,128)(2,1)} %broadcast_select_fusion), channel_id=1, source_target_pairs={{0,1},{1,0},{2,3},{3,2},{4,5},{5,4},{6,7},{7,6},{8,9},{9,8},{10,11... | collective-permute-start | bytes 1179656 | tf_op jit(solution)/shard_map/ppermute | solution.py:24
  78.0 13.7 %collective-permute-start.12 = (bf16[96,2048]{1,0:T(8,128)(2,1)}, bf16[96,2048]{1,0:T(8,128)(2,1)S(1)}, u32[]{:S(2)}, u32[]{:S(2)}) collective-permute-start(bf16[96,2048]{1,0:T(8,128)(2,1)} %collective-permute-done.11.onward_ref), channel_id=1, source_target_pairs={{0,16},{1,17},{2,18},{3,19},{4,20},{5,21},{6,22},{7,23},{8,24},{9,... | collective-permute-start | bytes 1179656 | tf_op jit(solution)/shard_map/ppermute | solution.py:24
  80.0 24.1 %collective-permute-start.6 = (bf16[96,2048]{1,0:T(8,128)(2,1)}, bf16[96,2048]{1,0:T(8,128)(2,1)}, u32[]{:S(2)}, u32[]{:S(2)}) collective-permute-start(bf16[96,2048]{1,0:T(8,128)(2,1)} %collective-permute-done.5.onward_ref), channel_id=1, source_target_pairs={{0,16},{1,17},{2,18},{3,19},{4,20},{5,21},{6,22},{7,23},{8,24},{9,... | collective-permute-start | bytes 1179656 | tf_op jit(solution)/shard_map/ppermute | solution.py:24
  91.7 0.9 copy-start.3
  92.6 0.8 copy-start.1
  93.4 24.2 %collective-permute-start.13 = (bf16[96,2048]{1,0:T(8,128)(2,1)}, bf16[96,2048]{1,0:T(8,128)(2,1)}, u32[]{:S(2)}, u32[]{:S(2)}) collective-permute-start(bf16[96,2048]{1,0:T(8,128)(2,1)} %broadcast_select_fusion.1), channel_id=1, source_target_pairs={{0,1},{1,0},{2,3},{3,2},{4,5},{5,4},{6,7},{7,6},{8,9},{9,8},{10,11... | collective-permute-start | bytes 1179656 | tf_op jit(solution)/shard_map/ppermute | solution.py:24
  98.8 18.8 %copy-start.2 = (bf16[96,2048]{1,0:T(8,128)(2,1)S(1)}, bf16[96,2048]{1,0:T(8,128)(2,1)}, u32[]{:S(2)}) copy-start(bf16[96,2048]{1,0:T(8,128)(2,1)} %copy-done.1) | copy-start | bytes 1179652
  98.9 18.8 %copy-start.4 = (bf16[96,2048]{1,0:T(8,128)(2,1)S(1)}, bf16[96,2048]{1,0:T(8,128)(2,1)}, u32[]{:S(2)}) copy-start(bf16[96,2048]{1,0:T(8,128)(2,1)} %copy-done.3) | copy-start | bytes 1179652
  98.9 8.9 %collective-permute-start = (bf16[2,2,80,256]{3,2,1,0:T(8,128)(2,1)S(1)}, bf16[2,2,80,256]{3,2,1,0:T(8,128)(2,1)S(1)}, u32[]{:S(2)}, u32[]{:S(2)}) collective-permute-start(bf16[2,2,80,256]{3,2,1,0:T(8,128)(2,1)S(1)} %get-tuple-element.9), channel_id=1, source_target_pairs={{0,1},{1,2},{2,3},{3,4},{4,5},{5,6},{6,7},{7,8},{8,9},{9,10},{10,1... | collective-permute-start | bytes 491528 | tf_op jit(solution)/shard_map/ppermute | solution.py:24
  104.2 7.5 %collective-permute-start.1 = (bf16[2,2,80,256]{3,2,1,0:T(8,128)(2,1)S(1)}, bf16[2,2,80,256]{3,2,1,0:T(8,128)(2,1)S(1)}, u32[]{:S(2)}, u32[]{:S(2)}) collective-permute-start(bf16[2,2,80,256]{3,2,1,0:T(8,128)(2,1)S(1)} %get-tuple-element.10), channel_id=1, source_target_pairs={{1,0},{2,1},{3,2},{4,3},{5,4},{6,5},{7,6},{8,7},{9,8},{10,9},{11,1... | collective-permute-start | bytes 491528 | tf_op jit(solution)/shard_map/ppermute | solution.py:24
  107.2 15.7 %collective-permute-start.8 = (bf16[96,2048]{1,0:T(8,128)(2,1)}, bf16[96,2048]{1,0:T(8,128)(2,1)S(1)}, u32[]{:S(2)}, u32[]{:S(2)}) collective-permute-start(bf16[96,2048]{1,0:T(8,128)(2,1)} %broadcast_select_fusion.2), channel_id=1, source_target_pairs={{0,1},{1,0},{2,3},{3,2},{4,5},{5,4},{6,7},{7,6},{8,9},{9,8},{10,11... | collective-permute-start | bytes 1179656 | tf_op jit(solution)/shard_map/ppermute | solution.py:24
  107.3 20.9 %collective-permute-start.7 = (bf16[96,2048]{1,0:T(8,128)(2,1)S(1)}, bf16[96,2048]{1,0:T(8,128)(2,1)S(1)}, u32[]{:S(2)}, u32[]{:S(2)}) collective-permute-start(bf16[96,2048]{1,0:T(8,128)(2,1)S(1)} %broadcast_select_fusion.3), channel_id=1, source_target_pairs={{0,1},{1,0},{2,3},{3,2},{4,5},{5,4},{6,7},{7,6},{8,9},{9,8},{10,11... | collective-permute-start | bytes 1179656 | tf_op jit(solution)/shard_map/ppermute | solution.py:24
  111.7 0.6 copy-start.5

commit v2 on v1

v2 whole, which is shorter than its diff:
```python
import functools
import math

import jax
import jax.numpy as jnp
from jax import lax
from jax.experimental import pallas as pl
from jax.experimental.pallas import tpu as pltpu
from jax.sharding import PartitionSpec as P

HALO = 80
CAP = 2
LANES = 128
PIECES = 2
BLOCK = 1024


def routed(value, route):
    groups, owners = lax.axis_size("kgrp"), lax.axis_size("orb")
    pairs = []
    for group in range(groups):
        for owner in range(owners):
            to_group, to_owner = route(group, owner)
            if 0 <= to_owner < owners:
                pairs.append((group * owners + owner, to_group * owners + to_owner))
    return lax.ppermute(value, ("kgrp", "orb"), pairs)


def to_sibling(value):
    return routed(value, lambda group, owner: (group, owner ^ 1))


def to_pair_chip(value):
    return routed(value, lambda group, owner: (group, owner ^ 2))


def onward(value):
    return routed(value, lambda group, owner: (group, owner + (4 if owner & 2 == 0 else -4)))


def to_other_group(value):
    return routed(value, lambda group, owner: (1 - group, owner))


def shifted(value, steps):
    return routed(value, lambda group, owner: (group, owner + steps))


def after(value, *sooner):
    return lax.optimization_barrier((value,) + sooner)[0]


def pack_kernel(dest_ref, tiles_ref, packed_ref, placed, source):
    slots = packed_ref.shape[0]
    tile_count = dest_ref.shape[0]
    step_count = tiles_ref.shape[0] // tile_count
    first_vector = lax.axis_index("orb") * step_count

    def clear(slot, carry):
        source[slot] = 0
        return carry

    def forget(owner, carry):
        placed[owner] = 0
        return carry

    def place(tile, carry):
        dest = dest_ref[lax.rem(tile, tile_count), first_vector + tile // tile_count]
        rank = placed[dest]
        placed[dest] = rank + 1
        source[dest * CAP + rank] = tile
        return carry

    def fill(slot, carry):
        packed_ref[slot] = tiles_ref[source[slot]]
        return carry

    lax.fori_loop(0, slots, clear, 0, unroll=4)
    lax.fori_loop(0, slots // CAP, forget, 0, unroll=4)
    lax.fori_loop(0, step_count * tile_count, place, 0)
    lax.fori_loop(0, slots, fill, 0, unroll=2)


def pack_tiles(tiles, dest, owners):
    slots = owners * CAP
    vmem = pl.BlockSpec(memory_space=pltpu.VMEM)
    return pl.pallas_call(
        pack_kernel,
        out_shape=jax.ShapeDtypeStruct((slots,) + tiles.shape[1:], tiles.dtype),
        in_specs=[pl.BlockSpec(memory_space=pltpu.SMEM), vmem],
        out_specs=vmem,
        scratch_shapes=[pltpu.SMEM((owners,), jnp.int32), pltpu.SMEM((slots,), jnp.int32)],
        compiler_params=pltpu.CompilerParams(vmem_limit_bytes=40 * 1024 * 1024),
        name="pack_tiles",
    )(dest, tiles)


def weight_kernel(slot_count, point_ref, cell_ref, dest_ref, column_ref, weight_ref):
    tile_count, vectors = dest_ref.shape
    owners = weight_ref.shape[1] // LANES
    step_count = vectors // owners
    k_count = point_ref.shape[0]
    mine = dest_ref[...] == lax.axis_index("orb")
    flags = mine.astype(jnp.float32)
    shape = (tile_count, tile_count)
    before = lax.broadcasted_iota(jnp.int32, shape, 1) < lax.broadcasted_iota(jnp.int32, shape, 0)
    rank = jnp.dot(before.astype(jnp.float32), flags, preferred_element_type=jnp.float32)
    shape = (vectors, vectors)
    sooner, later = lax.broadcasted_iota(jnp.int32, shape, 0), lax.broadcasted_iota(jnp.int32, shape, 1)
    same_owner = (sooner < later) & (sooner >= later - later % step_count)
    counts = jnp.broadcast_to(jnp.sum(flags, axis=0, keepdims=True), (8, vectors))
    above = jnp.dot(counts, same_owner.astype(jnp.float32), preferred_element_type=jnp.float32)
    rank = (rank + above[0:1]).astype(jnp.int32)
    cells = cell_ref[...].astype(jnp.float32)
    column = column_ref[...]
    values = []
    for k in range(k_count):
        fraction = point_ref[k, 0] * cells[0:1] + point_ref[k, 1] * cells[1:2]
        fraction = fraction + point_ref[k, 2] * cells[2:3]
        radians = 6.283185307179586 * fraction
        for wave in (jnp.cos(radians), jnp.sin(radians)):
            phase = wave.astype(jnp.bfloat16).astype(jnp.float32)
            for j in range(slot_count):
                for c in range(CAP):
                    here = mine & (rank == c) & (column == j)
                    values.append(jnp.sum(jnp.where(here, phase, 0.0), axis=0, keepdims=True))
    values = jnp.concatenate(values, axis=0)
    chunk = math.gcd(owners, 16)
    shape = (vectors, chunk * LANES)
    for first in range(0, owners, chunk):
        owner = first + lax.broadcasted_iota(jnp.int32, shape, 1) // LANES
        member = (lax.broadcasted_iota(jnp.int32, shape, 0) // step_count == owner).astype(jnp.float32)
        weight_ref[:, first * LANES : (first + chunk) * LANES] = jnp.dot(
            values, member, preferred_element_type=jnp.float32
        )


def receive_weights(kpoints, cells, dest, column, owners, slot_count):
    k_count = kpoints.shape[0]
    smem, vmem = (pl.BlockSpec(memory_space=space) for space in (pltpu.SMEM, pltpu.VMEM))
    return pl.pallas_call(
        functools.partial(weight_kernel, slot_count),
        out_shape=jax.ShapeDtypeStruct((k_count * 2 * slot_count * CAP, owners * LANES), jnp.float32),
        in_specs=[smem, vmem, vmem, vmem],
        out_specs=vmem,
        compiler_params=pltpu.CompilerParams(vmem_limit_bytes=40 * 1024 * 1024),
        name="receive_weights",
    )(kpoints, cells, dest, column)


def band_kernel(k_count, slot_count, weight_ref, tiles_ref, pair_ref, tail_ref, head_ref):
    slots, rows, width = tiles_ref.shape
    part = rows // 2
    band = slot_count * width
    kinds = k_count * 2 * slot_count
    for low in (0, part):

        def add(owner, totals):
            lanes = pl.ds(pl.multiple_of(owner * LANES, LANES), LANES)
            for c in range(CAP):
                tile = tiles_ref[owner * CAP + c, low : low + part, :].astype(jnp.float32)
                totals = tuple(
                    total + weight_ref[pl.ds(kind * CAP + c, 1), lanes] * tile
                    for kind, total in enumerate(totals)
                )
            return totals

        totals = lax.fori_loop(
            0, slots // CAP, add, tuple(jnp.zeros((part, width), jnp.float32) for _ in range(kinds))
        )
        for k in range(k_count):
            for p in range(2):
                for j in range(slot_count):
                    value = totals[(k * 2 + p) * slot_count + j].astype(jnp.bfloat16)
                    columns = slice(j * width, (j + 1) * width)
                    later = slice(band + j * width, band + (j + 1) * width)
                    if p == 0:
                        pair_ref[k, low : low + part, columns] = value
                        pair_ref[k, rows + low : rows + low + part, later] = value
                    else:
                        pair_ref[k, rows + low : rows + low + part, columns] = value
                        pair_ref[k, low : low + part, later] = -value
    for k in range(k_count):
        for p in range(2):
            tail_ref[k, p] = pair_ref[k, (p + 1) * rows - HALO : (p + 1) * rows, 0:band]
            head_ref[k, p] = pair_ref[k, p * rows : p * rows + HALO, 0:band]


def make_bands(weights, tiles, k_count, slot_count):
    rows, width = tiles.shape[1:]
    band = slot_count * width
    vmem = pl.BlockSpec(memory_space=pltpu.VMEM)
    edge = jax.ShapeDtypeStruct((k_count, 2, HALO, band), jnp.bfloat16)
    return pl.pallas_call(
        functools.partial(band_kernel, k_count, slot_count),
        out_shape=[jax.ShapeDtypeStruct((k_count, 2 * rows, 2 * band), jnp.bfloat16), edge, edge],
        in_specs=[vmem, vmem],
        out_specs=[vmem, vmem, vmem],
        compiler_params=pltpu.CompilerParams(vmem_limit_bytes=40 * 1024 * 1024),
        name="make_bands",
    )(weights, tiles)


def filter_kernel(pieces, block_of, where_ref, pair_ref, left_ref, right_ref, own_ref, sibling_ref, *rest):
    chip_refs, onward_refs, near_refs = (rest[part * pieces : (part + 1) * pieces] for part in range(3))
    out_ref, window, sems = rest[-3:]
    k_count, double_rows, _ = pair_ref.shape
    rows = double_rows // 2
    band = left_ref.shape[-1]
    block = out_ref.shape[-1]
    piece_steps = chip_refs[0].shape[1] // block
    steps = pieces * piece_steps
    step = pl.program_id(0)
    odd_chip, odd_core, first_block = where_ref[0], where_ref[1], block_of(where_ref[2])
    starts = [0, HALO, HALO + rows, HALO + 2 * rows, HALO + 3 * rows]

    def begin(number, slot):
        whole = pl.ds(pl.multiple_of((first_block + number) * block, block), block)
        piece = pl.ds(pl.multiple_of(lax.rem(number, piece_steps) * block, block), block)

        def fetch(source, part):
            count = source.shape[0]
            pltpu.make_async_copy(
                source, window.at[slot, starts[part] : starts[part] + count, :], sems.at[slot, part]
            ).start()

        fetch(own_ref.at[:, whole], 2)
        for odd in (0, 1):

            @pl.when(odd_core == odd)
            def _():
                fetch(sibling_ref.at[:, whole], 1 if odd else 3)

            for index in range(pieces):
                inside = number // piece_steps == index

                @pl.when((odd_core == odd) & inside)
                def _():
                    fetch(near_refs[index].at[:, piece], 3 if odd else 1)

                @pl.when((odd_chip == odd) & inside)
                def _():
                    before, after = chip_refs[index], onward_refs[index]
                    if odd == 0:
                        before, after = after, before
                    fetch(before.at[rows - HALO : rows, piece], 0)
                    fetch(after.at[0:HALO, piece], 4)

    @pl.when(step == 0)
    def _():
        begin(0, 0)

    slot = lax.rem(step, 2)

    @pl.when(step + 1 < steps)
    def _():
        begin(step + 1, 1 - slot)

    for part in range(5):
        count = HALO if part in (0, 4) else rows
        target = window.at[slot, starts[part] : starts[part] + count, :]
        pltpu.make_async_copy(target, target, sems.at[slot, part]).wait()

    def product(left, right):
        return jnp.dot(left, right, preferred_element_type=jnp.float32)

    lower = window[slot, 0:band, :]
    middle = window[slot, rows : rows + band, :]
    upper = window[slot, 2 * rows : 2 * rows + band, :]
    own_band = jnp.concatenate([pair_ref[k][:, 0:band] for k in range(k_count)], axis=0)
    edges = k_count * 2 * HALO
    own_first = product(own_band, middle).astype(jnp.bfloat16)
    left_first = product(left_ref[...].reshape(edges, band), lower).astype(jnp.bfloat16)
    right_first = product(right_ref[...].reshape(edges, band), upper).astype(jnp.bfloat16)
    center = window[slot, HALO + rows : HALO + 2 * rows, :].astype(jnp.float32)
    for k in range(k_count):
        wide = jnp.concatenate(
            [
                part
                for kind in (2 * k, 2 * k + 1)
                for part in (
                    left_first[kind * HALO : (kind + 1) * HALO],
                    own_first[kind * rows : (kind + 1) * rows],
                    right_first[kind * HALO : (kind + 1) * HALO],
                )
            ],
            axis=0,
        )
        both = 2.0 * product(pair_ref[k], wide)
        out_ref[k, 0] = (both[0:rows] - center).astype(jnp.bfloat16)
        out_ref[k, 1] = both[rows:].astype(jnp.bfloat16)


def filter_columns(where, block_of, pair, left, right, own, sibling, halos, so_far):
    k_count, double_rows, _ = pair.shape
    rows = double_rows // 2
    columns = own.shape[1]
    pieces = len(halos)
    width = halos[0][0].shape[1]
    block = min(BLOCK, width)
    vmem = pl.BlockSpec(memory_space=pltpu.VMEM)
    hbm = pl.BlockSpec(memory_space=pltpu.HBM)
    operands = [where, pair, left, right, own, sibling]
    operands += [halo[part] for part in range(3) for halo in halos]
    specs = [vmem] * 3 + [hbm] * (2 + 3 * pieces)
    aliases = {}
    if so_far is not None:
        aliases = {len(operands): 0}
        operands.append(so_far)
        specs.append(hbm)
    return pl.pallas_call(
        functools.partial(filter_kernel, pieces, block_of),
        out_shape=jax.ShapeDtypeStruct((k_count, 2, rows, columns), jnp.bfloat16),
        grid_spec=pltpu.PrefetchScalarGridSpec(
            num_scalar_prefetch=1,
            grid=(pieces * width // block,),
            in_specs=specs,
            out_specs=pl.BlockSpec((k_count, 2, rows, block), lambda i, where: (0, 0, 0, block_of(where[2]) + i)),
            scratch_shapes=[
                pltpu.VMEM((2, 3 * rows + 2 * HALO, block), jnp.bfloat16),
                pltpu.SemaphoreType.DMA((2, 5)),
            ],
        ),
        input_output_aliases=aliases,
        compiler_params=pltpu.CompilerParams(
            vmem_limit_bytes=40 * 1024 * 1024, dimension_semantics=("arbitrary",)
        ),
        cost_estimate=pl.CostEstimate(
            flops=2 * pieces * width * k_count * (4 * 256 * 256 + 2 * 192 * 256),
            bytes_accessed=pieces * width * 2 * (448 + 384),
            transcendentals=0,
        ),
        name="filter_columns",
    )(*operands)


def local(hopping_tiles, tile_strip, tile_column_slot, lattice, kpoints, start_block):
    owners = lax.axis_size("orb")
    device = lax.axis_index("orb")
    group = lax.axis_index("kgrp")
    odd_core = device & 1
    odd_chip = (device >> 1) & 1
    step_count, tile_count, row_count, col_width = hopping_tiles.shape
    slot_count = (row_count + 2 * HALO) // col_width
    k_count = kpoints.shape[0]
    half = start_block.shape[1] // 2
    piece = half // PIECES
    block = min(BLOCK, piece)

    dest = jnp.transpose(tile_strip, (2, 1, 0))[0]
    tiles = hopping_tiles.reshape(step_count * tile_count, row_count, col_width)
    outgoing = pack_tiles(tiles, dest, owners)
    incoming = lax.all_to_all(outgoing, "orb", split_axis=0, concat_axis=0, tiled=True)
    weights = receive_weights(kpoints, lattice.T, dest, tile_column_slot.T, owners, slot_count)

    chips, beyonds = [], []
    for number in range(PIECES):
        source = after(start_block, *chips[-1:])
        chip = to_pair_chip(lax.dynamic_slice_in_dim(source, group * half + number * piece, piece, axis=1))
        chips.append(after(chip, outgoing))
        beyonds.append(onward(chips[-1]))
    other_chips = [to_other_group(chip) for chip in chips]

    pair, tail, head = make_bands(weights, after(incoming, *other_chips), k_count, slot_count)
    left = shifted(tail, 1)
    right = shifted(head, -1)

    sibling = to_sibling(start_block)
    where = jnp.stack([odd_chip, odd_core, group]).astype(jnp.int32)

    def filtered(other, halos, so_far):
        return filter_columns(
            where,
            lambda group: (group + other - 2 * group * other) * (half // block),
            pair,
            left,
            right,
            start_block,
            sibling,
            halos,
            so_far,
        )

    passes = odd_chip == odd_core

    def to_near(chip, beyond):
        return to_sibling(jnp.where(passes, chip, beyond))

    beyonds[-1] = after(beyonds[-1], pair)
    other_beyonds = [to_other_group(beyond) for beyond in beyonds]
    nears = [to_near(chip, beyond) for chip, beyond in zip(chips, beyonds)]
    nears[0] = after(nears[0], *other_beyonds[:-1])
    result = filtered(0, list(zip(chips, beyonds, nears)), None)
    other_beyonds = [after(beyond, result) for beyond in other_beyonds]
    other_nears = [to_near(chip, beyond) for chip, beyond in zip(other_chips, other_beyonds)]
    return filtered(1, list(zip(other_chips, other_beyonds, other_nears)), result)


def solution(mesh):
    return jax.shard_map(
        local,
        mesh=mesh,
        in_specs=(P("orb", None, None, None), P(), P(), P(), P("kgrp", None), P("orb", None)),
        out_specs=P("kgrp", None, "orb", None),
        check_vma=False,
    )
```

time: 135 us -> 81.1 us (0.60)
  Pallas kernels: 50.1 us -> 19.8 us
  local copies, waits for them, and re-layouts: 19.2 us -> 3.59 us
  other arithmetic: 15.5 us -> 3.04 us
  waiting for transfers between devices: 20.9 us -> 26.5 us
    pallas_call x5 -> x4, Pallas kernels: 47.6 us -> 18.4 us  [the longest x2 15.2 us: filter_columns(): pl.pallas_call(functools.partial(filter_kernel, pieces, block_of), out_sh...]
    ppermute x15, waiting for transfers between devices: 20.9 us -> 26.5 us  [routed(): return lax.ppermute(value, ('kgrp', 'orb'), pairs)]
    eq x3 -> x0, local copies, waits for them, and re-layouts: 3.51 us -> none  [the longest x2 2.13 us: receive_weights(): mine = dest_all.reshape(owners, total) == device]
    another operation x5 -> x1, other arithmetic: 3.26 us -> 0.08 us  [local(): where = jnp.stack([odd_chip, odd_core, group]).astype(jnp.int32)]
    transpose x2 -> x0, local copies, waits for them, and re-layouts: 2.91 us -> none  [the longest x1 1.47 us: receive_weights(): phase_all.transpose(2, 0, 1)[:, None, None]]
    eq x2 -> x0, other arithmetic: 2.59 us -> none  [the longest x1 1.3 us: receive_weights(): column[None, None]]
    reduce_sum x2 -> x0, other arithmetic: 2.52 us -> none  [the longest x1 1.47 us: receive_weights(): jnp.sum(jnp.where(chosen[None], phase_all.transpose(2, 0, 1)[:, None, Non...]
    select_n x5 -> x4, other arithmetic: 5.2 us -> 2.96 us  [to_near(): return to_sibling(jnp.where(passes, chip, beyond))]
  transfers between devices with their start and end apart: 16 -> 16, of which waited for: 3 -> 6; matrix products, arithmetic and copies ran while one was open for 25% -> 4% of each run, Pallas kernels for 34% -> 15%
where the time goes in v2:
time: 81.1 us; the launch traced here: 80.5 us
  starting transfers between devices  27.5 us (34%)
  waiting for transfers between devices  26.5 us (33%)
  Pallas kernels  19.8 us (24%)
  local copies, waits for them, and re-layouts  3.59 us (4%)
  other arithmetic  3.04 us (4%)
    ppermute x15, waiting for transfers between devices, routed(): return lax.ppermute(value, ('kgrp', 'orb'), pairs)  26.5 us
    ppermute x15, starting transfers between devices, routed(): return lax.ppermute(value, ('kgrp', 'orb'), pairs)  20.6 us
    pallas_call x2, Pallas kernels, filter_columns(): pl.pallas_call(functools.partial(filter_kernel, pieces, block_of), out_sh...  15.2 us
    all_to_all x1, starting transfers between devices, local(): lax.all_to_all(outgoing, 'orb', split_axis=0, concat_axis=0, tiled=True)  6.86 us
    select_n x4, other arithmetic, to_near(): return to_sibling(jnp.where(passes, chip, beyond))  2.96 us
    pallas_call x1, Pallas kernels, pack_tiles(): pl.pallas_call(pack_kernel, out_shape=jax.ShapeDtypeStruct((slots,) + til...  2.39 us
    dynamic_slice x2, local copies, waits for them, and re-layouts, local(): lax.dynamic_slice_in_dim(source, group * half + number * piece, piece, ax...  1.82 us
    unnamed x11, local copies, waits for them, and re-layouts  1.77 us
  transfers between devices with their start and end apart: 16, of which 6 were waited for; matrix products, arithmetic and copies ran while one was open for 4% of the time, Pallas kernels for 15%

profile of v2, /device:TPU:11, one launch (start us, length us, event | category | flops | bytes accessed | tf_op | source)
XLA Modules:
  0.0 80.5 jit_solution(4839766361085771172)
XLA Ops:
  0.0 1.0 %constant_dynamic-slice_fusion.1 = bf16[96,2048]{1,0:T(8,128)(2,1)S(1)} fusion(bf16[96,8192]{1,0:T(8,128)(2,1)} %own_ref.3, s32[]{:T(128)S(6)} %select_n.26), kind=kLoop, calls=%fused_computation.7 | loop fusion | bytes 786436 | tf_op jit(solution)/shard_map/dynamic_slice | solution.py:359
  1.0 0.3 collective-permute-start
  1.3 0.7 copy.10
  2.0 0.0 copy-start
  2.0 1.1 %copy-done = bf16[2,12,96,128]{3,2,1,0:T(8,128)(2,1)S(1)} copy-done((bf16[2,12,96,128]{3,2,1,0:T(8,128)(2,1)S(1)}, bf16[2,12,96,128]{3,2,1,0:T(8,128)(2,1)}, u32[]{:S(2)}) %copy-start) | copy-done | bytes 589848
  3.1 0.0 copy-start.1
  3.1 0.0 copy-start.2
  3.1 0.0 copy-start.3
  3.1 0.0 copy-start.4
  3.1 2.4 %pack_tiles.1 = bf16[32,96,128]{2,1,0:T(8,128)(2,1)} custom-call(s32[12,32]{1,0:T(8,128)S(1)} %bitcast.12, bf16[24,96,128]{2,1,0:T(8,128)(2,1)S(1)} %bitcast.11), custom_call_target="tpu_custom_call" | custom-call | tf_op jit(solution)/shard_map/pack_tiles/pallas_call | solution.py:87
  5.5 6.9 %all-to-all-start = ((bf16[32,96,128]{2,1,0:T(8,128)(2,1)}), bf16[32,96,128]{2,1,0:T(8,128)(2,1)S(1)}, u32[]{:S(2)}, u32[]{:S(2)}) async-start(bf16[32,96,128]{2,1,0:T(8,128)(2,1)} %pack_tiles.1), calls=%async_computation | async-start | bytes 1572864 | tf_op jit(solution)/shard_map/all_to_all | solution.py:353
  12.4 0.0 collective-permute-done.rest_0_
  12.4 0.0 copy-done.1
  12.4 0.8 constant_dynamic-slice_fusion
  13.2 0.3 collective-permute-start.2
  13.5 2.0 %collective-permute-start.7 = (bf16[96,2048]{1,0:T(8,128)(2,1)S(1)}, bf16[96,2048]{1,0:T(8,128)(2,1)}, u32[]{:S(2)}, u32[]{:S(2)}) collective-permute-start(bf16[96,2048]{1,0:T(8,128)(2,1)S(1)} %collective-permute-done.rest_0_), channel_id=1, source_target_pairs={{0,4},{1,5},{4,8},{5,9},{6,2},{7,3},{8,12},{9,13},{10,6},{11,7},{1... | collective-permute-start | bytes 1179656 | tf_op jit(solution)/shard_map/ppermute | solution.py:26
  15.5 0.7 collective-permute-start.6
  16.2 0.0 copy-done.2
  16.2 0.0 copy-done.3
  16.2 0.0 copy-done.4
  16.2 0.8 %receive_weights.1.weight_ref = f32[16,2048]{1,0:T(8,128)S(1)} custom-call(f32[2,3]{1,0:T(2,128)S(1)} %copy-done.4, s32[3,32]{1,0:T(4,128)S(1)} %bitcast.15, s32[12,32]{1,0:T(8,128)S(1)} %bitcast.13, s32[12,32]{1,0:T(8,128)S(1)} %bitcast.14), custom_call_target="tpu_custom_call" | custom-call | tf_op jit(solution)/shard_map/receive_weights/pallas_call | solution.py:141
  17.0 1.5 %collective-permute-start.1 = (bf16[96,2048]{1,0:T(8,128)(2,1)S(1)}, bf16[96,2048]{1,0:T(8,128)(2,1)S(1)}, u32[]{:S(2)}, u32[]{:S(2)}) collective-permute-start(bf16[96,2048]{1,0:T(8,128)(2,1)S(1)} %collective-permute-done.rest_0_), channel_id=1, source_target_pairs={{0,16},{1,17},{2,18},{3,19},{4,20},{5,21},{6,22},{7,23},{8,24},{9,... | collective-permute-start | bytes 1179656 | tf_op jit(solution)/shard_map/ppermute | solution.py:26
  18.5 11.0 %collective-permute-done.2.rest_1_ = bf16[96,2048]{1,0:T(8,128)(2,1)} collective-permute-done((bf16[96,2048]{1,0:T(8,128)(2,1)}, bf16[96,2048]{1,0:T(8,128)(2,1)}, u32[]{:S(2)}, u32[]{:S(2)}) %collective-permute-start.2) | collective-permute-done | bytes 393248 | tf_op jit(solution)/shard_map/ppermute | solution.py:26
  29.5 2.0 %collective-permute-start.9 = (bf16[96,2048]{1,0:T(8,128)(2,1)}, bf16[96,2048]{1,0:T(8,128)(2,1)}, u32[]{:S(2)}, u32[]{:S(2)}) collective-permute-start(bf16[96,2048]{1,0:T(8,128)(2,1)} %collective-permute-done.2.rest_1_), channel_id=1, source_target_pairs={{0,4},{1,5},{4,8},{5,9},{6,2},{7,3},{8,12},{9,13},{10,6},{11,7},{1... | collective-permute-start | bytes 1179656 | tf_op jit(solution)/shard_map/ppermute | solution.py:26
  31.5 1.3 %collective-permute-start.3 = (bf16[96,2048]{1,0:T(8,128)(2,1)}, bf16[96,2048]{1,0:T(8,128)(2,1)}, u32[]{:S(2)}, u32[]{:S(2)}) collective-permute-start(bf16[96,2048]{1,0:T(8,128)(2,1)} %collective-permute-done.2.rest_1_), channel_id=1, source_target_pairs={{0,16},{1,17},{2,18},{3,19},{4,20},{5,21},{6,22},{7,23},{8,24},{9,... | collective-permute-start | bytes 1179656 | tf_op jit(solution)/shard_map/ppermute | solution.py:26
  32.8 7.2 %collective-permute-done.7.rest_2_ = bf16[96,2048]{1,0:T(8,128)(2,1)} collective-permute-done((bf16[96,2048]{1,0:T(8,128)(2,1)S(1)}, bf16[96,2048]{1,0:T(8,128)(2,1)}, u32[]{:S(2)}, u32[]{:S(2)}) %collective-permute-start.7) | collective-permute-done | bytes 393248 | tf_op jit(solution)/shard_map/ppermute | solution.py:26
  40.0 0.8 broadcast_select_fusion.3
  40.8 2.3 %collective-permute-start.10 = (bf16[96,2048]{1,0:T(8,128)(2,1)}, bf16[96,2048]{1,0:T(8,128)(2,1)}, u32[]{:S(2)}, u32[]{:S(2)}) collective-permute-start(bf16[96,2048]{1,0:T(8,128)(2,1)} %broadcast_select_fusion.3), channel_id=1, source_target_pairs={{0,1},{1,0},{2,3},{3,2},{4,5},{5,4},{6,7},{7,6},{8,9},{9,8},{10,11... | collective-permute-start | bytes 1179656 | tf_op jit(solution)/shard_map/ppermute | solution.py:26
  43.1 0.0 collective-permute-done.1.rest_0_
  43.1 1.2 %collective-permute-start.8 = (bf16[96,2048]{1,0:T(8,128)(2,1)}, bf16[96,2048]{1,0:T(8,128)(2,1)}, u32[]{:S(2)}, u32[]{:S(2)}) collective-permute-start(bf16[96,2048]{1,0:T(8,128)(2,1)} %collective-permute-done.7.rest_2_), channel_id=1, source_target_pairs={{0,16},{1,17},{2,18},{3,19},{4,20},{5,21},{6,22},{7,23},{8,24},{9,... | collective-permute-start | bytes 1179656 | tf_op jit(solution)/shard_map/ppermute | solution.py:26
  44.4 0.0 collective-permute-done.3.rest_1_
  44.4 0.0 all-to-all-done.tiles_ref
  44.4 1.4 %make_bands.1 = (bf16[2,192,512]{2,1,0:T(8,128)(2,1)S(1)}, bf16[2,2,80,256]{3,2,1,0:T(8,128)(2,1)S(1)}, bf16[2,2,80,256]{3,2,1,0:T(8,128)(2,1)S(1)}) custom-call(f32[16,2048]{1,0:T(8,128)S(1)} %receive_weights.1.weight_ref, bf16[32,96,128]{2,1,0:T(8,128)(2,1)S(1)} %all-to-all-done.tiles_ref), custom_call_target="tpu_custom_call" | custom-call | tf_op jit(solution)/shard_map/make_bands/pallas_call | solution.py:194
  45.8 2.7 %collective-permute-done.9.rest_3_ = bf16[96,2048]{1,0:T(8,128)(2,1)} collective-permute-done((bf16[96,2048]{1,0:T(8,128)(2,1)}, bf16[96,2048]{1,0:T(8,128)(2,1)}, u32[]{:S(2)}, u32[]{:S(2)}) %collective-permute-start.9) | collective-permute-done | bytes 393248 | tf_op jit(solution)/shard_map/ppermute | solution.py:26
  48.4 1.0 %broadcast_select_fusion.2 = bf16[96,2048]{1,0:T(8,128)(2,1)S(1)} fusion(bf16[96,2048]{1,0:T(8,128)(2,1)} %collective-permute-done.2.rest_1_, bf16[96,2048]{1,0:T(8,128)(2,1)} %collective-permute-done.9.rest_3_, pred[]{:T(512)S(6)} %eq.3), kind=kLoop, calls=%fused_computation.2 | loop fusion | flops 196608 | bytes 1179649 | tf_op jit(solution)/shard_map/jit(_where)/select_n | solution.py:387
  49.5 0.9 %collective-permute-start.11 = (bf16[96,2048]{1,0:T(8,128)(2,1)S(1)}, bf16[96,2048]{1,0:T(8,128)(2,1)S(1)}, u32[]{:S(2)}, u32[]{:S(2)}) collective-permute-start(bf16[96,2048]{1,0:T(8,128)(2,1)S(1)} %broadcast_select_fusion.2), channel_id=1, source_target_pairs={{0,1},{1,0},{2,3},{3,2},{4,5},{5,4},{6,7},{7,6},{8,9},{9,8},{10,11... | collective-permute-start | bytes 1179656 | tf_op jit(solution)/shard_map/ppermute | solution.py:26
  50.4 3.2 %collective-permute-start.4 = (bf16[2,2,80,256]{3,2,1,0:T(8,128)(2,1)S(1)}, bf16[2,2,80,256]{3,2,1,0:T(8,128)(2,1)S(1)}, u32[]{:S(2)}, u32[]{:S(2)}) collective-permute-start(bf16[2,2,80,256]{3,2,1,0:T(8,128)(2,1)S(1)} %get-tuple-element.21), channel_id=1, source_target_pairs={{0,1},{1,2},{2,3},{3,4},{4,5},{5,6},{6,7},{7,8},{8,9},{9,10},{10,1... | collective-permute-start | bytes 491528 | tf_op jit(solution)/shard_map/ppermute | solution.py:26
  53.7 0.0 collective-permute-done.10.rest_4_
  53.7 1.9 %collective-permute-start.5 = (bf16[2,2,80,256]{3,2,1,0:T(8,128)(2,1)S(1)}, bf16[2,2,80,256]{3,2,1,0:T(8,128)(2,1)S(1)}, u32[]{:S(2)}, u32[]{:S(2)}) collective-permute-start(bf16[2,2,80,256]{3,2,1,0:T(8,128)(2,1)S(1)} %get-tuple-element.22), channel_id=1, source_target_pairs={{1,0},{2,1},{3,2},{4,3},{5,4},{6,5},{7,6},{8,7},{9,8},{10,9},{11,1... | collective-permute-start | bytes 491528 | tf_op jit(solution)/shard_map/ppermute | solution.py:26
  55.6 0.1 pad_add_fusion.where_ref
  55.7 0.0 collective-permute-done.8.rest_2_
  55.7 1.3 %collective-permute-start.12 = (bf16[96,2048]{1,0:T(8,128)(2,1)}, bf16[96,2048]{1,0:T(8,128)(2,1)S(1)}, u32[]{:S(2)}, u32[]{:S(2)}) collective-permute-start(bf16[96,2048]{1,0:T(8,128)(2,1)} %collective-permute-done.9.rest_3_), channel_id=1, source_target_pairs={{0,16},{1,17},{2,18},{3,19},{4,20},{5,21},{6,22},{7,23},{8,24},{9,... | collective-permute-start | bytes 1179656 | tf_op jit(solution)/shard_map/ppermute | solution.py:26
  56.9 0.0 collective-permute-done.6.sibling_ref
  56.9 0.0 collective-permute-done.4.left_ref
  56.9 4.3 %collective-permute-done.5.right_ref = bf16[2,2,80,256]{3,2,1,0:T(8,128)(2,1)S(1)} collective-permute-done((bf16[2,2,80,256]{3,2,1,0:T(8,128)(2,1)S(1)}, bf16[2,2,80,256]{3,2,1,0:T(8,128)(2,1)S(1)}, u32[]{:S(2)}, u32[]{:S(2)}) %collective-permute-start.5) | collective-permute-done | bytes 163872 | tf_op jit(solution)/shard_map/ppermute | solution.py:26
  61.2 0.0 collective-permute-done.11.rest_5_
  61.2 7.6 %filter_columns.2.rest_6_ = bf16[2,2,96,8192]{3,2,1,0:T(8,128)(2,1)} custom-call(s32[3]{0:T(128)S(1)} %pad_add_fusion.where_ref, bf16[2,192,512]{2,1,0:T(8,128)(2,1)S(1)} %get-tuple-element.20.pair_ref, bf16[2,2,80,256]{3,2,1,0:T(8,128)(2,1)S(1)} %collective-permute-done.4.left_ref, bf16[2,2,80,256]{3,2,1,0:T(8,128)(2,1)S(1)} %collective-permute-done.5.right_ref, ...), custom_call_target="tpu_custom_call" | custom-call | flops 5905580032 | bytes 6815744 | tf_op jit(solution)/shard_map/filter_columns/pallas_call | solution.py:311
  68.8 0.0 collective-permute-done.12.rest_3_
  68.9 1.1 %broadcast_select_fusion = bf16[96,2048]{1,0:T(8,128)(2,1)S(1)} fusion(bf16[96,2048]{1,0:T(8,128)(2,1)} %collective-permute-done.3.rest_1_, bf16[96,2048]{1,0:T(8,128)(2,1)S(1)} %collective-permute-done.12.rest_3_, pred[]{:T(512)S(6)} %eq.3), kind=kLoop, calls=%fused_computation | loop fusion | flops 196608 | bytes 1179649 | tf_op jit(solution)/shard_map/jit(_where)/select_n | solution.py:387
  69.9 0.1 collective-permute-start.14
  70.0 0.1 broadcast_select_fusion.1
  70.1 1.5 %collective-permute-start.13 = (bf16[96,2048]{1,0:T(8,128)(2,1)S(1)}, bf16[96,2048]{1,0:T(8,128)(2,1)S(1)}, u32[]{:S(2)}, u32[]{:S(2)}) collective-permute-start(bf16[96,2048]{1,0:T(8,128)(2,1)S(1)} %broadcast_select_fusion.1), channel_id=1, source_target_pairs={{0,1},{1,0},{2,3},{3,2},{4,5},{5,4},{6,7},{7,6},{8,9},{9,8},{10,11... | collective-permute-start | bytes 1179656 | tf_op jit(solution)/shard_map/ppermute | solution.py:26
  71.6 0.1 collective-permute-done.14.rest_5_
  71.7 1.2 %collective-permute-done.13.rest_4_ = bf16[96,2048]{1,0:T(8,128)(2,1)S(1)} collective-permute-done((bf16[96,2048]{1,0:T(8,128)(2,1)S(1)}, bf16[96,2048]{1,0:T(8,128)(2,1)S(1)}, u32[]{:S(2)}, u32[]{:S(2)}) %collective-permute-start.13) | collective-permute-done | bytes 393248 | tf_op jit(solution)/shard_map/ppermute | solution.py:26
  73.0 7.6 %filter_columns.3 = bf16[2,2,96,8192]{3,2,1,0:T(8,128)(2,1)} custom-call(s32[3]{0:T(128)S(1)} %pad_add_fusion.where_ref, bf16[2,192,512]{2,1,0:T(8,128)(2,1)S(1)} %get-tuple-element.20.pair_ref, bf16[2,2,80,256]{3,2,1,0:T(8,128)(2,1)S(1)} %collective-permute-done.4.left_ref, ...), custom_call_target="tpu_custom_call", output_to_operand_aliasing={{}: (12, {})} | custom-call | flops 5905580032 | bytes 6815744 | tf_op jit(solution)/shard_map/filter_columns/pallas_call | solution.py:311
Async XLA Ops:
  1.0 11.3 %collective-permute-start = (bf16[96,2048]{1,0:T(8,128)(2,1)S(1)}, bf16[96,2048]{1,0:T(8,128)(2,1)S(1)}, u32[]{:S(2)}, u32[]{:S(2)}) collective-permute-start(bf16[96,2048]{1,0:T(8,128)(2,1)S(1)} %constant_dynamic-slice_fusion.1), channel_id=1, source_target_pairs={{0,2},{1,3},{2,0},{3,1},{4,6},{5,7},{6,4},{7,5},{8,10},{9,11},{10,... | collective-permute-start | bytes 1179656 | tf_op jit(solution)/shard_map/ppermute | solution.py:26
  2.0 1.1 %copy-start = (bf16[2,12,96,128]{3,2,1,0:T(8,128)(2,1)S(1)}, bf16[2,12,96,128]{3,2,1,0:T(8,128)(2,1)}, u32[]{:S(2)}) copy-start(bf16[2,12,96,128]{3,2,1,0:T(8,128)(2,1)} %param.6) | copy-start | bytes 1769476
  3.1 9.3 %copy-start.1 = (bf16[96,8192]{1,0:T(8,128)(2,1)S(1)}, bf16[96,8192]{1,0:T(8,128)(2,1)}, u32[]{:S(2)}) copy-start(bf16[96,8192]{1,0:T(8,128)(2,1)} %own_ref.3) | copy-start | bytes 4718596
  3.1 13.1 %copy-start.2 = (s32[32,12]{0,1:T(8,128)S(1)}, s32[32,12]{0,1:T(8,128)}, u32[]{:S(2)}) copy-start(s32[32,12]{0,1:T(8,128)} %param.8) | copy-start | bytes 4612
  3.1 13.1 %copy-start.3 = (s32[32,3]{0,1:T(4,128)S(1)}, s32[32,3]{0,1:T(4,128)}, u32[]{:S(2)}) copy-start(s32[32,3]{0,1:T(4,128)} %param.9) | copy-start | bytes 1156
  3.1 13.1 %copy-start.4 = (f32[2,3]{1,0:T(2,128)S(1)}, f32[2,3]{1,0:T(2,128)}, u32[]{:S(2)}) copy-start(f32[2,3]{1,0:T(2,128)} %point_ref.1) | copy-start | bytes 76
  5.5 38.9 %all-to-all-start = ((bf16[32,96,128]{2,1,0:T(8,128)(2,1)}), bf16[32,96,128]{2,1,0:T(8,128)(2,1)S(1)}, u32[]{:S(2)}, u32[]{:S(2)}) async-start(bf16[32,96,128]{2,1,0:T(8,128)(2,1)} %pack_tiles.1), calls=%async_computation | async-start | bytes 1572864 | tf_op jit(solution)/shard_map/all_to_all | solution.py:353
  13.2 16.3 %collective-permute-start.2 = (bf16[96,2048]{1,0:T(8,128)(2,1)}, bf16[96,2048]{1,0:T(8,128)(2,1)}, u32[]{:S(2)}, u32[]{:S(2)}) collective-permute-start(bf16[96,2048]{1,0:T(8,128)(2,1)} %constant_dynamic-slice_fusion), channel_id=1, source_target_pairs={{0,2},{1,3},{2,0},{3,1},{4,6},{5,7},{6,4},{7,5},{8,10},{9,11},{10,... | collective-permute-start | bytes 1179656 | tf_op jit(solution)/shard_map/ppermute | solution.py:26
  13.5 26.5 %collective-permute-start.7 = (bf16[96,2048]{1,0:T(8,128)(2,1)S(1)}, bf16[96,2048]{1,0:T(8,128)(2,1)}, u32[]{:S(2)}, u32[]{:S(2)}) collective-permute-start(bf16[96,2048]{1,0:T(8,128)(2,1)S(1)} %collective-permute-done.rest_0_), channel_id=1, source_target_pairs={{0,4},{1,5},{4,8},{5,9},{6,2},{7,3},{8,12},{9,13},{10,6},{11,7},{1... | collective-permute-start | bytes 1179656 | tf_op jit(solution)/shard_map/ppermute | solution.py:26
  15.5 41.5 %collective-permute-start.6 = (bf16[96,8192]{1,0:T(8,128)(2,1)S(1)}, bf16[96,8192]{1,0:T(8,128)(2,1)}, u32[]{:S(2)}, u32[]{:S(2)}) collective-permute-start(bf16[96,8192]{1,0:T(8,128)(2,1)S(1)} %copy-done.1), channel_id=1, source_target_pairs={{0,1},{1,0},{2,3},{3,2},{4,5},{5,4},{6,7},{7,6},{8,9},{9,8},{10,11... | collective-permute-start | bytes 4718600 | tf_op jit(solution)/shard_map/ppermute | solution.py:26
  17.0 26.1 %collective-permute-start.1 = (bf16[96,2048]{1,0:T(8,128)(2,1)S(1)}, bf16[96,2048]{1,0:T(8,128)(2,1)S(1)}, u32[]{:S(2)}, u32[]{:S(2)}) collective-permute-start(bf16[96,2048]{1,0:T(8,128)(2,1)S(1)} %collective-permute-done.rest_0_), channel_id=1, source_target_pairs={{0,16},{1,17},{2,18},{3,19},{4,20},{5,21},{6,22},{7,23},{8,24},{9,... | collective-permute-start | bytes 1179656 | tf_op jit(solution)/shard_map/ppermute | solution.py:26
  29.5 18.9 %collective-permute-start.9 = (bf16[96,2048]{1,0:T(8,128)(2,1)}, bf16[96,2048]{1,0:T(8,128)(2,1)}, u32[]{:S(2)}, u32[]{:S(2)}) collective-permute-start(bf16[96,2048]{1,0:T(8,128)(2,1)} %collective-permute-done.2.rest_1_), channel_id=1, source_target_pairs={{0,4},{1,5},{4,8},{5,9},{6,2},{7,3},{8,12},{9,13},{10,6},{11,7},{1... | collective-permute-start | bytes 1179656 | tf_op jit(solution)/shard_map/ppermute | solution.py:26
  31.5 12.9 %collective-permute-start.3 = (bf16[96,2048]{1,0:T(8,128)(2,1)}, bf16[96,2048]{1,0:T(8,128)(2,1)}, u32[]{:S(2)}, u32[]{:S(2)}) collective-permute-start(bf16[96,2048]{1,0:T(8,128)(2,1)} %collective-permute-done.2.rest_1_), channel_id=1, source_target_pairs={{0,16},{1,17},{2,18},{3,19},{4,20},{5,21},{6,22},{7,23},{8,24},{9,... | collective-permute-start | bytes 1179656 | tf_op jit(solution)/shard_map/ppermute | solution.py:26
  40.8 12.9 %collective-permute-start.10 = (bf16[96,2048]{1,0:T(8,128)(2,1)}, bf16[96,2048]{1,0:T(8,128)(2,1)}, u32[]{:S(2)}, u32[]{:S(2)}) collective-permute-start(bf16[96,2048]{1,0:T(8,128)(2,1)} %broadcast_select_fusion.3), channel_id=1, source_target_pairs={{0,1},{1,0},{2,3},{3,2},{4,5},{5,4},{6,7},{7,6},{8,9},{9,8},{10,11... | collective-permute-start | bytes 1179656 | tf_op jit(solution)/shard_map/ppermute | solution.py:26
  43.1 12.5 %collective-permute-start.8 = (bf16[96,2048]{1,0:T(8,128)(2,1)}, bf16[96,2048]{1,0:T(8,128)(2,1)}, u32[]{:S(2)}, u32[]{:S(2)}) collective-permute-start(bf16[96,2048]{1,0:T(8,128)(2,1)} %collective-permute-done.7.rest_2_), channel_id=1, source_target_pairs={{0,16},{1,17},{2,18},{3,19},{4,20},{5,21},{6,22},{7,23},{8,24},{9,... | collective-permute-start | bytes 1179656 | tf_op jit(solution)/shard_map/ppermute | solution.py:26
  49.5 11.7 %collective-permute-start.11 = (bf16[96,2048]{1,0:T(8,128)(2,1)S(1)}, bf16[96,2048]{1,0:T(8,128)(2,1)S(1)}, u32[]{:S(2)}, u32[]{:S(2)}) collective-permute-start(bf16[96,2048]{1,0:T(8,128)(2,1)S(1)} %broadcast_select_fusion.2), channel_id=1, source_target_pairs={{0,1},{1,0},{2,3},{3,2},{4,5},{5,4},{6,7},{7,6},{8,9},{9,8},{10,11... | collective-permute-start | bytes 1179656 | tf_op jit(solution)/shard_map/ppermute | solution.py:26
  50.4 6.5 %collective-permute-start.4 = (bf16[2,2,80,256]{3,2,1,0:T(8,128)(2,1)S(1)}, bf16[2,2,80,256]{3,2,1,0:T(8,128)(2,1)S(1)}, u32[]{:S(2)}, u32[]{:S(2)}) collective-permute-start(bf16[2,2,80,256]{3,2,1,0:T(8,128)(2,1)S(1)} %get-tuple-element.21), channel_id=1, source_target_pairs={{0,1},{1,2},{2,3},{3,4},{4,5},{5,6},{6,7},{7,8},{8,9},{9,10},{10,1... | collective-permute-start | bytes 491528 | tf_op jit(solution)/shard_map/ppermute | solution.py:26
  53.7 7.5 %collective-permute-start.5 = (bf16[2,2,80,256]{3,2,1,0:T(8,128)(2,1)S(1)}, bf16[2,2,80,256]{3,2,1,0:T(8,128)(2,1)S(1)}, u32[]{:S(2)}, u32[]{:S(2)}) collective-permute-start(bf16[2,2,80,256]{3,2,1,0:T(8,128)(2,1)S(1)} %get-tuple-element.22), channel_id=1, source_target_pairs={{1,0},{2,1},{3,2},{4,3},{5,4},{6,5},{7,6},{8,7},{9,8},{10,9},{11,1... | collective-permute-start | bytes 491528 | tf_op jit(solution)/shard_map/ppermute | solution.py:26
  55.7 13.2 %collective-permute-start.12 = (bf16[96,2048]{1,0:T(8,128)(2,1)}, bf16[96,2048]{1,0:T(8,128)(2,1)S(1)}, u32[]{:S(2)}, u32[]{:S(2)}) collective-permute-start(bf16[96,2048]{1,0:T(8,128)(2,1)} %collective-permute-done.9.rest_3_), channel_id=1, source_target_pairs={{0,16},{1,17},{2,18},{3,19},{4,20},{5,21},{6,22},{7,23},{8,24},{9,... | collective-permute-start | bytes 1179656 | tf_op jit(solution)/shard_map/ppermute | solution.py:26
  69.9 1.8 %collective-permute-start.14 = (bf16[96,2048]{1,0:T(8,128)(2,1)S(1)}, bf16[96,2048]{1,0:T(8,128)(2,1)S(1)}, u32[]{:S(2)}, u32[]{:S(2)}) collective-permute-start(bf16[96,2048]{1,0:T(8,128)(2,1)S(1)} %broadcast_select_fusion), channel_id=1, source_target_pairs={{0,1},{1,0},{2,3},{3,2},{4,5},{5,4},{6,7},{7,6},{8,9},{9,8},{10,11... | collective-permute-start | bytes 1179656 | tf_op jit(solution)/shard_map/ppermute | solution.py:26
  70.1 2.9 %collective-permute-start.13 = (bf16[96,2048]{1,0:T(8,128)(2,1)S(1)}, bf16[96,2048]{1,0:T(8,128)(2,1)S(1)}, u32[]{:S(2)}, u32[]{:S(2)}) collective-permute-start(bf16[96,2048]{1,0:T(8,128)(2,1)S(1)} %broadcast_select_fusion.1), channel_id=1, source_target_pairs={{0,1},{1,0},{2,3},{3,2},{4,5},{5,4},{6,7},{7,6},{8,9},{9,8},{10,11... | collective-permute-start | bytes 1179656 | tf_op jit(solution)/shard_map/ppermute | solution.py:26

commit v3 on v2

v3 whole, which is shorter than its diff:
```python
import functools
import math

import jax
import jax.numpy as jnp
from jax import lax
from jax.experimental import pallas as pl
from jax.experimental.pallas import tpu as pltpu
from jax.sharding import PartitionSpec as P

HALO = 80
CAP = 2
LANES = 128
MUCH = 60 << 20
LITTLE = 32 << 20
BLOCK = 1024


def routed(value, route):
    groups, owners = lax.axis_size("kgrp"), lax.axis_size("orb")
    pairs = []
    for group in range(groups):
        for owner in range(owners):
            to_group, to_owner = route(group, owner)
            if 0 <= to_owner < owners:
                pairs.append((group * owners + owner, to_group * owners + to_owner))
    return lax.ppermute(value, ("kgrp", "orb"), pairs)


def to_sibling(value):
    return routed(value, lambda group, owner: (group, owner ^ 1))


def to_pair_chip(value):
    return routed(value, lambda group, owner: (group, owner ^ 2))


def onward(value):
    return routed(value, lambda group, owner: (group, owner + (4 if owner & 2 == 0 else -4)))


def to_other_group(value):
    return routed(value, lambda group, owner: (1 - group, owner))


def to_next_chip(value):
    return routed(value, lambda group, owner: (group, owner + (1 if owner & 1 else -1)))


def after(value, *sooner):
    return lax.optimization_barrier((value,) + sooner)[0]


def pack_kernel(dest_ref, tiles_ref, packed_ref, placed, source):
    slots = packed_ref.shape[0]
    tile_count = dest_ref.shape[0]
    step_count = tiles_ref.shape[0] // tile_count
    first_vector = lax.axis_index("orb") * step_count
    part = packed_ref.shape[1]
    rows = pl.ds(pl.multiple_of(lax.axis_index("kgrp") * part, part), part)

    def clear(slot, carry):
        source[slot] = 0
        return carry

    def forget(owner, carry):
        placed[owner] = 0
        return carry

    def place(tile, carry):
        dest = dest_ref[lax.rem(tile, tile_count), 0, first_vector + tile // tile_count]
        rank = placed[dest]
        placed[dest] = rank + 1
        source[dest * CAP + rank] = tile
        return carry

    def fill(slot, carry):
        packed_ref[slot] = tiles_ref[source[slot], rows, :]
        return carry

    lax.fori_loop(0, slots, clear, 0, unroll=4)
    lax.fori_loop(0, slots // CAP, forget, 0, unroll=4)
    lax.fori_loop(0, step_count * tile_count, place, 0)
    lax.fori_loop(0, slots, fill, 0, unroll=2)


def pack_tiles(tiles, dest, owners):
    slots = owners * CAP
    rows, width = tiles.shape[1:]
    vmem = pl.BlockSpec(memory_space=pltpu.VMEM)
    return pl.pallas_call(
        pack_kernel,
        out_shape=jax.ShapeDtypeStruct((slots, rows // lax.axis_size("kgrp"), width), tiles.dtype),
        in_specs=[pl.BlockSpec(memory_space=pltpu.SMEM), vmem],
        out_specs=vmem,
        scratch_shapes=[pltpu.SMEM((owners,), jnp.int32), pltpu.SMEM((slots,), jnp.int32)],
        compiler_params=pltpu.CompilerParams(vmem_limit_bytes=MUCH),
        cost_estimate=pl.CostEstimate(flops=0, bytes_accessed=0, transcendentals=0),
        name="pack_tiles",
    )(dest, tiles)


def weight_kernel(slot_count, *refs):
    sources, (weight_ref, point_ref, cell_ref, dest_ref, column_ref, sems) = refs[:4], refs[4:]
    copies = [
        pltpu.make_async_copy(source, target, sems.at[index])
        for index, (source, target) in enumerate(zip(sources, (point_ref, cell_ref, dest_ref, column_ref)))
    ]
    for copy in copies:
        copy.start()
    for copy in copies:
        copy.wait()
    tile_count, _, vectors = dest_ref.shape
    owners = weight_ref.shape[1] // LANES
    step_count = vectors // owners
    k_count = point_ref.shape[0]
    mine = dest_ref[:, 0, :] == lax.axis_index("orb")
    flags = mine.astype(jnp.float32)
    shape = (tile_count, tile_count)
    before = lax.broadcasted_iota(jnp.int32, shape, 1) < lax.broadcasted_iota(jnp.int32, shape, 0)
    rank = jnp.dot(before.astype(jnp.float32), flags, preferred_element_type=jnp.float32)
    shape = (vectors, vectors)
    sooner, later = lax.broadcasted_iota(jnp.int32, shape, 0), lax.broadcasted_iota(jnp.int32, shape, 1)
    same_owner = (sooner < later) & (sooner >= later - later % step_count)
    counts = jnp.broadcast_to(jnp.sum(flags, axis=0, keepdims=True), (8, vectors))
    above = jnp.dot(counts, same_owner.astype(jnp.float32), preferred_element_type=jnp.float32)
    rank = (rank + above[0:1]).astype(jnp.int32)
    cells = cell_ref[...].astype(jnp.float32)
    column = column_ref[...]
    values = []
    for k in range(k_count):
        fraction = point_ref[k, 0] * cells[0:1] + point_ref[k, 1] * cells[1:2]
        fraction = fraction + point_ref[k, 2] * cells[2:3]
        radians = 6.283185307179586 * fraction
        for wave in (jnp.cos(radians), jnp.sin(radians)):
            phase = wave.astype(jnp.bfloat16).astype(jnp.float32)
            for j in range(slot_count):
                for c in range(CAP):
                    here = mine & (rank == c) & (column == j)
                    values.append(jnp.sum(jnp.where(here, phase, 0.0), axis=0, keepdims=True))
    values = jnp.concatenate(values, axis=0)
    chunk = math.gcd(owners, 16)
    shape = (vectors, chunk * LANES)
    for first in range(0, owners, chunk):
        owner = first + lax.broadcasted_iota(jnp.int32, shape, 1) // LANES
        member = (lax.broadcasted_iota(jnp.int32, shape, 0) // step_count == owner).astype(jnp.float32)
        weight_ref[:, first * LANES : (first + chunk) * LANES] = jnp.dot(
            values, member, preferred_element_type=jnp.float32
        )


def receive_weights(kpoints, cells, dest, column, owners, slot_count):
    k_count = kpoints.shape[0]
    operands = (kpoints, cells, dest, column)
    spaces = (pltpu.SMEM, pltpu.VMEM, pltpu.VMEM, pltpu.VMEM)
    return pl.pallas_call(
        functools.partial(weight_kernel, slot_count),
        out_shape=jax.ShapeDtypeStruct((k_count * 2 * slot_count * CAP, owners * LANES), jnp.float32),
        in_specs=[pl.BlockSpec(memory_space=pltpu.HBM)] * 4,
        out_specs=pl.BlockSpec(memory_space=pltpu.VMEM),
        scratch_shapes=[space(array.shape, array.dtype) for space, array in zip(spaces, operands)]
        + [pltpu.SemaphoreType.DMA((4,))],
        compiler_params=pltpu.CompilerParams(vmem_limit_bytes=LITTLE),
        cost_estimate=pl.CostEstimate(flops=0, bytes_accessed=0, transcendentals=0),
        name="receive_weights",
    )(*operands)


def add_tiles(weight_ref, tiles_ref, pair_ref, index, k_count, slot_count):
    slots, part, width = tiles_ref.shape
    rows = pair_ref.shape[1] // 2
    band = slot_count * width
    kinds = k_count * 2 * slot_count

    def add(owner, totals):
        lanes = pl.ds(pl.multiple_of(owner * LANES, LANES), LANES)
        for c in range(CAP):
            tile = tiles_ref[owner * CAP + c].astype(jnp.float32)
            totals = tuple(
                total + weight_ref[pl.ds(kind * CAP + c, 1), lanes] * tile for kind, total in enumerate(totals)
            )
        return totals

    totals = lax.fori_loop(
        0, slots // CAP, add, tuple(jnp.zeros((part, width), jnp.float32) for _ in range(kinds))
    )
    top = pl.ds(pl.multiple_of(index * part, part), part)
    bottom = pl.ds(pl.multiple_of(rows + index * part, part), part)
    for k in range(k_count):
        for p in range(2):
            for j in range(slot_count):
                value = totals[(k * 2 + p) * slot_count + j].astype(jnp.bfloat16)
                columns = slice(j * width, (j + 1) * width)
                later = slice(band + j * width, band + (j + 1) * width)
                if p == 0:
                    pair_ref[k, top, columns] = value
                    pair_ref[k, bottom, later] = value
                else:
                    pair_ref[k, bottom, columns] = value
                    pair_ref[k, top, later] = -value


def begin_kernel(k_count, slot_count, weight_ref, tiles_ref, pair_ref):
    add_tiles(weight_ref, tiles_ref, pair_ref, lax.axis_index("kgrp"), k_count, slot_count)


def band_kernel(k_count, slot_count, weight_ref, tiles_ref, begun_ref, pair_ref, core_ref, chip_ref):
    rows = pair_ref.shape[1] // 2
    band = core_ref.shape[-1]
    pair_ref[...] = begun_ref[...]
    add_tiles(weight_ref, tiles_ref, pair_ref, 1 - lax.axis_index("kgrp"), k_count, slot_count)
    odd_core = lax.axis_index("orb") & 1
    for odd in (0, 1):

        @pl.when(odd_core == odd)
        def _():
            tail_ref, head_ref = (chip_ref, core_ref) if odd else (core_ref, chip_ref)
            for k in range(k_count):
                for p in range(2):
                    tail_ref[k, p] = pair_ref[k, (p + 1) * rows - HALO : (p + 1) * rows, 0:band]
                    head_ref[k, p] = pair_ref[k, p * rows : p * rows + HALO, 0:band]


def begin_bands(weights, tiles, k_count, slot_count):
    part, width = tiles.shape[1:]
    vmem = pl.BlockSpec(memory_space=pltpu.VMEM)
    return pl.pallas_call(
        functools.partial(begin_kernel, k_count, slot_count),
        out_shape=jax.ShapeDtypeStruct((k_count, 4 * part, 2 * slot_count * width), jnp.bfloat16),
        in_specs=[vmem, vmem],
        out_specs=vmem,
        compiler_params=pltpu.CompilerParams(vmem_limit_bytes=LITTLE),
        cost_estimate=pl.CostEstimate(flops=0, bytes_accessed=0, transcendentals=0),
        name="begin_bands",
    )(weights, tiles)


def make_bands(weights, tiles, begun, k_count, slot_count):
    band = slot_count * tiles.shape[2]
    edge = (k_count, 2, HALO, band)
    vmem = pl.BlockSpec(memory_space=pltpu.VMEM)
    return pl.pallas_call(
        functools.partial(band_kernel, k_count, slot_count),
        out_shape=[jax.ShapeDtypeStruct(shape, jnp.bfloat16) for shape in (begun.shape, edge, edge)],
        in_specs=[vmem, vmem, vmem],
        out_specs=[vmem, vmem, vmem],
        compiler_params=pltpu.CompilerParams(vmem_limit_bytes=LITTLE),
        cost_estimate=pl.CostEstimate(flops=0, bytes_accessed=0, transcendentals=0),
        name="make_bands",
    )(weights, tiles, begun)


def filter_kernel(places, pair_ref, core_ref, chip_ref, own_ref, sibling_ref, *rest):
    pieces = len(places)
    chip_refs, onward_refs, near_chip_refs, near_onward_refs = (
        rest[part * pieces : (part + 1) * pieces] for part in range(4)
    )
    result_ref, window, done, edges, sems, done_sems = rest[-6:]
    chunks, _, block = window.shape
    k_count, double_rows, _ = pair_ref.shape
    rows = double_rows // 2
    band = core_ref.shape[-1]
    per_piece = chunks // pieces
    group = lax.axis_index("kgrp")
    state = lax.axis_index("orb") & 3
    starts = [0, HALO, HALO + rows, HALO + 2 * rows, HALO + 3 * rows]

    def columns_of(chunk):
        fixed, by_group = places[chunk // per_piece]
        first = fixed + by_group * group + chunk % per_piece * block
        return pl.ds(pl.multiple_of(first, block), block)

    for odd_chip in (0, 1):
        for odd_core in (0, 1):

            @pl.when(state == odd_chip * 2 + odd_core)
            def _():
                for chunk in range(chunks):
                    whole = columns_of(chunk)
                    index, place = chunk // per_piece, chunk % per_piece
                    piece = pl.ds(place * block, block)
                    sibling = sibling_ref.at[:, whole]
                    near = (near_onward_refs if odd_chip == odd_core else near_chip_refs)[index].at[:, piece]
                    before, beyond = chip_refs[index], onward_refs[index]
                    if odd_chip == 0:
                        before, beyond = beyond, before
                    sources = [
                        before.at[rows - HALO : rows, piece],
                        sibling if odd_core else near,
                        own_ref.at[:, whole],
                        near if odd_core else sibling,
                        beyond.at[0:HALO, piece],
                    ]
                    for part, source in enumerate(sources):
                        count = source.shape[0]
                        target = window.at[chunk, starts[part] : starts[part] + count, :]
                        pltpu.make_async_copy(source, target, sems.at[chunk, part]).start()
                edges[1 - odd_core] = core_ref[...]
                edges[odd_core] = chip_ref[...]

    def product(left, right):
        return jnp.dot(left, right, preferred_element_type=jnp.float32)

    own_band = jnp.concatenate([pair_ref[k][:, 0:band] for k in range(k_count)], axis=0)
    halo_rows = k_count * 2 * HALO

    def result_copy(chunk):
        return pltpu.make_async_copy(
            done.at[chunk], result_ref.at[:, :, :, columns_of(chunk)], done_sems.at[chunk]
        )

    for chunk in range(chunks):
        for part in range(5):
            count = HALO if part in (0, 4) else rows
            target = window.at[chunk, starts[part] : starts[part] + count, :]
            pltpu.make_async_copy(target, target, sems.at[chunk, part]).wait()
        lower = window[chunk, 0:band, :]
        middle = window[chunk, rows : rows + band, :]
        upper = window[chunk, 2 * rows : 2 * rows + band, :]
        own_first = product(own_band, middle).astype(jnp.bfloat16)
        left_first = product(edges[0].reshape(halo_rows, band), lower).astype(jnp.bfloat16)
        right_first = product(edges[1].reshape(halo_rows, band), upper).astype(jnp.bfloat16)
        center = window[chunk, HALO + rows : HALO + 2 * rows, :].astype(jnp.float32)
        for k in range(k_count):
            wide = jnp.concatenate(
                [
                    part
                    for kind in (2 * k, 2 * k + 1)
                    for part in (
                        left_first[kind * HALO : (kind + 1) * HALO],
                        own_first[kind * rows : (kind + 1) * rows],
                        right_first[kind * HALO : (kind + 1) * HALO],
                    )
                ],
                axis=0,
            )
            both = 2.0 * product(pair_ref[k], wide)
            done[chunk, k, 0] = (both[0:rows] - center).astype(jnp.bfloat16)
            done[chunk, k, 1] = both[rows:].astype(jnp.bfloat16)
        result_copy(chunk).start()
    for chunk in range(chunks):
        result_copy(chunk).wait()


def filter_columns(places, pair, core_band, chip_band, own, sibling, halos, so_far):
    k_count, double_rows, _ = pair.shape
    rows = double_rows // 2
    columns = own.shape[1]
    pieces = len(halos)
    width = halos[0][0].shape[1]
    block = min(BLOCK, width)
    chunks = pieces * width // block
    vmem = pl.BlockSpec(memory_space=pltpu.VMEM)
    hbm = pl.BlockSpec(memory_space=pltpu.HBM)
    operands = [pair, core_band, chip_band, own, sibling]
    operands += [halo[part] for part in range(4) for halo in halos]
    specs = [vmem] * 3 + [hbm] * (2 + 4 * pieces)
    aliases = {}
    if so_far is not None:
        aliases = {len(operands): 0}
        operands.append(so_far)
        specs.append(hbm)
    return pl.pallas_call(
        functools.partial(filter_kernel, places),
        out_shape=jax.ShapeDtypeStruct((k_count, 2, rows, columns), jnp.bfloat16),
        in_specs=specs,
        out_specs=hbm,
        scratch_shapes=[
            pltpu.VMEM((chunks, 3 * rows + 2 * HALO, block), jnp.bfloat16),
            pltpu.VMEM((chunks, k_count, 2, rows, block), jnp.bfloat16),
            pltpu.VMEM((2,) + core_band.shape, jnp.bfloat16),
            pltpu.SemaphoreType.DMA((chunks, 5)),
            pltpu.SemaphoreType.DMA((chunks,)),
        ],
        input_output_aliases=aliases,
        compiler_params=pltpu.CompilerParams(vmem_limit_bytes=MUCH),
        cost_estimate=pl.CostEstimate(
            flops=0,
            bytes_accessed=0,
            transcendentals=0,
        ),
        name="filter_columns",
    )(*operands)


def local(hopping_tiles, tile_strip, tile_column_slot, lattice, kpoints, start_block):
    owners = lax.axis_size("orb")
    group = lax.axis_index("kgrp")
    step_count, tile_count, row_count, col_width = hopping_tiles.shape
    slot_count = (row_count + 2 * HALO) // col_width
    k_count = kpoints.shape[0]
    piece = start_block.shape[1] // 4

    dest = jnp.transpose(tile_strip, (1, 2, 0))
    tiles = hopping_tiles.reshape(step_count * tile_count, row_count, col_width)
    outgoing = pack_tiles(tiles, dest, owners)
    weights = receive_weights(kpoints, lattice.T, dest, tile_column_slot.T, owners, slot_count)
    incoming = lax.all_to_all(outgoing, "orb", split_axis=0, concat_axis=0, tiled=True)

    shared = to_pair_chip(lax.dynamic_slice_in_dim(start_block, group * piece, piece, axis=1))
    shared = after(shared, outgoing)
    third = to_pair_chip(after(start_block, shared)[:, 2 * piece : 3 * piece])
    other = to_other_group(shared)
    near_shared = to_sibling(shared)
    sibling = to_sibling(start_block)
    shared_beyond = onward(shared)

    begun = begin_bands(weights, after(incoming, other, near_shared, sibling), k_count, slot_count)
    theirs = to_other_group(after(incoming, begun))
    third = after(third, begun)
    fourth = to_pair_chip(after(start_block, third)[:, 3 * piece : 4 * piece])
    third_beyond = onward(third)
    begun = after(begun, shared_beyond)
    pair, for_core, for_chip = make_bands(weights, theirs, begun, k_count, slot_count)
    core_band, chip_band = to_sibling(for_core), to_next_chip(for_chip)

    swapped = (core_band, chip_band)
    fourth = after(fourth, *swapped)
    shared_beyond, third_beyond = after(shared_beyond, *swapped), after(third_beyond, fourth)
    near_shared_beyond, near_third_beyond = to_sibling(shared_beyond), to_sibling(third_beyond)
    near_third, near_other = to_sibling(after(third, pair)), to_sibling(after(other, pair))
    other_beyond = to_other_group(shared_beyond)
    fourth_beyond = onward(fourth)
    near_fourth = to_sibling(fourth)

    def filtered(places, halos, so_far):
        return filter_columns(places, pair, core_band, chip_band, start_block, sibling, halos, so_far)

    result = filtered(
        [(0, piece), (2 * piece, 0)],
        [
            (shared, shared_beyond, near_shared, near_shared_beyond),
            (third, third_beyond, near_third, near_third_beyond),
        ],
        None,
    )
    other_beyond, fourth_beyond = after(other_beyond, result), after(fourth_beyond, result)
    return filtered(
        [(piece, -piece), (3 * piece, 0)],
        [
            (other, other_beyond, near_other, to_sibling(other_beyond)),
            (fourth, fourth_beyond, near_fourth, to_sibling(fourth_beyond)),
        ],
        result,
    )


def solution(mesh):
    return jax.shard_map(
        local,
        mesh=mesh,
        in_specs=(P("orb", None, None, None), P(), P(), P(), P("kgrp", None), P("orb", None)),
        out_specs=P("kgrp", None, "orb", None),
        check_vma=False,
    )
```

time: 81.1 us -> 74.3 us (0.916)
  the two profiles are of different devices: /device:TPU:11 before, /device:TPU:0 now
where the time goes in v3:
time: 74.3 us; the launch traced here: 74 us
  starting transfers between devices  37.4 us (50%)
  Pallas kernels  21 us (28%)
  waiting for transfers between devices  10.5 us (14%)
  local copies, waits for them, and re-layouts  4.78 us (6%)
    ppermute x20, starting transfers between devices, routed(): return lax.ppermute(value, ('kgrp', 'orb'), pairs)  32.4 us
    pallas_call x2, Pallas kernels, filter_columns(): pl.pallas_call(functools.partial(filter_kernel, places), out_shape=jax.Sh...  16 us
    ppermute x20, waiting for transfers between devices, routed(): return lax.ppermute(value, ('kgrp', 'orb'), pairs)  9.19 us
    all_to_all x1, starting transfers between devices, local(): lax.all_to_all(outgoing, 'orb', split_axis=0, concat_axis=0, tiled=True)  4.98 us
    unnamed x40, local copies, waits for them, and re-layouts  2.89 us
    pallas_call x1, Pallas kernels, pack_tiles(): pl.pallas_call(pack_kernel, out_shape=jax.ShapeDtypeStruct((slots, rows /...  2.66 us
  transfers between devices with their start and end apart: 21, of which 7 were waited for; matrix products, arithmetic and copies ran while one was open for 3% of the time, Pallas kernels for 18%

profile of v3, /device:TPU:0, one launch (start us, length us, event | category | flops | bytes accessed | tf_op | source)
XLA Modules:
  0.0 74.0 jit_solution(14141990650649769084)
XLA Ops:
  0.0 0.5 collective-permute-start.3
  0.5 1.1 %constant_dynamic-slice_fusion = bf16[96,2048]{1,0:T(8,128)(2,1)S(1)} fusion(bf16[96,8192]{1,0:T(8,128)(2,1)} %own_ref.3, s32[]{:T(128)S(6)} %select_n.3), kind=kLoop, calls=%fused_computation | loop fusion | bytes 786436 | tf_op jit(solution)/shard_map/dynamic_slice | solution.py:400
  1.6 2.6 %collective-permute-start = (bf16[96,2048]{1,0:T(8,128)(2,1)S(1)}, bf16[96,2048]{1,0:T(8,128)(2,1)S(1)}, u32[]{:S(2)}, u32[]{:S(2)}) collective-permute-start(bf16[96,2048]{1,0:T(8,128)(2,1)S(1)} %constant_dynamic-slice_fusion), channel_id=1, source_target_pairs={{0,2},{1,3},{2,0},{3,1},{4,6},{5,7},{6,4},{7,5},{8,10},{9,11},{10,... | collective-permute-start | bytes 1179656 | tf_op jit(solution)/shard_map/ppermute | solution.py:27
  4.2 2.7 %pack_tiles.1 = bf16[32,48,128]{2,1,0:T(8,128)(2,1)} custom-call(s32[12,1,32]{2,1,0:T(1,128)} %bitcast.4, bf16[24,96,128]{2,1,0:T(8,128)(2,1)} %bitcast.8), custom_call_target="tpu_custom_call" | custom-call | tf_op jit(solution)/shard_map/pack_tiles/pallas_call | solution.py:91
  6.8 5.0 %all-to-all-start = ((bf16[32,48,128]{2,1,0:T(8,128)(2,1)}), bf16[32,48,128]{2,1,0:T(8,128)(2,1)S(1)}, u32[]{:S(2)}, u32[]{:S(2)}) async-start(bf16[32,48,128]{2,1,0:T(8,128)(2,1)} %pack_tiles.1), calls=%async_computation | async-start | bytes 786432 | tf_op jit(solution)/shard_map/all_to_all | solution.py:398
  11.8 2.0 %collective-permute-done.rest_0_ = bf16[96,2048]{1,0:T(8,128)(2,1)S(1)} collective-permute-done((bf16[96,2048]{1,0:T(8,128)(2,1)S(1)}, bf16[96,2048]{1,0:T(8,128)(2,1)S(1)}, u32[]{:S(2)}, u32[]{:S(2)}) %collective-permute-start) | collective-permute-done | bytes 393248 | tf_op jit(solution)/shard_map/ppermute | solution.py:27
  13.9 0.0 collective-permute-start.2
  13.9 1.8 %collective-permute-start.1 = (bf16[96,2048]{1,0:T(8,128)(2,1)S(1)}, bf16[96,2048]{1,0:T(8,128)(2,1)}, u32[]{:S(2)}, u32[]{:S(2)}) collective-permute-start(bf16[96,2048]{1,0:T(8,128)(2,1)S(1)} %collective-permute-done.rest_0_), channel_id=1, source_target_pairs={{0,16},{1,17},{2,18},{3,19},{4,20},{5,21},{6,22},{7,23},{8,24},{9,... | collective-permute-start | bytes 1179656 | tf_op jit(solution)/shard_map/ppermute | solution.py:27
  15.7 0.0 copy-done.5
  15.7 0.8 %slice.6 = bf16[96,2048]{1,0:T(8,128)(2,1)} slice(bf16[96,8192]{1,0:T(8,128)(2,1)S(1)} %copy-done.5), slice={[0:96], [4096:6144]} | slice | bytes 786432 | tf_op jit(solution)/shard_map/slice | solution.py:402
  16.5 1.7 %collective-permute-start.8 = (bf16[96,2048]{1,0:T(8,128)(2,1)}, bf16[96,2048]{1,0:T(8,128)(2,1)}, u32[]{:S(2)}, u32[]{:S(2)}) collective-permute-start(bf16[96,2048]{1,0:T(8,128)(2,1)} %slice.6), channel_id=1, source_target_pairs={{0,2},{1,3},{2,0},{3,1},{4,6},{5,7},{6,4},{7,5},{8,10},{9,11},{10,... | collective-permute-start | bytes 1179656 | tf_op jit(solution)/shard_map/ppermute | solution.py:27
  18.2 0.0 copy-done.1
  18.2 0.0 copy-done.2
  18.2 0.0 copy-done.3
  18.2 0.9 %receive_weights.1.weight_ref = f32[16,2048]{1,0:T(8,128)S(1)} custom-call(f32[2,3]{1,0:T(2,128)S(1)} %copy-done.4, s32[3,32]{1,0:T(4,128)S(1)} %bitcast.7, s32[12,1,32]{2,1,0:T(1,128)S(1)} %bitcast.5, s32[12,32]{1,0:T(8,128)S(1)} %bitcast.6), custom_call_target="tpu_custom_call" | custom-call | tf_op jit(solution)/shard_map/receive_weights/pallas_call | solution.py:156
  19.1 3.6 %collective-permute-start.5 = (bf16[96,2048]{1,0:T(8,128)(2,1)S(1)}, bf16[96,2048]{1,0:T(8,128)(2,1)S(1)}, u32[]{:S(2)}, u32[]{:S(2)}) collective-permute-start(bf16[96,2048]{1,0:T(8,128)(2,1)S(1)} %collective-permute-done.rest_0_), channel_id=1, source_target_pairs={{0,4},{1,5},{4,8},{5,9},{6,2},{7,3},{8,12},{9,13},{10,6},{11,7},{1... | collective-permute-start | bytes 1179656 | tf_op jit(solution)/shard_map/ppermute | solution.py:27
  22.7 1.3 %all-to-all-done.tiles_ref = bf16[32,48,128]{2,1,0:T(8,128)(2,1)S(1)} async-done(((bf16[32,48,128]{2,1,0:T(8,128)(2,1)}), bf16[32,48,128]{2,1,0:T(8,128)(2,1)S(1)}, u32[]{:S(2)}, u32[]{:S(2)}) %all-to-all-start) | async-done | bytes 393248 | tf_op jit(solution)/shard_map/all_to_all | solution.py:398
  24.1 0.0 collective-permute-done.2.rest_4_
  24.1 1.5 %collective-permute-done.1.rest_0_ = bf16[96,2048]{1,0:T(8,128)(2,1)} collective-permute-done((bf16[96,2048]{1,0:T(8,128)(2,1)S(1)}, bf16[96,2048]{1,0:T(8,128)(2,1)}, u32[]{:S(2)}, u32[]{:S(2)}) %collective-permute-start.1) | collective-permute-done | bytes 393248 | tf_op jit(solution)/shard_map/ppermute | solution.py:27
  25.6 0.0 collective-permute-done.3.sibling_ref
  25.6 0.7 begin_bands.1.begun_ref
  26.3 1.8 %collective-permute-start.4 = (bf16[32,48,128]{2,1,0:T(8,128)(2,1)S(1)}, bf16[32,48,128]{2,1,0:T(8,128)(2,1)S(1)}, u32[]{:S(2)}, u32[]{:S(2)}) collective-permute-start(bf16[32,48,128]{2,1,0:T(8,128)(2,1)S(1)} %all-to-all-done.tiles_ref), channel_id=1, source_target_pairs={{0,16},{1,17},{2,18},{3,19},{4,20},{5,21},{6,22},{7,23},{8,24},{9,... | collective-permute-start | bytes 1179656 | tf_op jit(solution)/shard_map/ppermute | solution.py:27
  28.1 1.5 %collective-permute-done.8.rest_1_ = bf16[96,2048]{1,0:T(8,128)(2,1)} collective-permute-done((bf16[96,2048]{1,0:T(8,128)(2,1)}, bf16[96,2048]{1,0:T(8,128)(2,1)}, u32[]{:S(2)}, u32[]{:S(2)}) %collective-permute-start.8) | collective-permute-done | bytes 393248 | tf_op jit(solution)/shard_map/ppermute | solution.py:27
  29.6 1.3 %collective-permute-start.9 = (bf16[96,2048]{1,0:T(8,128)(2,1)S(1)}, bf16[96,2048]{1,0:T(8,128)(2,1)}, u32[]{:S(2)}, u32[]{:S(2)}) collective-permute-start(bf16[96,2048]{1,0:T(8,128)(2,1)S(1)} %slice.7), channel_id=1, source_target_pairs={{0,2},{1,3},{2,0},{3,1},{4,6},{5,7},{6,4},{7,5},{8,10},{9,11},{10,... | collective-permute-start | bytes 1179656 | tf_op jit(solution)/shard_map/ppermute | solution.py:27
  30.9 3.9 %collective-permute-start.11 = (bf16[96,2048]{1,0:T(8,128)(2,1)}, bf16[96,2048]{1,0:T(8,128)(2,1)S(1)}, u32[]{:S(2)}, u32[]{:S(2)}) collective-permute-start(bf16[96,2048]{1,0:T(8,128)(2,1)} %collective-permute-done.8.rest_1_), channel_id=1, source_target_pairs={{0,4},{1,5},{4,8},{5,9},{6,2},{7,3},{8,12},{9,13},{10,6},{11,7},{1... | collective-permute-start | bytes 1179656 | tf_op jit(solution)/shard_map/ppermute | solution.py:27
  34.8 0.0 collective-permute-done.5.rest_2_
  34.8 2.3 %collective-permute-done.4.tiles_ref = bf16[32,48,128]{2,1,0:T(8,128)(2,1)S(1)} collective-permute-done((bf16[32,48,128]{2,1,0:T(8,128)(2,1)S(1)}, bf16[32,48,128]{2,1,0:T(8,128)(2,1)S(1)}, u32[]{:S(2)}, u32[]{:S(2)}) %collective-permute-start.4) | collective-permute-done | bytes 393248 | tf_op jit(solution)/shard_map/ppermute | solution.py:27
  37.1 0.7 make_bands.1
  37.8 0.0 copy-done.8
  37.9 0.0 copy-start
  37.9 0.8 %copy-done = bf16[2,192,512]{2,1,0:T(8,128)(2,1)} copy-done((bf16[2,192,512]{2,1,0:T(8,128)(2,1)}, bf16[2,192,512]{2,1,0:T(8,128)(2,1)S(1)}, u32[]{:S(2)}) %copy-start) | copy-done | bytes 393240
  38.6 0.0 collective-permute-start.6
  38.6 0.7 collective-permute-start.7
  39.3 3.3 %collective-permute-start.12 = (bf16[96,2048]{1,0:T(8,128)(2,1)}, bf16[96,2048]{1,0:T(8,128)(2,1)S(1)}, u32[]{:S(2)}, u32[]{:S(2)}) collective-permute-start(bf16[96,2048]{1,0:T(8,128)(2,1)} %collective-permute-done.8.rest_1_), channel_id=1, source_target_pairs={{0,1},{1,0},{2,3},{3,2},{4,5},{5,4},{6,7},{7,6},{8,9},{9,8},{10,11... | collective-permute-start | bytes 1179656 | tf_op jit(solution)/shard_map/ppermute | solution.py:27
  42.6 0.0 collective-permute-done.6.core_ref
  42.6 0.0 collective-permute-done.7.chip_ref
  42.6 0.0 collective-permute-done.9.rest_1_
  42.7 3.1 %collective-permute-start.13 = (bf16[96,2048]{1,0:T(8,128)(2,1)S(1)}, bf16[96,2048]{1,0:T(8,128)(2,1)S(1)}, u32[]{:S(2)}, u32[]{:S(2)}) collective-permute-start(bf16[96,2048]{1,0:T(8,128)(2,1)S(1)} %collective-permute-done.5.rest_2_), channel_id=1, source_target_pairs={{0,1},{1,0},{2,3},{3,2},{4,5},{5,4},{6,7},{7,6},{8,9},{9,8},{10,11... | collective-permute-start | bytes 1179656 | tf_op jit(solution)/shard_map/ppermute | solution.py:27
  45.8 0.0 collective-permute-done.11.rest_3_
  45.8 0.1 collective-permute-start.14
  45.8 5.4 %collective-permute-start.15 = (bf16[96,2048]{1,0:T(8,128)(2,1)}, bf16[96,2048]{1,0:T(8,128)(2,1)S(1)}, u32[]{:S(2)}, u32[]{:S(2)}) collective-permute-start(bf16[96,2048]{1,0:T(8,128)(2,1)} %collective-permute-done.9.rest_1_), channel_id=1, source_target_pairs={{0,4},{1,5},{4,8},{5,9},{6,2},{7,3},{8,12},{9,13},{10,6},{11,7},{1... | collective-permute-start | bytes 1179656 | tf_op jit(solution)/shard_map/ppermute | solution.py:27
  51.3 1.6 %collective-permute-start.10 = (bf16[96,2048]{1,0:T(8,128)(2,1)S(1)}, bf16[96,2048]{1,0:T(8,128)(2,1)S(1)}, u32[]{:S(2)}, u32[]{:S(2)}) collective-permute-start(bf16[96,2048]{1,0:T(8,128)(2,1)S(1)} %collective-permute-done.5.rest_2_), channel_id=1, source_target_pairs={{0,16},{1,17},{2,18},{3,19},{4,20},{5,21},{6,22},{7,23},{8,24},{9,... | collective-permute-start | bytes 1179656 | tf_op jit(solution)/shard_map/ppermute | solution.py:27
  52.9 0.0 collective-permute-done.12.rest_5_
  52.9 0.0 collective-permute-start.16
  52.9 0.0 collective-permute-done.13.rest_6_
  52.9 0.5 collective-permute-start.17
  53.4 0.0 collective-permute-done.14.rest_7_
  53.4 0.2 copy-done.12
  53.6 0.1 copy-done.13
  53.8 0.8 %copy-done.14 = bf16[96,2048]{1,0:T(8,128)(2,1)} copy-done((bf16[96,2048]{1,0:T(8,128)(2,1)}, bf16[96,2048]{1,0:T(8,128)(2,1)S(1)}, u32[]{:S(2)}) %copy-start.14) | copy-done | bytes 393240
  54.5 8.0 %filter_columns.2.rest_8_ = bf16[2,2,96,8192]{3,2,1,0:T(8,128)(2,1)} custom-call(bf16[2,192,512]{2,1,0:T(8,128)(2,1)} %copy-done, bf16[2,2,80,256]{3,2,1,0:T(8,128)(2,1)} %copy-done.6, bf16[2,2,80,256]{3,2,1,0:T(8,128)(2,1)} %copy-done.7, bf16[96,8192]{1,0:T(8,128)(2,1)} %own_ref.3, bf16[96,8192]{1,0:T(8,128)(2,1)} %collective-permute-done.3.sibling_ref, ...), custom_call_target="tpu_custom_call" | custom-call | tf_op jit(solution)/shard_map/filter_columns/pallas_call | solution.py:363
  62.6 0.0 collective-permute-done.15.rest_3_
  62.6 0.0 collective-permute-done.10.rest_2_
  62.6 0.4 collective-permute-start.18
  63.1 0.1 collective-permute-start.19
  63.2 0.0 collective-permute-done.16.rest_4_
  63.2 0.0 collective-permute-done.17.rest_5_
  63.2 1.2 %collective-permute-done.18.rest_6_ = bf16[96,2048]{1,0:T(8,128)(2,1)S(1)} collective-permute-done((bf16[96,2048]{1,0:T(8,128)(2,1)S(1)}, bf16[96,2048]{1,0:T(8,128)(2,1)S(1)}, u32[]{:S(2)}, u32[]{:S(2)}) %collective-permute-start.18) | collective-permute-done | bytes 393248 | tf_op jit(solution)/shard_map/ppermute | solution.py:27
  64.4 0.6 collective-permute-done.19.rest_7_
  65.0 0.0 copy-done.15
  65.0 0.0 copy-done.17
  65.0 0.2 copy-done.18
  65.2 0.8 %copy-done.19 = bf16[96,2048]{1,0:T(8,128)(2,1)} copy-done((bf16[96,2048]{1,0:T(8,128)(2,1)}, bf16[96,2048]{1,0:T(8,128)(2,1)S(1)}, u32[]{:S(2)}) %copy-start.19) | copy-done | bytes 393240
  65.9 8.0 %filter_columns.3 = bf16[2,2,96,8192]{3,2,1,0:T(8,128)(2,1)} custom-call(bf16[2,192,512]{2,1,0:T(8,128)(2,1)} %copy-done, bf16[2,2,80,256]{3,2,1,0:T(8,128)(2,1)} %copy-done.6, bf16[2,2,80,256]{3,2,1,0:T(8,128)(2,1)} %copy-done.7, bf16[96,8192]{1,0:T(8,128)(2,1)} %own_ref.3, ...), custom_call_target="tpu_custom_call", output_to_operand_aliasing={{}: (13, {})} | custom-call | tf_op jit(solution)/shard_map/filter_columns/pallas_call | solution.py:363
  (27 shorter events, 0.1 us)
Async XLA Ops:
  0.0 15.7 %copy-start.5 = (bf16[96,8192]{1,0:T(8,128)(2,1)S(1)}, bf16[96,8192]{1,0:T(8,128)(2,1)}, u32[]{:S(2)}) copy-start(bf16[96,8192]{1,0:T(8,128)(2,1)} %own_ref.3) | copy-start | bytes 4718596
  0.0 25.6 %collective-permute-start.3 = (bf16[96,8192]{1,0:T(8,128)(2,1)}, bf16[96,8192]{1,0:T(8,128)(2,1)}, u32[]{:S(2)}, u32[]{:S(2)}) collective-permute-start(bf16[96,8192]{1,0:T(8,128)(2,1)} %own_ref.3), channel_id=1, source_target_pairs={{0,1},{1,0},{2,3},{3,2},{4,5},{5,4},{6,7},{7,6},{8,9},{9,8},{10,11... | collective-permute-start | bytes 4718600 | tf_op jit(solution)/shard_map/ppermute | solution.py:27
  0.5 17.7 %copy-start.1 = (s32[32,12,1]{0,2,1:T(1,128)S(1)}, s32[32,12,1]{0,2,1:T(1,128)}, u32[]{:S(2)}) copy-start(s32[32,12,1]{0,2,1:T(1,128)} %param.7) | copy-start | bytes 4612
  0.5 17.7 %copy-start.2 = (s32[32,12]{0,1:T(8,128)S(1)}, s32[32,12]{0,1:T(8,128)}, u32[]{:S(2)}) copy-start(s32[32,12]{0,1:T(8,128)} %param.8) | copy-start | bytes 4612
  0.5 17.7 %copy-start.3 = (s32[32,3]{0,1:T(4,128)S(1)}, s32[32,3]{0,1:T(4,128)}, u32[]{:S(2)}) copy-start(s32[32,3]{0,1:T(4,128)} %param.9) | copy-start | bytes 1156
  0.5 17.7 %copy-start.4 = (f32[2,3]{1,0:T(2,128)S(1)}, f32[2,3]{1,0:T(2,128)}, u32[]{:S(2)}) copy-start(f32[2,3]{1,0:T(2,128)} %refs_0_.1) | copy-start | bytes 76
  1.6 12.3 %collective-permute-start = (bf16[96,2048]{1,0:T(8,128)(2,1)S(1)}, bf16[96,2048]{1,0:T(8,128)(2,1)S(1)}, u32[]{:S(2)}, u32[]{:S(2)}) collective-permute-start(bf16[96,2048]{1,0:T(8,128)(2,1)S(1)} %constant_dynamic-slice_fusion), channel_id=1, source_target_pairs={{0,2},{1,3},{2,0},{3,1},{4,6},{5,7},{6,4},{7,5},{8,10},{9,11},{10,... | collective-permute-start | bytes 1179656 | tf_op jit(solution)/shard_map/ppermute | solution.py:27
  6.8 17.2 %all-to-all-start = ((bf16[32,48,128]{2,1,0:T(8,128)(2,1)}), bf16[32,48,128]{2,1,0:T(8,128)(2,1)S(1)}, u32[]{:S(2)}, u32[]{:S(2)}) async-start(bf16[32,48,128]{2,1,0:T(8,128)(2,1)} %pack_tiles.1), calls=%async_computation | async-start | bytes 786432 | tf_op jit(solution)/shard_map/all_to_all | solution.py:398
  13.9 24.0 %copy-start.8 = (bf16[96,2048]{1,0:T(8,128)(2,1)}, bf16[96,2048]{1,0:T(8,128)(2,1)S(1)}, u32[]{:S(2)}) copy-start(bf16[96,2048]{1,0:T(8,128)(2,1)S(1)} %collective-permute-done.rest_0_) | copy-start | bytes 1179652
  13.9 10.2 %collective-permute-start.2 = (bf16[96,2048]{1,0:T(8,128)(2,1)S(1)}, bf16[96,2048]{1,0:T(8,128)(2,1)S(1)}, u32[]{:S(2)}, u32[]{:S(2)}) collective-permute-start(bf16[96,2048]{1,0:T(8,128)(2,1)S(1)} %collective-permute-done.rest_0_), channel_id=1, source_target_pairs={{0,1},{1,0},{2,3},{3,2},{4,5},{5,4},{6,7},{7,6},{8,9},{9,8},{10,11... | collective-permute-start | bytes 1179656 | tf_op jit(solution)/shard_map/ppermute | solution.py:27
  13.9 11.7 %collective-permute-start.1 = (bf16[96,2048]{1,0:T(8,128)(2,1)S(1)}, bf16[96,2048]{1,0:T(8,128)(2,1)}, u32[]{:S(2)}, u32[]{:S(2)}) collective-permute-start(bf16[96,2048]{1,0:T(8,128)(2,1)S(1)} %collective-permute-done.rest_0_), channel_id=1, source_target_pairs={{0,16},{1,17},{2,18},{3,19},{4,20},{5,21},{6,22},{7,23},{8,24},{9,... | collective-permute-start | bytes 1179656 | tf_op jit(solution)/shard_map/ppermute | solution.py:27
  16.5 13.1 %collective-permute-start.8 = (bf16[96,2048]{1,0:T(8,128)(2,1)}, bf16[96,2048]{1,0:T(8,128)(2,1)}, u32[]{:S(2)}, u32[]{:S(2)}) collective-permute-start(bf16[96,2048]{1,0:T(8,128)(2,1)} %slice.6), channel_id=1, source_target_pairs={{0,2},{1,3},{2,0},{3,1},{4,6},{5,7},{6,4},{7,5},{8,10},{9,11},{10,... | collective-permute-start | bytes 1179656 | tf_op jit(solution)/shard_map/ppermute | solution.py:27
  19.1 15.7 %collective-permute-start.5 = (bf16[96,2048]{1,0:T(8,128)(2,1)S(1)}, bf16[96,2048]{1,0:T(8,128)(2,1)S(1)}, u32[]{:S(2)}, u32[]{:S(2)}) collective-permute-start(bf16[96,2048]{1,0:T(8,128)(2,1)S(1)} %collective-permute-done.rest_0_), channel_id=1, source_target_pairs={{0,4},{1,5},{4,8},{5,9},{6,2},{7,3},{8,12},{9,13},{10,6},{11,7},{1... | collective-permute-start | bytes 1179656 | tf_op jit(solution)/shard_map/ppermute | solution.py:27
  24.1 29.3 %copy-start.9 = (bf16[96,2048]{1,0:T(8,128)(2,1)}, bf16[96,2048]{1,0:T(8,128)(2,1)S(1)}, u32[]{:S(2)}) copy-start(bf16[96,2048]{1,0:T(8,128)(2,1)S(1)} %collective-permute-done.2.rest_4_) | copy-start | bytes 1179652
  26.3 10.9 %collective-permute-start.4 = (bf16[32,48,128]{2,1,0:T(8,128)(2,1)S(1)}, bf16[32,48,128]{2,1,0:T(8,128)(2,1)S(1)}, u32[]{:S(2)}, u32[]{:S(2)}) collective-permute-start(bf16[32,48,128]{2,1,0:T(8,128)(2,1)S(1)} %all-to-all-done.tiles_ref), channel_id=1, source_target_pairs={{0,16},{1,17},{2,18},{3,19},{4,20},{5,21},{6,22},{7,23},{8,24},{9,... | collective-permute-start | bytes 1179656 | tf_op jit(solution)/shard_map/ppermute | solution.py:27
  29.6 13.0 %collective-permute-start.9 = (bf16[96,2048]{1,0:T(8,128)(2,1)S(1)}, bf16[96,2048]{1,0:T(8,128)(2,1)}, u32[]{:S(2)}, u32[]{:S(2)}) collective-permute-start(bf16[96,2048]{1,0:T(8,128)(2,1)S(1)} %slice.7), channel_id=1, source_target_pairs={{0,2},{1,3},{2,0},{3,1},{4,6},{5,7},{6,4},{7,5},{8,10},{9,11},{10,... | collective-permute-start | bytes 1179656 | tf_op jit(solution)/shard_map/ppermute | solution.py:27
  30.9 14.9 %collective-permute-start.11 = (bf16[96,2048]{1,0:T(8,128)(2,1)}, bf16[96,2048]{1,0:T(8,128)(2,1)S(1)}, u32[]{:S(2)}, u32[]{:S(2)}) collective-permute-start(bf16[96,2048]{1,0:T(8,128)(2,1)} %collective-permute-done.8.rest_1_), channel_id=1, source_target_pairs={{0,4},{1,5},{4,8},{5,9},{6,2},{7,3},{8,12},{9,13},{10,6},{11,7},{1... | collective-permute-start | bytes 1179656 | tf_op jit(solution)/shard_map/ppermute | solution.py:27
  34.8 18.6 %copy-start.10 = (bf16[96,2048]{1,0:T(8,128)(2,1)}, bf16[96,2048]{1,0:T(8,128)(2,1)S(1)}, u32[]{:S(2)}) copy-start(bf16[96,2048]{1,0:T(8,128)(2,1)S(1)} %collective-permute-done.5.rest_2_) | copy-start | bytes 1179652
  37.9 0.8 %copy-start = (bf16[2,192,512]{2,1,0:T(8,128)(2,1)}, bf16[2,192,512]{2,1,0:T(8,128)(2,1)S(1)}, u32[]{:S(2)}) copy-start(bf16[2,192,512]{2,1,0:T(8,128)(2,1)S(1)} %get-tuple-element.26.pair_ref) | copy-start | bytes 1179652
  38.6 4.0 %collective-permute-start.6 = (bf16[2,2,80,256]{3,2,1,0:T(8,128)(2,1)S(1)}, bf16[2,2,80,256]{3,2,1,0:T(8,128)(2,1)S(1)}, u32[]{:S(2)}, u32[]{:S(2)}) collective-permute-start(bf16[2,2,80,256]{3,2,1,0:T(8,128)(2,1)S(1)} %get-tuple-element.27), channel_id=1, source_target_pairs={{0,1},{1,0},{2,3},{3,2},{4,5},{5,4},{6,7},{7,6},{8,9},{9,8},{10,11... | collective-permute-start | bytes 491528 | tf_op jit(solution)/shard_map/ppermute | solution.py:27
  38.6 4.0 %collective-permute-start.7 = (bf16[2,2,80,256]{3,2,1,0:T(8,128)(2,1)S(1)}, bf16[2,2,80,256]{3,2,1,0:T(8,128)(2,1)S(1)}, u32[]{:S(2)}, u32[]{:S(2)}) collective-permute-start(bf16[2,2,80,256]{3,2,1,0:T(8,128)(2,1)S(1)} %get-tuple-element.28), channel_id=1, source_target_pairs={{1,2},{2,1},{3,4},{4,3},{5,6},{6,5},{7,8},{8,7},{9,10},{10,9},{11,... | collective-permute-start | bytes 491528 | tf_op jit(solution)/shard_map/ppermute | solution.py:27
  39.3 13.6 %collective-permute-start.12 = (bf16[96,2048]{1,0:T(8,128)(2,1)}, bf16[96,2048]{1,0:T(8,128)(2,1)S(1)}, u32[]{:S(2)}, u32[]{:S(2)}) collective-permute-start(bf16[96,2048]{1,0:T(8,128)(2,1)} %collective-permute-done.8.rest_1_), channel_id=1, source_target_pairs={{0,1},{1,0},{2,3},{3,2},{4,5},{5,4},{6,7},{7,6},{8,9},{9,8},{10,11... | collective-permute-start | bytes 1179656 | tf_op jit(solution)/shard_map/ppermute | solution.py:27
  42.6 10.8 %copy-start.6 = (bf16[2,2,80,256]{3,2,1,0:T(8,128)(2,1)}, bf16[2,2,80,256]{3,2,1,0:T(8,128)(2,1)S(1)}, u32[]{:S(2)}) copy-start(bf16[2,2,80,256]{3,2,1,0:T(8,128)(2,1)S(1)} %collective-permute-done.6.core_ref) | copy-start | bytes 491524
  42.6 10.8 %copy-start.7 = (bf16[2,2,80,256]{3,2,1,0:T(8,128)(2,1)}, bf16[2,2,80,256]{3,2,1,0:T(8,128)(2,1)S(1)}, u32[]{:S(2)}) copy-start(bf16[2,2,80,256]{3,2,1,0:T(8,128)(2,1)S(1)} %collective-permute-done.7.chip_ref) | copy-start | bytes 491524
  42.7 10.2 %collective-permute-start.13 = (bf16[96,2048]{1,0:T(8,128)(2,1)S(1)}, bf16[96,2048]{1,0:T(8,128)(2,1)S(1)}, u32[]{:S(2)}, u32[]{:S(2)}) collective-permute-start(bf16[96,2048]{1,0:T(8,128)(2,1)S(1)} %collective-permute-done.5.rest_2_), channel_id=1, source_target_pairs={{0,1},{1,0},{2,3},{3,2},{4,5},{5,4},{6,7},{7,6},{8,9},{9,8},{10,11... | collective-permute-start | bytes 1179656 | tf_op jit(solution)/shard_map/ppermute | solution.py:27
  45.8 7.7 %copy-start.11 = (bf16[96,2048]{1,0:T(8,128)(2,1)}, bf16[96,2048]{1,0:T(8,128)(2,1)S(1)}, u32[]{:S(2)}) copy-start(bf16[96,2048]{1,0:T(8,128)(2,1)S(1)} %collective-permute-done.11.rest_3_) | copy-start | bytes 1179652
  45.8 7.6 %collective-permute-start.14 = (bf16[96,2048]{1,0:T(8,128)(2,1)S(1)}, bf16[96,2048]{1,0:T(8,128)(2,1)S(1)}, u32[]{:S(2)}, u32[]{:S(2)}) collective-permute-start(bf16[96,2048]{1,0:T(8,128)(2,1)S(1)} %collective-permute-done.11.rest_3_), channel_id=1, source_target_pairs={{0,1},{1,0},{2,3},{3,2},{4,5},{5,4},{6,7},{7,6},{8,9},{9,8},{10,11... | collective-permute-start | bytes 1179656 | tf_op jit(solution)/shard_map/ppermute | solution.py:27
  45.8 16.7 %collective-permute-start.15 = (bf16[96,2048]{1,0:T(8,128)(2,1)}, bf16[96,2048]{1,0:T(8,128)(2,1)S(1)}, u32[]{:S(2)}, u32[]{:S(2)}) collective-permute-start(bf16[96,2048]{1,0:T(8,128)(2,1)} %collective-permute-done.9.rest_1_), channel_id=1, source_target_pairs={{0,4},{1,5},{4,8},{5,9},{6,2},{7,3},{8,12},{9,13},{10,6},{11,7},{1... | collective-permute-start | bytes 1179656 | tf_op jit(solution)/shard_map/ppermute | solution.py:27
  51.3 11.3 %collective-permute-start.10 = (bf16[96,2048]{1,0:T(8,128)(2,1)S(1)}, bf16[96,2048]{1,0:T(8,128)(2,1)S(1)}, u32[]{:S(2)}, u32[]{:S(2)}) collective-permute-start(bf16[96,2048]{1,0:T(8,128)(2,1)S(1)} %collective-permute-done.5.rest_2_), channel_id=1, source_target_pairs={{0,16},{1,17},{2,18},{3,19},{4,20},{5,21},{6,22},{7,23},{8,24},{9,... | collective-permute-start | bytes 1179656 | tf_op jit(solution)/shard_map/ppermute | solution.py:27
  52.9 0.8 %copy-start.12 = (bf16[96,2048]{1,0:T(8,128)(2,1)}, bf16[96,2048]{1,0:T(8,128)(2,1)S(1)}, u32[]{:S(2)}) copy-start(bf16[96,2048]{1,0:T(8,128)(2,1)S(1)} %collective-permute-done.12.rest_5_) | copy-start | bytes 1179652
  52.9 10.3 %collective-permute-start.16 = (bf16[96,2048]{1,0:T(8,128)(2,1)}, bf16[96,2048]{1,0:T(8,128)(2,1)S(1)}, u32[]{:S(2)}, u32[]{:S(2)}) collective-permute-start(bf16[96,2048]{1,0:T(8,128)(2,1)} %collective-permute-done.1.rest_0_), channel_id=1, source_target_pairs={{0,1},{1,0},{2,3},{3,2},{4,5},{5,4},{6,7},{7,6},{8,9},{9,8},{10,11... | collective-permute-start | bytes 1179656 | tf_op jit(solution)/shard_map/ppermute | solution.py:27
  52.9 0.9 %copy-start.13 = (bf16[96,2048]{1,0:T(8,128)(2,1)}, bf16[96,2048]{1,0:T(8,128)(2,1)S(1)}, u32[]{:S(2)}) copy-start(bf16[96,2048]{1,0:T(8,128)(2,1)S(1)} %collective-permute-done.13.rest_6_) | copy-start | bytes 1179652
  52.9 10.3 %collective-permute-start.17 = (bf16[96,2048]{1,0:T(8,128)(2,1)}, bf16[96,2048]{1,0:T(8,128)(2,1)}, u32[]{:S(2)}, u32[]{:S(2)}) collective-permute-start(bf16[96,2048]{1,0:T(8,128)(2,1)} %collective-permute-done.9.rest_1_), channel_id=1, source_target_pairs={{0,1},{1,0},{2,3},{3,2},{4,5},{5,4},{6,7},{7,6},{8,9},{9,8},{10,11... | collective-permute-start | bytes 1179656 | tf_op jit(solution)/shard_map/ppermute | solution.py:27
  53.8 0.8 %copy-start.14 = (bf16[96,2048]{1,0:T(8,128)(2,1)}, bf16[96,2048]{1,0:T(8,128)(2,1)S(1)}, u32[]{:S(2)}) copy-start(bf16[96,2048]{1,0:T(8,128)(2,1)S(1)} %collective-permute-done.14.rest_7_) | copy-start | bytes 1179652
  62.6 2.4 %copy-start.15 = (bf16[96,2048]{1,0:T(8,128)(2,1)}, bf16[96,2048]{1,0:T(8,128)(2,1)S(1)}, u32[]{:S(2)}) copy-start(bf16[96,2048]{1,0:T(8,128)(2,1)S(1)} %collective-permute-done.15.rest_3_) | copy-start | bytes 1179652
  62.6 2.4 %copy-start.16 = (bf16[96,2048]{1,0:T(8,128)(2,1)}, bf16[96,2048]{1,0:T(8,128)(2,1)S(1)}, u32[]{:S(2)}) copy-start(bf16[96,2048]{1,0:T(8,128)(2,1)S(1)} %collective-permute-done.10.rest_2_) | copy-start | bytes 1179652
  62.6 1.8 %collective-permute-start.18 = (bf16[96,2048]{1,0:T(8,128)(2,1)S(1)}, bf16[96,2048]{1,0:T(8,128)(2,1)S(1)}, u32[]{:S(2)}, u32[]{:S(2)}) collective-permute-start(bf16[96,2048]{1,0:T(8,128)(2,1)S(1)} %collective-permute-done.10.rest_2_), channel_id=1, source_target_pairs={{0,1},{1,0},{2,3},{3,2},{4,5},{5,4},{6,7},{7,6},{8,9},{9,8},{10,11... | collective-permute-start | bytes 1179656 | tf_op jit(solution)/shard_map/ppermute | solution.py:27
  63.1 1.9 %collective-permute-start.19 = (bf16[96,2048]{1,0:T(8,128)(2,1)S(1)}, bf16[96,2048]{1,0:T(8,128)(2,1)S(1)}, u32[]{:S(2)}, u32[]{:S(2)}) collective-permute-start(bf16[96,2048]{1,0:T(8,128)(2,1)S(1)} %collective-permute-done.15.rest_3_), channel_id=1, source_target_pairs={{0,1},{1,0},{2,3},{3,2},{4,5},{5,4},{6,7},{7,6},{8,9},{9,8},{10,11... | collective-permute-start | bytes 1179656 | tf_op jit(solution)/shard_map/ppermute | solution.py:27
  63.2 1.8 %copy-start.17 = (bf16[96,2048]{1,0:T(8,128)(2,1)}, bf16[96,2048]{1,0:T(8,128)(2,1)S(1)}, u32[]{:S(2)}) copy-start(bf16[96,2048]{1,0:T(8,128)(2,1)S(1)} %collective-permute-done.16.rest_4_) | copy-start | bytes 1179652
  64.4 0.8 %copy-start.18 = (bf16[96,2048]{1,0:T(8,128)(2,1)}, bf16[96,2048]{1,0:T(8,128)(2,1)S(1)}, u32[]{:S(2)}) copy-start(bf16[96,2048]{1,0:T(8,128)(2,1)S(1)} %collective-permute-done.18.rest_6_) | copy-start | bytes 1179652
  65.2 0.8 %copy-start.19 = (bf16[96,2048]{1,0:T(8,128)(2,1)}, bf16[96,2048]{1,0:T(8,128)(2,1)S(1)}, u32[]{:S(2)}) copy-start(bf16[96,2048]{1,0:T(8,128)(2,1)S(1)} %collective-permute-done.19.rest_7_) | copy-start | bytes 1179652

commit v4 on v3

--- a/solution.py
+++ b/solution.py
@@ -250,12 +250,12 @@
     )(weights, tiles, begun)
 
 
-def filter_kernel(places, pair_ref, core_ref, chip_ref, own_ref, sibling_ref, *rest):
+def filter_kernel(places, pair_source, core_ref, chip_ref, own_ref, sibling_ref, *rest):
     pieces = len(places)
     chip_refs, onward_refs, near_chip_refs, near_onward_refs = (
         rest[part * pieces : (part + 1) * pieces] for part in range(4)
     )
-    result_ref, window, done, edges, sems, done_sems = rest[-6:]
+    result_ref, pair_ref, window, done, edges, band_sems, sems, done_sems = rest[-8:]
     chunks, _, block = window.shape
     k_count, double_rows, _ = pair_ref.shape
     rows = double_rows // 2
@@ -266,10 +266,17 @@
     starts = [0, HALO, HALO + rows, HALO + 2 * rows, HALO + 3 * rows]
 
     def columns_of(chunk):
-        fixed, by_group = places[chunk // per_piece]
+        fixed, by_group, _ = places[chunk // per_piece]
         first = fixed + by_group * group + chunk % per_piece * block
         return pl.ds(pl.multiple_of(first, block), block)
 
+    bands = [
+        pltpu.make_async_copy(pair_source, pair_ref, band_sems.at[0]),
+        pltpu.make_async_copy(core_ref, edges.at[1 - (state & 1)], band_sems.at[1]),
+        pltpu.make_async_copy(chip_ref, edges.at[state & 1], band_sems.at[2]),
+    ]
+    for copy in bands:
+        copy.start()
     for odd_chip in (0, 1):
         for odd_core in (0, 1):
 
@@ -280,23 +287,28 @@
                     index, place = chunk // per_piece, chunk % per_piece
                     piece = pl.ds(place * block, block)
                     sibling = sibling_ref.at[:, whole]
-                    near = (near_onward_refs if odd_chip == odd_core else near_chip_refs)[index].at[:, piece]
-                    before, beyond = chip_refs[index], onward_refs[index]
+                    low = places[index][2]
+                    near = near_chip_refs[index].at[0:rows, piece]
+                    if odd_chip == odd_core:
+                        near = near_onward_refs[index].at[low : low + rows, piece]
+                    before, beyond = (chip_refs[index], 0), (onward_refs[index], low)
                     if odd_chip == 0:
                         before, beyond = beyond, before
+                    (before, last), (beyond, first) = before, beyond
                     sources = [
-                        before.at[rows - HALO : rows, piece],
+                        before.at[last + rows - HALO : last + rows, piece],
                         sibling if odd_core else near,
                         own_ref.at[:, whole],
                         near if odd_core else sibling,
-                        beyond.at[0:HALO, piece],
+                        beyond.at[first : first + HALO, piece],
                     ]
                     for part, source in enumerate(sources):
                         count = source.shape[0]
                         target = window.at[chunk, starts[part] : starts[part] + count, :]
                         pltpu.make_async_copy(source, target, sems.at[chunk, part]).start()
-                edges[1 - odd_core] = core_ref[...]
-                edges[odd_core] = chip_ref[...]
+
+    for copy in bands:
+        copy.wait()
 
     def product(left, right):
         return jnp.dot(left, right, preferred_element_type=jnp.float32)
@@ -350,11 +362,11 @@
     width = halos[0][0].shape[1]
     block = min(BLOCK, width)
     chunks = pieces * width // block
-    vmem = pl.BlockSpec(memory_space=pltpu.VMEM)
+    anywhere = pl.BlockSpec(memory_space=pl.ANY)
     hbm = pl.BlockSpec(memory_space=pltpu.HBM)
     operands = [pair, core_band, chip_band, own, sibling]
     operands += [halo[part] for part in range(4) for halo in halos]
-    specs = [vmem] * 3 + [hbm] * (2 + 4 * pieces)
+    specs = [anywhere] * (5 + 4 * pieces)
     aliases = {}
     if so_far is not None:
         aliases = {len(operands): 0}
@@ -366,14 +378,16 @@
         in_specs=specs,
         out_specs=hbm,
         scratch_shapes=[
+            pltpu.VMEM(pair.shape, jnp.bfloat16),
             pltpu.VMEM((chunks, 3 * rows + 2 * HALO, block), jnp.bfloat16),
             pltpu.VMEM((chunks, k_count, 2, rows, block), jnp.bfloat16),
             pltpu.VMEM((2,) + core_band.shape, jnp.bfloat16),
+            pltpu.SemaphoreType.DMA((3,)),
             pltpu.SemaphoreType.DMA((chunks, 5)),
             pltpu.SemaphoreType.DMA((chunks,)),
         ],
         input_output_aliases=aliases,
-        compiler_params=pltpu.CompilerParams(vmem_limit_bytes=MUCH),
+        compiler_params=pltpu.CompilerParams(vmem_limit_bytes=40 << 20),
         cost_estimate=pl.CostEstimate(
             flops=0,
             bytes_accessed=0,
@@ -400,26 +414,24 @@
     shared = to_pair_chip(lax.dynamic_slice_in_dim(start_block, group * piece, piece, axis=1))
     shared = after(shared, outgoing)
     third = to_pair_chip(after(start_block, shared)[:, 2 * piece : 3 * piece])
-    other = to_other_group(shared)
     near_shared = to_sibling(shared)
     sibling = to_sibling(start_block)
     shared_beyond = onward(shared)
 
-    begun = begin_bands(weights, after(incoming, other, near_shared, sibling), k_count, slot_count)
+    begun = begin_bands(weights, after(incoming, near_shared, sibling), k_count, slot_count)
     theirs = to_other_group(after(incoming, begun))
     third = after(third, begun)
-    fourth = to_pair_chip(after(start_block, third)[:, 3 * piece : 4 * piece])
+    fourth = to_pair_chip(after(start_block, third, shared_beyond)[:, 3 * piece : 4 * piece])
     third_beyond = onward(third)
-    begun = after(begun, shared_beyond)
     pair, for_core, for_chip = make_bands(weights, theirs, begun, k_count, slot_count)
     core_band, chip_band = to_sibling(for_core), to_next_chip(for_chip)
 
-    swapped = (core_band, chip_band)
-    fourth = after(fourth, *swapped)
-    shared_beyond, third_beyond = after(shared_beyond, *swapped), after(third_beyond, fourth)
-    near_shared_beyond, near_third_beyond = to_sibling(shared_beyond), to_sibling(third_beyond)
-    near_third, near_other = to_sibling(after(third, pair)), to_sibling(after(other, pair))
-    other_beyond = to_other_group(shared_beyond)
+    other = to_other_group(after(jnp.concatenate([shared, shared_beyond], axis=0), pair))
+    fourth = after(fourth, core_band, chip_band)
+    third_beyond = after(third_beyond, fourth)
+    near_shared_beyond = to_sibling(after(shared_beyond, chip_band))
+    near_third_beyond = to_sibling(third_beyond)
+    near_third = to_sibling(after(third, pair))
     fourth_beyond = onward(fourth)
     near_fourth = to_sibling(fourth)
 
@@ -427,18 +439,19 @@
         return filter_columns(places, pair, core_band, chip_band, start_block, sibling, halos, so_far)
 
     result = filtered(
-        [(0, piece), (2 * piece, 0)],
+        [(0, piece, 0), (2 * piece, 0, 0)],
         [
             (shared, shared_beyond, near_shared, near_shared_beyond),
             (third, third_beyond, near_third, near_third_beyond),
         ],
         None,
     )
-    other_beyond, fourth_beyond = after(other_beyond, result), after(fourth_beyond, result)
+    other, fourth_beyond = after(other, result), after(fourth_beyond, result)
+    near_other = to_sibling(other)
     return filtered(
-        [(piece, -piece), (3 * piece, 0)],
+        [(piece, -piece, row_count), (3 * piece, 0, 0)],
         [
-            (other, other_beyond, near_other, to_sibling(other_beyond)),
+            (other, other, near_other, near_other),
             (fourth, fourth_beyond, near_fourth, to_sibling(fourth_beyond)),
         ],
         result,

time: 74.3 us -> 71.7 us (0.965)
  the two profiles are of different devices: /device:TPU:0 before, /device:TPU:11 now
where the time goes in v4:
time: 71.7 us; the launch traced here: 70.8 us
  starting transfers between devices  24.9 us (35%)
  Pallas kernels  20.3 us (28%)
  waiting for transfers between devices  18.6 us (26%)
  local copies, waits for them, and re-layouts  5.54 us (8%)
  other arithmetic  1.06 us (1%)
    ppermute x18, starting transfers between devices, routed(): return lax.ppermute(value, ('kgrp', 'orb'), pairs)  18.7 us
    ppermute x18, waiting for transfers between devices, routed(): return lax.ppermute(value, ('kgrp', 'orb'), pairs)  16 us
    pallas_call x2, Pallas kernels, filter_columns(): pl.pallas_call(functools.partial(filter_kernel, places), out_shape=jax.Sh...  14.4 us
    all_to_all x1, starting transfers between devices, local(): lax.all_to_all(outgoing, 'orb', split_axis=0, concat_axis=0, tiled=True)  6.27 us
    unnamed x14, local copies, waits for them, and re-layouts  2.91 us
    pallas_call x1, Pallas kernels, pack_tiles(): pl.pallas_call(pack_kernel, out_shape=jax.ShapeDtypeStruct((slots, rows /...  2.66 us
    all_to_all x1, waiting for transfers between devices, local(): lax.all_to_all(outgoing, 'orb', split_axis=0, concat_axis=0, tiled=True)  2.51 us
    dynamic_slice x1, local copies, waits for them, and re-layouts, local(): lax.dynamic_slice_in_dim(start_block, group * piece, piece, axis=1)  1.79 us
  transfers between devices with their start and end apart: 19, of which 9 were waited for; matrix products, arithmetic and copies ran while one was open for 5% of the time, Pallas kernels for 19%

profile of v4, /device:TPU:11, one launch (start us, length us, event | category | flops | bytes accessed | tf_op | source)
XLA Modules:
  0.0 70.8 jit_solution(3128149167344914356)
XLA Ops:
  0.0 0.0 copy-start
  0.0 0.7 collective-permute-start.2
  0.7 0.0 copy-start.3
  0.7 0.0 copy-start.4
  0.7 1.8 %constant_dynamic-slice_fusion = bf16[96,2048]{1,0:T(8,128)(2,1)} fusion(bf16[96,8192]{1,0:T(8,128)(2,1)} %own_ref.3, s32[]{:T(128)S(6)} %select_n.3), kind=kLoop, calls=%fused_computation.1 | loop fusion | bytes 786436 | tf_op jit(solution)/shard_map/dynamic_slice | solution.py:414
  2.5 0.3 collective-permute-start
  2.8 2.7 %pack_tiles.1 = bf16[32,48,128]{2,1,0:T(8,128)(2,1)} custom-call(s32[12,1,32]{2,1,0:T(1,128)} %bitcast.4, bf16[24,96,128]{2,1,0:T(8,128)(2,1)} %bitcast.8), custom_call_target="tpu_custom_call" | custom-call | tf_op jit(solution)/shard_map/pack_tiles/pallas_call | solution.py:91
  5.4 6.3 %all-to-all-start = ((bf16[32,48,128]{2,1,0:T(8,128)(2,1)}), bf16[32,48,128]{2,1,0:T(8,128)(2,1)}, u32[]{:S(2)}, u32[]{:S(2)}) async-start(bf16[32,48,128]{2,1,0:T(8,128)(2,1)} %pack_tiles.1), calls=%async_computation | async-start | bytes 786432 | tf_op jit(solution)/shard_map/all_to_all | solution.py:412
  11.7 1.7 %collective-permute-done.rest_0_ = bf16[96,2048]{1,0:T(8,128)(2,1)S(1)} collective-permute-done((bf16[96,2048]{1,0:T(8,128)(2,1)}, bf16[96,2048]{1,0:T(8,128)(2,1)S(1)}, u32[]{:S(2)}, u32[]{:S(2)}) %collective-permute-start) | collective-permute-done | bytes 393248 | tf_op jit(solution)/shard_map/ppermute | solution.py:27
  13.4 1.8 %collective-permute-start.1 = (bf16[96,2048]{1,0:T(8,128)(2,1)S(1)}, bf16[96,2048]{1,0:T(8,128)(2,1)}, u32[]{:S(2)}, u32[]{:S(2)}) collective-permute-start(bf16[96,2048]{1,0:T(8,128)(2,1)S(1)} %collective-permute-done.rest_0_), channel_id=1, source_target_pairs={{0,1},{1,0},{2,3},{3,2},{4,5},{5,4},{6,7},{7,6},{8,9},{9,8},{10,11... | collective-permute-start | bytes 1179656 | tf_op jit(solution)/shard_map/ppermute | solution.py:27
  15.1 0.0 copy-done
  15.1 0.8 %slice.6 = bf16[96,2048]{1,0:T(8,128)(2,1)} slice(bf16[96,8192]{1,0:T(8,128)(2,1)S(1)} %copy-done), slice={[0:96], [4096:6144]} | slice | bytes 786432 | tf_op jit(solution)/shard_map/slice | solution.py:416
  16.0 0.0 collective-permute-start.8
  16.0 1.9 %collective-permute-start.6 = (bf16[96,2048]{1,0:T(8,128)(2,1)S(1)}, bf16[96,2048]{1,0:T(8,128)(2,1)}, u32[]{:S(2)}, u32[]{:S(2)}) collective-permute-start(bf16[96,2048]{1,0:T(8,128)(2,1)S(1)} %collective-permute-done.rest_0_), channel_id=1, source_target_pairs={{0,4},{1,5},{4,8},{5,9},{6,2},{7,3},{8,12},{9,13},{10,6},{11,7},{1... | collective-permute-start | bytes 1179656 | tf_op jit(solution)/shard_map/ppermute | solution.py:27
  17.9 0.0 copy-done.3
  17.9 0.0 copy-done.4
  17.9 0.0 copy-start.5
  17.9 0.7 copy-done.5
  18.6 0.0 copy-start.6
  18.6 0.7 copy-done.6
  19.3 0.9 %receive_weights.1.weight_ref = f32[16,2048]{1,0:T(8,128)S(1)} custom-call(f32[2,3]{1,0:T(2,128)S(1)} %copy-done.6, s32[3,32]{1,0:T(4,128)S(1)} %bitcast.7, s32[12,1,32]{2,1,0:T(1,128)S(1)} %bitcast.5, s32[12,32]{1,0:T(8,128)S(1)} %bitcast.6), custom_call_target="tpu_custom_call" | custom-call | tf_op jit(solution)/shard_map/receive_weights/pallas_call | solution.py:156
  20.2 0.0 copy-start.1
  20.2 0.6 copy-done.1
  20.8 2.5 %all-to-all-done.tiles_ref = bf16[32,48,128]{2,1,0:T(8,128)(2,1)} async-done(((bf16[32,48,128]{2,1,0:T(8,128)(2,1)}), bf16[32,48,128]{2,1,0:T(8,128)(2,1)}, u32[]{:S(2)}, u32[]{:S(2)}) %all-to-all-start) | async-done | bytes 393248 | tf_op jit(solution)/shard_map/all_to_all | solution.py:412
  23.3 0.0 collective-permute-done.1.rest_4_
  23.3 0.0 collective-permute-done.2.sibling_ref
  23.3 0.0 copy-start.2
  23.3 0.9 %copy-done.2 = f32[16,2048]{1,0:T(8,128)S(1)} copy-done((f32[16,2048]{1,0:T(8,128)S(1)}, f32[16,2048]{1,0:T(8,128)}, u32[]{:S(2)}) %copy-start.2) | copy-done | bytes 131096
  24.2 1.7 %begin_bands.1.begun_ref = bf16[2,192,512]{2,1,0:T(8,128)(2,1)S(1)} custom-call(f32[16,2048]{1,0:T(8,128)S(1)} %copy-done.2, bf16[32,48,128]{2,1,0:T(8,128)(2,1)} %all-to-all-done.tiles_ref), custom_call_target="tpu_custom_call" | custom-call | tf_op jit(solution)/shard_map/begin_bands/pallas_call | solution.py:227
  25.9 1.3 %collective-permute-start.3 = (bf16[32,48,128]{2,1,0:T(8,128)(2,1)}, bf16[32,48,128]{2,1,0:T(8,128)(2,1)S(1)}, u32[]{:S(2)}, u32[]{:S(2)}) collective-permute-start(bf16[32,48,128]{2,1,0:T(8,128)(2,1)} %all-to-all-done.tiles_ref), channel_id=1, source_target_pairs={{0,16},{1,17},{2,18},{3,19},{4,20},{5,21},{6,22},{7,23},{8,24},{9,... | collective-permute-start | bytes 1179656 | tf_op jit(solution)/shard_map/ppermute | solution.py:27
  27.2 1.1 %collective-permute-done.8.rest_1_ = bf16[96,2048]{1,0:T(8,128)(2,1)} collective-permute-done((bf16[96,2048]{1,0:T(8,128)(2,1)}, bf16[96,2048]{1,0:T(8,128)(2,1)}, u32[]{:S(2)}, u32[]{:S(2)}) %collective-permute-start.8) | collective-permute-done | bytes 393248 | tf_op jit(solution)/shard_map/ppermute | solution.py:27
  28.3 2.5 %collective-permute-done.6.rest_2_ = bf16[96,2048]{1,0:T(8,128)(2,1)} collective-permute-done((bf16[96,2048]{1,0:T(8,128)(2,1)S(1)}, bf16[96,2048]{1,0:T(8,128)(2,1)}, u32[]{:S(2)}, u32[]{:S(2)}) %collective-permute-start.6) | collective-permute-done | bytes 393248 | tf_op jit(solution)/shard_map/ppermute | solution.py:27
  30.8 0.1 collective-permute-start.10
  30.9 1.1 %pad_maximum_fusion = bf16[192,2048]{1,0:T(8,128)(2,1)S(1)} fusion(bf16[96,2048]{1,0:T(8,128)(2,1)} %collective-permute-done.6.rest_2_, bf16[96,2048]{1,0:T(8,128)(2,1)S(1)} %collective-permute-done.rest_0_), kind=kLoop, calls=%fused_computation | loop fusion | flops 1572864 | bytes 1572864 | tf_op jit(solution)/shard_map/concatenate | solution.py:429
  32.0 1.9 %collective-permute-start.9 = (bf16[96,2048]{1,0:T(8,128)(2,1)}, bf16[96,2048]{1,0:T(8,128)(2,1)S(1)}, u32[]{:S(2)}, u32[]{:S(2)}) collective-permute-start(bf16[96,2048]{1,0:T(8,128)(2,1)} %collective-permute-done.8.rest_1_), channel_id=1, source_target_pairs={{0,4},{1,5},{4,8},{5,9},{6,2},{7,3},{8,12},{9,13},{10,6},{11,7},{1... | collective-permute-start | bytes 1179656 | tf_op jit(solution)/shard_map/ppermute | solution.py:27
  33.9 3.3 %collective-permute-done.3.tiles_ref = bf16[32,48,128]{2,1,0:T(8,128)(2,1)S(1)} collective-permute-done((bf16[32,48,128]{2,1,0:T(8,128)(2,1)}, bf16[32,48,128]{2,1,0:T(8,128)(2,1)S(1)}, u32[]{:S(2)}, u32[]{:S(2)}) %collective-permute-start.3) | collective-permute-done | bytes 393248 | tf_op jit(solution)/shard_map/ppermute | solution.py:27
  37.2 0.7 %make_bands.1 = (bf16[2,192,512]{2,1,0:T(8,128)(2,1)S(1)}, bf16[2,2,80,256]{3,2,1,0:T(8,128)(2,1)S(1)}, bf16[2,2,80,256]{3,2,1,0:T(8,128)(2,1)S(1)}) custom-call(f32[16,2048]{1,0:T(8,128)S(1)} %copy-done.2, bf16[32,48,128]{2,1,0:T(8,128)(2,1)S(1)} %collective-permute-done.3.tiles_ref, bf16[2,192,512]{2,1,0:T(8,128)(2,1)S(1)} %begin_bands.1.begun_ref), custom_call_target="tpu_custom_call" | custom-call | tf_op jit(solution)/shard_map/make_bands/pallas_call | solution.py:242
  38.0 1.3 %collective-permute-start.7 = (bf16[192,2048]{1,0:T(8,128)(2,1)S(1)}, bf16[192,2048]{1,0:T(8,128)(2,1)S(1)}, u32[]{:S(2)}, u32[]{:S(2)}) collective-permute-start(bf16[192,2048]{1,0:T(8,128)(2,1)S(1)} %pad_maximum_fusion), channel_id=1, source_target_pairs={{0,16},{1,17},{2,18},{3,19},{4,20},{5,21},{6,22},{7,23},{8,24},{9,... | collective-permute-start | bytes 2359304 | tf_op jit(solution)/shard_map/ppermute | solution.py:27
  39.3 4.2 %collective-permute-start.5 = (bf16[2,2,80,256]{3,2,1,0:T(8,128)(2,1)S(1)}, bf16[2,2,80,256]{3,2,1,0:T(8,128)(2,1)S(1)}, u32[]{:S(2)}, u32[]{:S(2)}) collective-permute-start(bf16[2,2,80,256]{3,2,1,0:T(8,128)(2,1)S(1)} %get-tuple-element.26), channel_id=1, source_target_pairs={{1,2},{2,1},{3,4},{4,3},{5,6},{6,5},{7,8},{8,7},{9,10},{10,9},{11,... | collective-permute-start | bytes 491528 | tf_op jit(solution)/shard_map/ppermute | solution.py:27
  43.4 0.1 collective-permute-start.4
  43.5 3.4 %collective-permute-done.5.chip_ref = bf16[2,2,80,256]{3,2,1,0:T(8,128)(2,1)S(1)} collective-permute-done((bf16[2,2,80,256]{3,2,1,0:T(8,128)(2,1)S(1)}, bf16[2,2,80,256]{3,2,1,0:T(8,128)(2,1)S(1)}, u32[]{:S(2)}, u32[]{:S(2)}) %collective-permute-start.5) | collective-permute-done | bytes 163872 | tf_op jit(solution)/shard_map/ppermute | solution.py:27
  46.9 1.3 %collective-permute-start.11 = (bf16[96,2048]{1,0:T(8,128)(2,1)}, bf16[96,2048]{1,0:T(8,128)(2,1)S(1)}, u32[]{:S(2)}, u32[]{:S(2)}) collective-permute-start(bf16[96,2048]{1,0:T(8,128)(2,1)} %collective-permute-done.8.rest_1_), channel_id=1, source_target_pairs={{0,1},{1,0},{2,3},{3,2},{4,5},{5,4},{6,7},{7,6},{8,9},{9,8},{10,11... | collective-permute-start | bytes 1179656 | tf_op jit(solution)/shard_map/ppermute | solution.py:27
  48.2 0.0 collective-permute-done.10.rest_1_
  48.2 0.0 collective-permute-done.4.core_ref
  48.2 0.1 collective-permute-start.12
  48.3 0.0 collective-permute-done.9.rest_3_
  48.3 0.4 collective-permute-start.13
  48.8 1.9 %collective-permute-start.14 = (bf16[96,2048]{1,0:T(8,128)(2,1)S(1)}, bf16[96,2048]{1,0:T(8,128)(2,1)S(1)}, u32[]{:S(2)}, u32[]{:S(2)}) collective-permute-start(bf16[96,2048]{1,0:T(8,128)(2,1)S(1)} %collective-permute-done.10.rest_1_), channel_id=1, source_target_pairs={{0,4},{1,5},{4,8},{5,9},{6,2},{7,3},{8,12},{9,13},{10,6},{11,7},{1... | collective-permute-start | bytes 1179656 | tf_op jit(solution)/shard_map/ppermute | solution.py:27
  50.7 0.0 collective-permute-done.11.rest_5_
  50.7 0.2 collective-permute-done.12.rest_6_
  50.9 0.0 collective-permute-done.13.rest_7_
  50.9 7.3 %filter_columns.2.rest_8_ = bf16[2,2,96,8192]{3,2,1,0:T(8,128)(2,1)} custom-call(bf16[2,192,512]{2,1,0:T(8,128)(2,1)S(1)} %get-tuple-element.24.pair_source, bf16[2,2,80,256]{3,2,1,0:T(8,128)(2,1)S(1)} %collective-permute-done.4.core_ref, bf16[2,2,80,256]{3,2,1,0:T(8,128)(2,1)S(1)} %collective-permute-done.5.chip_ref, bf16[96,8192]{1,0:T(8,128)(2,1)S(1)} %copy-done, ...), custom_call_target="tpu_custom_call" | custom-call | tf_op jit(solution)/shard_map/filter_columns/pallas_call | solution.py:375
  58.3 0.0 collective-permute-done.7.rest_0_.rest_2_
  58.3 0.5 collective-permute-start.15
  58.7 0.1 collective-permute-start.16
  58.8 2.5 %collective-permute-done.14.rest_3_ = bf16[96,2048]{1,0:T(8,128)(2,1)S(1)} collective-permute-done((bf16[96,2048]{1,0:T(8,128)(2,1)S(1)}, bf16[96,2048]{1,0:T(8,128)(2,1)S(1)}, u32[]{:S(2)}, u32[]{:S(2)}) %collective-permute-start.14) | collective-permute-done | bytes 393248 | tf_op jit(solution)/shard_map/ppermute | solution.py:27
  61.3 0.8 %collective-permute-start.17 = (bf16[96,2048]{1,0:T(8,128)(2,1)S(1)}, bf16[96,2048]{1,0:T(8,128)(2,1)S(1)}, u32[]{:S(2)}, u32[]{:S(2)}) collective-permute-start(bf16[96,2048]{1,0:T(8,128)(2,1)S(1)} %collective-permute-done.14.rest_3_), channel_id=1, source_target_pairs={{0,1},{1,0},{2,3},{3,2},{4,5},{5,4},{6,7},{7,6},{8,9},{9,8},{10,11... | collective-permute-start | bytes 1179656 | tf_op jit(solution)/shard_map/ppermute | solution.py:27
  62.2 0.0 collective-permute-done.16.rest_5_
  62.2 1.3 %collective-permute-done.17.rest_7_ = bf16[96,2048]{1,0:T(8,128)(2,1)S(1)} collective-permute-done((bf16[96,2048]{1,0:T(8,128)(2,1)S(1)}, bf16[96,2048]{1,0:T(8,128)(2,1)S(1)}, u32[]{:S(2)}, u32[]{:S(2)}) %collective-permute-start.17) | collective-permute-done | bytes 393248 | tf_op jit(solution)/shard_map/ppermute | solution.py:27
  63.5 0.0 collective-permute-done.15.rest_4_.rest_6_
  63.5 7.1 %filter_columns.3 = bf16[2,2,96,8192]{3,2,1,0:T(8,128)(2,1)} custom-call(bf16[2,192,512]{2,1,0:T(8,128)(2,1)S(1)} %get-tuple-element.24.pair_source, bf16[2,2,80,256]{3,2,1,0:T(8,128)(2,1)S(1)} %collective-permute-done.4.core_ref, bf16[2,2,80,256]{3,2,1,0:T(8,128)(2,1)S(1)} %collective-permute-done.5.chip_ref, ...), custom_call_target="tpu_custom_call", output_to_operand_aliasing={{}: (13, {})} | custom-call | tf_op jit(solution)/shard_map/filter_columns/pallas_call | solution.py:375
  (1 shorter events, 0.0 us)
Async XLA Ops:
  0.0 15.1 %copy-start = (bf16[96,8192]{1,0:T(8,128)(2,1)S(1)}, bf16[96,8192]{1,0:T(8,128)(2,1)}, u32[]{:S(2)}) copy-start(bf16[96,8192]{1,0:T(8,128)(2,1)} %own_ref.3) | copy-start | bytes 4718596
  0.0 23.3 %collective-permute-start.2 = (bf16[96,8192]{1,0:T(8,128)(2,1)}, bf16[96,8192]{1,0:T(8,128)(2,1)S(1)}, u32[]{:S(2)}, u32[]{:S(2)}) collective-permute-start(bf16[96,8192]{1,0:T(8,128)(2,1)} %own_ref.3), channel_id=1, source_target_pairs={{0,1},{1,0},{2,3},{3,2},{4,5},{5,4},{6,7},{7,6},{8,9},{9,8},{10,11... | collective-permute-start | bytes 4718600 | tf_op jit(solution)/shard_map/ppermute | solution.py:27
  0.7 17.2 %copy-start.3 = (s32[32,12,1]{0,2,1:T(1,128)S(1)}, s32[32,12,1]{0,2,1:T(1,128)}, u32[]{:S(2)}) copy-start(s32[32,12,1]{0,2,1:T(1,128)} %param.7) | copy-start | bytes 4612
  0.7 17.2 %copy-start.4 = (s32[32,12]{0,1:T(8,128)S(1)}, s32[32,12]{0,1:T(8,128)}, u32[]{:S(2)}) copy-start(s32[32,12]{0,1:T(8,128)} %param.8) | copy-start | bytes 4612
  2.5 10.9 %collective-permute-start = (bf16[96,2048]{1,0:T(8,128)(2,1)}, bf16[96,2048]{1,0:T(8,128)(2,1)S(1)}, u32[]{:S(2)}, u32[]{:S(2)}) collective-permute-start(bf16[96,2048]{1,0:T(8,128)(2,1)} %constant_dynamic-slice_fusion), channel_id=1, source_target_pairs={{0,2},{1,3},{2,0},{3,1},{4,6},{5,7},{6,4},{7,5},{8,10},{9,11},{10,... | collective-permute-start | bytes 1179656 | tf_op jit(solution)/shard_map/ppermute | solution.py:27
  5.4 17.9 %all-to-all-start = ((bf16[32,48,128]{2,1,0:T(8,128)(2,1)}), bf16[32,48,128]{2,1,0:T(8,128)(2,1)}, u32[]{:S(2)}, u32[]{:S(2)}) async-start(bf16[32,48,128]{2,1,0:T(8,128)(2,1)} %pack_tiles.1), calls=%async_computation | async-start | bytes 786432 | tf_op jit(solution)/shard_map/all_to_all | solution.py:412
  13.4 9.9 %collective-permute-start.1 = (bf16[96,2048]{1,0:T(8,128)(2,1)S(1)}, bf16[96,2048]{1,0:T(8,128)(2,1)}, u32[]{:S(2)}, u32[]{:S(2)}) collective-permute-start(bf16[96,2048]{1,0:T(8,128)(2,1)S(1)} %collective-permute-done.rest_0_), channel_id=1, source_target_pairs={{0,1},{1,0},{2,3},{3,2},{4,5},{5,4},{6,7},{7,6},{8,9},{9,8},{10,11... | collective-permute-start | bytes 1179656 | tf_op jit(solution)/shard_map/ppermute | solution.py:27
  16.0 12.4 %collective-permute-start.8 = (bf16[96,2048]{1,0:T(8,128)(2,1)}, bf16[96,2048]{1,0:T(8,128)(2,1)}, u32[]{:S(2)}, u32[]{:S(2)}) collective-permute-start(bf16[96,2048]{1,0:T(8,128)(2,1)} %slice.6), channel_id=1, source_target_pairs={{0,2},{1,3},{2,0},{3,1},{4,6},{5,7},{6,4},{7,5},{8,10},{9,11},{10,... | collective-permute-start | bytes 1179656 | tf_op jit(solution)/shard_map/ppermute | solution.py:27
  16.0 14.8 %collective-permute-start.6 = (bf16[96,2048]{1,0:T(8,128)(2,1)S(1)}, bf16[96,2048]{1,0:T(8,128)(2,1)}, u32[]{:S(2)}, u32[]{:S(2)}) collective-permute-start(bf16[96,2048]{1,0:T(8,128)(2,1)S(1)} %collective-permute-done.rest_0_), channel_id=1, source_target_pairs={{0,4},{1,5},{4,8},{5,9},{6,2},{7,3},{8,12},{9,13},{10,6},{11,7},{1... | collective-permute-start | bytes 1179656 | tf_op jit(solution)/shard_map/ppermute | solution.py:27
  17.9 0.7 copy-start.5
  18.6 0.7 copy-start.6
  20.2 0.6 copy-start.1
  23.3 0.9 %copy-start.2 = (f32[16,2048]{1,0:T(8,128)S(1)}, f32[16,2048]{1,0:T(8,128)}, u32[]{:S(2)}) copy-start(f32[16,2048]{1,0:T(8,128)} %copy-done.1) | copy-start | bytes 393220
  25.9 11.3 %collective-permute-start.3 = (bf16[32,48,128]{2,1,0:T(8,128)(2,1)}, bf16[32,48,128]{2,1,0:T(8,128)(2,1)S(1)}, u32[]{:S(2)}, u32[]{:S(2)}) collective-permute-start(bf16[32,48,128]{2,1,0:T(8,128)(2,1)} %all-to-all-done.tiles_ref), channel_id=1, source_target_pairs={{0,16},{1,17},{2,18},{3,19},{4,20},{5,21},{6,22},{7,23},{8,24},{9,... | collective-permute-start | bytes 1179656 | tf_op jit(solution)/shard_map/ppermute | solution.py:27
  30.8 17.4 %collective-permute-start.10 = (bf16[96,2048]{1,0:T(8,128)(2,1)S(1)}, bf16[96,2048]{1,0:T(8,128)(2,1)S(1)}, u32[]{:S(2)}, u32[]{:S(2)}) collective-permute-start(bf16[96,2048]{1,0:T(8,128)(2,1)S(1)} %slice.7), channel_id=1, source_target_pairs={{0,2},{1,3},{2,0},{3,1},{4,6},{5,7},{6,4},{7,5},{8,10},{9,11},{10,... | collective-permute-start | bytes 1179656 | tf_op jit(solution)/shard_map/ppermute | solution.py:27
  32.0 16.3 %collective-permute-start.9 = (bf16[96,2048]{1,0:T(8,128)(2,1)}, bf16[96,2048]{1,0:T(8,128)(2,1)S(1)}, u32[]{:S(2)}, u32[]{:S(2)}) collective-permute-start(bf16[96,2048]{1,0:T(8,128)(2,1)} %collective-permute-done.8.rest_1_), channel_id=1, source_target_pairs={{0,4},{1,5},{4,8},{5,9},{6,2},{7,3},{8,12},{9,13},{10,6},{11,7},{1... | collective-permute-start | bytes 1179656 | tf_op jit(solution)/shard_map/ppermute | solution.py:27
  38.0 20.3 %collective-permute-start.7 = (bf16[192,2048]{1,0:T(8,128)(2,1)S(1)}, bf16[192,2048]{1,0:T(8,128)(2,1)S(1)}, u32[]{:S(2)}, u32[]{:S(2)}) collective-permute-start(bf16[192,2048]{1,0:T(8,128)(2,1)S(1)} %pad_maximum_fusion), channel_id=1, source_target_pairs={{0,16},{1,17},{2,18},{3,19},{4,20},{5,21},{6,22},{7,23},{8,24},{9,... | collective-permute-start | bytes 2359304 | tf_op jit(solution)/shard_map/ppermute | solution.py:27
  39.3 7.6 %collective-permute-start.5 = (bf16[2,2,80,256]{3,2,1,0:T(8,128)(2,1)S(1)}, bf16[2,2,80,256]{3,2,1,0:T(8,128)(2,1)S(1)}, u32[]{:S(2)}, u32[]{:S(2)}) collective-permute-start(bf16[2,2,80,256]{3,2,1,0:T(8,128)(2,1)S(1)} %get-tuple-element.26), channel_id=1, source_target_pairs={{1,2},{2,1},{3,4},{4,3},{5,6},{6,5},{7,8},{8,7},{9,10},{10,9},{11,... | collective-permute-start | bytes 491528 | tf_op jit(solution)/shard_map/ppermute | solution.py:27
  43.4 4.8 %collective-permute-start.4 = (bf16[2,2,80,256]{3,2,1,0:T(8,128)(2,1)S(1)}, bf16[2,2,80,256]{3,2,1,0:T(8,128)(2,1)S(1)}, u32[]{:S(2)}, u32[]{:S(2)}) collective-permute-start(bf16[2,2,80,256]{3,2,1,0:T(8,128)(2,1)S(1)} %get-tuple-element.25), channel_id=1, source_target_pairs={{0,1},{1,0},{2,3},{3,2},{4,5},{5,4},{6,7},{7,6},{8,9},{9,8},{10,11... | collective-permute-start | bytes 491528 | tf_op jit(solution)/shard_map/ppermute | solution.py:27
  46.9 3.8 %collective-permute-start.11 = (bf16[96,2048]{1,0:T(8,128)(2,1)}, bf16[96,2048]{1,0:T(8,128)(2,1)S(1)}, u32[]{:S(2)}, u32[]{:S(2)}) collective-permute-start(bf16[96,2048]{1,0:T(8,128)(2,1)} %collective-permute-done.8.rest_1_), channel_id=1, source_target_pairs={{0,1},{1,0},{2,3},{3,2},{4,5},{5,4},{6,7},{7,6},{8,9},{9,8},{10,11... | collective-permute-start | bytes 1179656 | tf_op jit(solution)/shard_map/ppermute | solution.py:27
  48.2 2.7 %collective-permute-start.12 = (bf16[96,2048]{1,0:T(8,128)(2,1)}, bf16[96,2048]{1,0:T(8,128)(2,1)S(1)}, u32[]{:S(2)}, u32[]{:S(2)}) collective-permute-start(bf16[96,2048]{1,0:T(8,128)(2,1)} %collective-permute-done.6.rest_2_), channel_id=1, source_target_pairs={{0,1},{1,0},{2,3},{3,2},{4,5},{5,4},{6,7},{7,6},{8,9},{9,8},{10,11... | collective-permute-start | bytes 1179656 | tf_op jit(solution)/shard_map/ppermute | solution.py:27
  48.3 2.6 %collective-permute-start.13 = (bf16[96,2048]{1,0:T(8,128)(2,1)S(1)}, bf16[96,2048]{1,0:T(8,128)(2,1)S(1)}, u32[]{:S(2)}, u32[]{:S(2)}) collective-permute-start(bf16[96,2048]{1,0:T(8,128)(2,1)S(1)} %collective-permute-done.9.rest_3_), channel_id=1, source_target_pairs={{0,1},{1,0},{2,3},{3,2},{4,5},{5,4},{6,7},{7,6},{8,9},{9,8},{10,11... | collective-permute-start | bytes 1179656 | tf_op jit(solution)/shard_map/ppermute | solution.py:27
  48.8 12.6 %collective-permute-start.14 = (bf16[96,2048]{1,0:T(8,128)(2,1)S(1)}, bf16[96,2048]{1,0:T(8,128)(2,1)S(1)}, u32[]{:S(2)}, u32[]{:S(2)}) collective-permute-start(bf16[96,2048]{1,0:T(8,128)(2,1)S(1)} %collective-permute-done.10.rest_1_), channel_id=1, source_target_pairs={{0,4},{1,5},{4,8},{5,9},{6,2},{7,3},{8,12},{9,13},{10,6},{11,7},{1... | collective-permute-start | bytes 1179656 | tf_op jit(solution)/shard_map/ppermute | solution.py:27
  58.3 5.3 %collective-permute-start.15 = (bf16[192,2048]{1,0:T(8,128)(2,1)S(1)}, bf16[192,2048]{1,0:T(8,128)(2,1)S(1)}, u32[]{:S(2)}, u32[]{:S(2)}) collective-permute-start(bf16[192,2048]{1,0:T(8,128)(2,1)S(1)} %collective-permute-done.7.rest_0_.rest_2_), channel_id=1, source_target_pairs={{0,1},{1,0},{2,3},{3,2},{4,5},{5,4},{6,7},{7,6},{8,9},{9,8},{10,11... | collective-permute-start | bytes 2359304 | tf_op jit(solution)/shard_map/ppermute | solution.py:27
  58.7 3.5 %collective-permute-start.16 = (bf16[96,2048]{1,0:T(8,128)(2,1)S(1)}, bf16[96,2048]{1,0:T(8,128)(2,1)S(1)}, u32[]{:S(2)}, u32[]{:S(2)}) collective-permute-start(bf16[96,2048]{1,0:T(8,128)(2,1)S(1)} %collective-permute-done.10.rest_1_), channel_id=1, source_target_pairs={{0,1},{1,0},{2,3},{3,2},{4,5},{5,4},{6,7},{7,6},{8,9},{9,8},{10,11... | collective-permute-start | bytes 1179656 | tf_op jit(solution)/shard_map/ppermute | solution.py:27
  61.3 2.2 %collective-permute-start.17 = (bf16[96,2048]{1,0:T(8,128)(2,1)S(1)}, bf16[96,2048]{1,0:T(8,128)(2,1)S(1)}, u32[]{:S(2)}, u32[]{:S(2)}) collective-permute-start(bf16[96,2048]{1,0:T(8,128)(2,1)S(1)} %collective-permute-done.14.rest_3_), channel_id=1, source_target_pairs={{0,1},{1,0},{2,3},{3,2},{4,5},{5,4},{6,7},{7,6},{8,9},{9,8},{10,11... | collective-permute-start | bytes 1179656 | tf_op jit(solution)/shard_map/ppermute | solution.py:27

commit v5 on v4

--- a/solution.py
+++ b/solution.py
@@ -387,7 +387,7 @@
             pltpu.SemaphoreType.DMA((chunks,)),
         ],
         input_output_aliases=aliases,
-        compiler_params=pltpu.CompilerParams(vmem_limit_bytes=40 << 20),
+        compiler_params=pltpu.CompilerParams(vmem_limit_bytes=49 << 20),
         cost_estimate=pl.CostEstimate(
             flops=0,
             bytes_accessed=0,
@@ -418,10 +418,11 @@
     sibling = to_sibling(start_block)
     shared_beyond = onward(shared)
 
-    begun = begin_bands(weights, after(incoming, near_shared, sibling), k_count, slot_count)
+    last = after(start_block, shared)[:, 3 * piece : 4 * piece]
+    begun = begin_bands(weights, after(incoming, near_shared, sibling, last), k_count, slot_count)
     theirs = to_other_group(after(incoming, begun))
     third = after(third, begun)
-    fourth = to_pair_chip(after(start_block, third, shared_beyond)[:, 3 * piece : 4 * piece])
+    fourth = to_pair_chip(after(last, third, shared_beyond))
     third_beyond = onward(third)
     pair, for_core, for_chip = make_bands(weights, theirs, begun, k_count, slot_count)
     core_band, chip_band = to_sibling(for_core), to_next_chip(for_chip)

time: 71.7 us -> 68.9 us (0.961)
  waiting for transfers between devices: 18.6 us -> 22.9 us
  local copies, waits for them, and re-layouts: 5.54 us -> 2.2 us
  starting transfers between devices: 24.9 us -> 22.8 us
  other arithmetic: 1.06 us -> 0.05 us
    unnamed x14 -> x8, local copies, waits for them, and re-layouts: 2.91 us -> 0.01 us
    ppermute x18, waiting for transfers between devices: 16 us -> 18.3 us  [routed(): return lax.ppermute(value, ('kgrp', 'orb'), pairs)]
    all_to_all x1, waiting for transfers between devices: 2.51 us -> 4.62 us  [local(): lax.all_to_all(outgoing, 'orb', split_axis=0, concat_axis=0, tiled=True)]
    ppermute x18, starting transfers between devices: 18.7 us -> 16.7 us  [routed(): return lax.ppermute(value, ('kgrp', 'orb'), pairs)]
    concatenate x1, other arithmetic: 1.06 us -> 0.05 us  [local(): jnp.concatenate([shared, shared_beyond], axis=0)]
    pallas_call x1, Pallas kernels: 1.69 us -> 0.69 us  [begin_bands(): pl.pallas_call(functools.partial(begin_kernel, k_count, slot_count), out_...]
    dynamic_slice x1, local copies, waits for them, and re-layouts: 1.79 us -> 1.02 us  [local(): lax.dynamic_slice_in_dim(start_block, group * piece, piece, axis=1)]
  transfers between devices with their start and end apart: 19 -> 19, of which waited for: 9 -> 8; matrix products, arithmetic and copies ran while one was open for 5% -> 3% of each run, Pallas kernels for 19% -> 18%
where the time goes in v5:
time: 68.9 us; the launch traced here: 67.9 us
  waiting for transfers between devices  22.9 us (33%)
  starting transfers between devices  22.8 us (33%)
  Pallas kernels  19.7 us (29%)
  local copies, waits for them, and re-layouts  2.2 us (3%)
    ppermute x18, waiting for transfers between devices, routed(): return lax.ppermute(value, ('kgrp', 'orb'), pairs)  18.3 us
    ppermute x18, starting transfers between devices, routed(): return lax.ppermute(value, ('kgrp', 'orb'), pairs)  16.7 us
    pallas_call x2, Pallas kernels, filter_columns(): pl.pallas_call(functools.partial(filter_kernel, places), out_shape=jax.Sh...  14.7 us
    all_to_all x1, starting transfers between devices, local(): lax.all_to_all(outgoing, 'orb', split_axis=0, concat_axis=0, tiled=True)  6.19 us
    all_to_all x1, waiting for transfers between devices, local(): lax.all_to_all(outgoing, 'orb', split_axis=0, concat_axis=0, tiled=True)  4.62 us
    pallas_call x1, Pallas kernels, pack_tiles(): pl.pallas_call(pack_kernel, out_shape=jax.ShapeDtypeStruct((slots, rows /...  2.71 us
  transfers between devices with their start and end apart: 19, of which 8 were waited for; matrix products, arithmetic and copies ran while one was open for 3% of the time, Pallas kernels for 18%

profile of v5, /device:TPU:11, one launch (start us, length us, event | category | flops | bytes accessed | tf_op | source)
XLA Modules:
  0.0 67.9 jit_solution(12936282671763164129)
XLA Ops:
  0.0 0.7 collective-permute-start.2
  0.7 1.0 %constant_dynamic-slice_fusion = bf16[96,2048]{1,0:T(8,128)(2,1)S(1)} fusion(bf16[96,8192]{1,0:T(8,128)(2,1)} %own_ref.3, s32[]{:T(128)S(6)} %select_n.3), kind=kLoop, calls=%fused_computation.1 | loop fusion | bytes 786436 | tf_op jit(solution)/shard_map/dynamic_slice | solution.py:414
  1.7 0.3 collective-permute-start
  2.0 0.0 copy-start
  2.0 0.0 copy-start.1
  2.0 0.0 copy-start.2
  2.0 0.0 copy-start.3
  2.0 2.7 %pack_tiles.1 = bf16[32,48,128]{2,1,0:T(8,128)(2,1)} custom-call(s32[12,1,32]{2,1,0:T(1,128)} %bitcast.4, bf16[24,96,128]{2,1,0:T(8,128)(2,1)} %bitcast.8), custom_call_target="tpu_custom_call" | custom-call | tf_op jit(solution)/shard_map/pack_tiles/pallas_call | solution.py:91
  4.7 6.2 %all-to-all-start = ((bf16[32,48,128]{2,1,0:T(8,128)(2,1)}), bf16[32,48,128]{2,1,0:T(8,128)(2,1)S(1)}, u32[]{:S(2)}, u32[]{:S(2)}) async-start(bf16[32,48,128]{2,1,0:T(8,128)(2,1)} %pack_tiles.1), calls=%async_computation | async-start | bytes 786432 | tf_op jit(solution)/shard_map/all_to_all | solution.py:412
  10.9 1.6 %collective-permute-done.rest_0_ = bf16[96,2048]{1,0:T(8,128)(2,1)S(1)} collective-permute-done((bf16[96,2048]{1,0:T(8,128)(2,1)S(1)}, bf16[96,2048]{1,0:T(8,128)(2,1)S(1)}, u32[]{:S(2)}, u32[]{:S(2)}) %collective-permute-start) | collective-permute-done | bytes 393248 | tf_op jit(solution)/shard_map/ppermute | solution.py:27
  12.5 1.2 %collective-permute-start.1 = (bf16[96,2048]{1,0:T(8,128)(2,1)S(1)}, bf16[96,2048]{1,0:T(8,128)(2,1)S(1)}, u32[]{:S(2)}, u32[]{:S(2)}) collective-permute-start(bf16[96,2048]{1,0:T(8,128)(2,1)S(1)} %collective-permute-done.rest_0_), channel_id=1, source_target_pairs={{0,1},{1,0},{2,3},{3,2},{4,5},{5,4},{6,7},{7,6},{8,9},{9,8},{10,11... | collective-permute-start | bytes 1179656 | tf_op jit(solution)/shard_map/ppermute | solution.py:27
  13.7 1.2 %fusion = (bf16[96,2048]{1,0:T(8,128)(2,1)S(1)}, bf16[96,2048]{1,0:T(8,128)(2,1)S(1)}) fusion(bf16[96,8192]{1,0:T(8,128)(2,1)} %own_ref.3), kind=kLoop, calls=%fused_computation.2 | loop fusion | bytes 1572864 | tf_op jit(solution)/shard_map/slice | solution.py:416
  14.8 0.1 collective-permute-start.8
  14.9 2.0 %collective-permute-start.6 = (bf16[96,2048]{1,0:T(8,128)(2,1)S(1)}, bf16[96,2048]{1,0:T(8,128)(2,1)S(1)}, u32[]{:S(2)}, u32[]{:S(2)}) collective-permute-start(bf16[96,2048]{1,0:T(8,128)(2,1)S(1)} %collective-permute-done.rest_0_), channel_id=1, source_target_pairs={{0,4},{1,5},{4,8},{5,9},{6,2},{7,3},{8,12},{9,13},{10,6},{11,7},{1... | collective-permute-start | bytes 1179656 | tf_op jit(solution)/shard_map/ppermute | solution.py:27
  16.9 0.0 copy-done
  16.9 0.0 copy-done.1
  16.9 0.0 copy-done.2
  16.9 0.0 copy-done.3
  16.9 0.9 %receive_weights.1.weight_ref = f32[16,2048]{1,0:T(8,128)S(1)} custom-call(f32[2,3]{1,0:T(2,128)S(1)} %copy-done.3, s32[3,32]{1,0:T(4,128)S(1)} %bitcast.7, s32[12,1,32]{2,1,0:T(1,128)S(1)} %bitcast.5, s32[12,32]{1,0:T(8,128)S(1)} %bitcast.6), custom_call_target="tpu_custom_call" | custom-call | tf_op jit(solution)/shard_map/receive_weights/pallas_call | solution.py:156
  17.8 4.6 %all-to-all-done.tiles_ref = bf16[32,48,128]{2,1,0:T(8,128)(2,1)S(1)} async-done(((bf16[32,48,128]{2,1,0:T(8,128)(2,1)}), bf16[32,48,128]{2,1,0:T(8,128)(2,1)S(1)}, u32[]{:S(2)}, u32[]{:S(2)}) %all-to-all-start) | async-done | bytes 393248 | tf_op jit(solution)/shard_map/all_to_all | solution.py:412
  22.5 0.0 collective-permute-done.1.rest_4_
  22.5 0.0 collective-permute-done.2.sibling_ref
  22.5 0.7 %begin_bands.1.begun_ref = bf16[2,192,512]{2,1,0:T(8,128)(2,1)S(1)} custom-call(f32[16,2048]{1,0:T(8,128)S(1)} %receive_weights.1.weight_ref, bf16[32,48,128]{2,1,0:T(8,128)(2,1)S(1)} %all-to-all-done.tiles_ref), custom_call_target="tpu_custom_call" | custom-call | tf_op jit(solution)/shard_map/begin_bands/pallas_call | solution.py:227
  23.2 1.3 %collective-permute-start.3 = (bf16[32,48,128]{2,1,0:T(8,128)(2,1)S(1)}, bf16[32,48,128]{2,1,0:T(8,128)(2,1)S(1)}, u32[]{:S(2)}, u32[]{:S(2)}) collective-permute-start(bf16[32,48,128]{2,1,0:T(8,128)(2,1)S(1)} %all-to-all-done.tiles_ref), channel_id=1, source_target_pairs={{0,16},{1,17},{2,18},{3,19},{4,20},{5,21},{6,22},{7,23},{8,24},{9,... | collective-permute-start | bytes 1179656 | tf_op jit(solution)/shard_map/ppermute | solution.py:27
  24.5 2.5 %collective-permute-done.8.rest_1_ = bf16[96,2048]{1,0:T(8,128)(2,1)S(1)} collective-permute-done((bf16[96,2048]{1,0:T(8,128)(2,1)S(1)}, bf16[96,2048]{1,0:T(8,128)(2,1)S(1)}, u32[]{:S(2)}, u32[]{:S(2)}) %collective-permute-start.8) | collective-permute-done | bytes 393248 | tf_op jit(solution)/shard_map/ppermute | solution.py:27
  27.0 3.0 %collective-permute-done.6.rest_2_ = bf16[96,2048]{1,0:T(8,128)(2,1)S(1)} collective-permute-done((bf16[96,2048]{1,0:T(8,128)(2,1)S(1)}, bf16[96,2048]{1,0:T(8,128)(2,1)S(1)}, u32[]{:S(2)}, u32[]{:S(2)}) %collective-permute-start.6) | collective-permute-done | bytes 393248 | tf_op jit(solution)/shard_map/ppermute | solution.py:27
  29.9 0.0 collective-permute-start.10
  29.9 0.1 pad_maximum_fusion
  30.0 1.9 %collective-permute-start.9 = (bf16[96,2048]{1,0:T(8,128)(2,1)S(1)}, bf16[96,2048]{1,0:T(8,128)(2,1)S(1)}, u32[]{:S(2)}, u32[]{:S(2)}) collective-permute-start(bf16[96,2048]{1,0:T(8,128)(2,1)S(1)} %collective-permute-done.8.rest_1_), channel_id=1, source_target_pairs={{0,4},{1,5},{4,8},{5,9},{6,2},{7,3},{8,12},{9,13},{10,6},{11,7},{1... | collective-permute-start | bytes 1179656 | tf_op jit(solution)/shard_map/ppermute | solution.py:27
  31.9 2.4 %collective-permute-done.3.tiles_ref = bf16[32,48,128]{2,1,0:T(8,128)(2,1)S(1)} collective-permute-done((bf16[32,48,128]{2,1,0:T(8,128)(2,1)S(1)}, bf16[32,48,128]{2,1,0:T(8,128)(2,1)S(1)}, u32[]{:S(2)}, u32[]{:S(2)}) %collective-permute-start.3) | collective-permute-done | bytes 393248 | tf_op jit(solution)/shard_map/ppermute | solution.py:27
  34.3 0.7 %make_bands.1 = (bf16[2,192,512]{2,1,0:T(8,128)(2,1)S(1)}, bf16[2,2,80,256]{3,2,1,0:T(8,128)(2,1)S(1)}, bf16[2,2,80,256]{3,2,1,0:T(8,128)(2,1)S(1)}) custom-call(f32[16,2048]{1,0:T(8,128)S(1)} %receive_weights.1.weight_ref, bf16[32,48,128]{2,1,0:T(8,128)(2,1)S(1)} %collective-permute-done.3.tiles_ref, bf16[2,192,512]{2,1,0:T(8,128)(2,1)S(1)} %begin_bands.1.begun_ref), custom_call_target="tpu_custom_call" | custom-call | tf_op jit(solution)/shard_map/make_bands/pallas_call | solution.py:242
  35.0 1.3 %collective-permute-start.7 = (bf16[192,2048]{1,0:T(8,128)(2,1)S(1)}, bf16[192,2048]{1,0:T(8,128)(2,1)S(1)}, u32[]{:S(2)}, u32[]{:S(2)}) collective-permute-start(bf16[192,2048]{1,0:T(8,128)(2,1)S(1)} %pad_maximum_fusion), channel_id=1, source_target_pairs={{0,16},{1,17},{2,18},{3,19},{4,20},{5,21},{6,22},{7,23},{8,24},{9,... | collective-permute-start | bytes 2359304 | tf_op jit(solution)/shard_map/ppermute | solution.py:27
  36.3 2.7 %collective-permute-start.5 = (bf16[2,2,80,256]{3,2,1,0:T(8,128)(2,1)S(1)}, bf16[2,2,80,256]{3,2,1,0:T(8,128)(2,1)S(1)}, u32[]{:S(2)}, u32[]{:S(2)}) collective-permute-start(bf16[2,2,80,256]{3,2,1,0:T(8,128)(2,1)S(1)} %get-tuple-element.27), channel_id=1, source_target_pairs={{1,2},{2,1},{3,4},{4,3},{5,6},{6,5},{7,8},{8,7},{9,10},{10,9},{11,... | collective-permute-start | bytes 491528 | tf_op jit(solution)/shard_map/ppermute | solution.py:27
  39.0 0.1 collective-permute-start.4
  39.1 4.9 %collective-permute-done.5.chip_ref = bf16[2,2,80,256]{3,2,1,0:T(8,128)(2,1)S(1)} collective-permute-done((bf16[2,2,80,256]{3,2,1,0:T(8,128)(2,1)S(1)}, bf16[2,2,80,256]{3,2,1,0:T(8,128)(2,1)S(1)}, u32[]{:S(2)}, u32[]{:S(2)}) %collective-permute-start.5) | collective-permute-done | bytes 163872 | tf_op jit(solution)/shard_map/ppermute | solution.py:27
  43.9 1.3 %collective-permute-start.11 = (bf16[96,2048]{1,0:T(8,128)(2,1)S(1)}, bf16[96,2048]{1,0:T(8,128)(2,1)S(1)}, u32[]{:S(2)}, u32[]{:S(2)}) collective-permute-start(bf16[96,2048]{1,0:T(8,128)(2,1)S(1)} %collective-permute-done.8.rest_1_), channel_id=1, source_target_pairs={{0,1},{1,0},{2,3},{3,2},{4,5},{5,4},{6,7},{7,6},{8,9},{9,8},{10,11... | collective-permute-start | bytes 1179656 | tf_op jit(solution)/shard_map/ppermute | solution.py:27
  45.3 0.0 collective-permute-done.10.rest_1_
  45.3 0.0 collective-permute-start.12
  45.3 0.0 collective-permute-done.4.core_ref
  45.3 0.0 collective-permute-done.9.rest_3_
  45.3 0.5 collective-permute-start.13
  45.8 1.9 %collective-permute-start.14 = (bf16[96,2048]{1,0:T(8,128)(2,1)S(1)}, bf16[96,2048]{1,0:T(8,128)(2,1)S(1)}, u32[]{:S(2)}, u32[]{:S(2)}) collective-permute-start(bf16[96,2048]{1,0:T(8,128)(2,1)S(1)} %collective-permute-done.10.rest_1_), channel_id=1, source_target_pairs={{0,4},{1,5},{4,8},{5,9},{6,2},{7,3},{8,12},{9,13},{10,6},{11,7},{1... | collective-permute-start | bytes 1179656 | tf_op jit(solution)/shard_map/ppermute | solution.py:27
  47.7 0.0 collective-permute-done.11.rest_5_
  47.7 0.0 collective-permute-done.12.rest_6_
  47.8 0.0 collective-permute-done.13.rest_7_
  47.8 7.4 %filter_columns.2.rest_8_ = bf16[2,2,96,8192]{3,2,1,0:T(8,128)(2,1)} custom-call(bf16[2,192,512]{2,1,0:T(8,128)(2,1)S(1)} %get-tuple-element.25.pair_source, bf16[2,2,80,256]{3,2,1,0:T(8,128)(2,1)S(1)} %collective-permute-done.4.core_ref, bf16[2,2,80,256]{3,2,1,0:T(8,128)(2,1)S(1)} %collective-permute-done.5.chip_ref, bf16[96,8192]{1,0:T(8,128)(2,1)} %own_ref.3, ...), custom_call_target="tpu_custom_call" | custom-call | tf_op jit(solution)/shard_map/filter_columns/pallas_call | solution.py:375
  55.1 0.0 collective-permute-done.7.rest_0_.rest_2_
  55.2 0.4 collective-permute-start.15
  55.6 0.1 collective-permute-start.16
  55.7 2.6 %collective-permute-done.14.rest_3_ = bf16[96,2048]{1,0:T(8,128)(2,1)S(1)} collective-permute-done((bf16[96,2048]{1,0:T(8,128)(2,1)S(1)}, bf16[96,2048]{1,0:T(8,128)(2,1)S(1)}, u32[]{:S(2)}, u32[]{:S(2)}) %collective-permute-start.14) | collective-permute-done | bytes 393248 | tf_op jit(solution)/shard_map/ppermute | solution.py:27
  58.4 0.8 %collective-permute-start.17 = (bf16[96,2048]{1,0:T(8,128)(2,1)S(1)}, bf16[96,2048]{1,0:T(8,128)(2,1)S(1)}, u32[]{:S(2)}, u32[]{:S(2)}) collective-permute-start(bf16[96,2048]{1,0:T(8,128)(2,1)S(1)} %collective-permute-done.14.rest_3_), channel_id=1, source_target_pairs={{0,1},{1,0},{2,3},{3,2},{4,5},{5,4},{6,7},{7,6},{8,9},{9,8},{10,11... | collective-permute-start | bytes 1179656 | tf_op jit(solution)/shard_map/ppermute | solution.py:27
  59.2 0.0 collective-permute-done.16.rest_5_
  59.2 1.3 %collective-permute-done.17.rest_7_ = bf16[96,2048]{1,0:T(8,128)(2,1)S(1)} collective-permute-done((bf16[96,2048]{1,0:T(8,128)(2,1)S(1)}, bf16[96,2048]{1,0:T(8,128)(2,1)S(1)}, u32[]{:S(2)}, u32[]{:S(2)}) %collective-permute-start.17) | collective-permute-done | bytes 393248 | tf_op jit(solution)/shard_map/ppermute | solution.py:27
  60.6 0.0 collective-permute-done.15.rest_4_.rest_6_
  60.6 7.3 %filter_columns.3 = bf16[2,2,96,8192]{3,2,1,0:T(8,128)(2,1)} custom-call(bf16[2,192,512]{2,1,0:T(8,128)(2,1)S(1)} %get-tuple-element.25.pair_source, bf16[2,2,80,256]{3,2,1,0:T(8,128)(2,1)S(1)} %collective-permute-done.4.core_ref, bf16[2,2,80,256]{3,2,1,0:T(8,128)(2,1)S(1)} %collective-permute-done.5.chip_ref, ...), custom_call_target="tpu_custom_call", output_to_operand_aliasing={{}: (13, {})} | custom-call | tf_op jit(solution)/shard_map/filter_columns/pallas_call | solution.py:375
Async XLA Ops:
  0.0 22.5 %collective-permute-start.2 = (bf16[96,8192]{1,0:T(8,128)(2,1)}, bf16[96,8192]{1,0:T(8,128)(2,1)}, u32[]{:S(2)}, u32[]{:S(2)}) collective-permute-start(bf16[96,8192]{1,0:T(8,128)(2,1)} %own_ref.3), channel_id=1, source_target_pairs={{0,1},{1,0},{2,3},{3,2},{4,5},{5,4},{6,7},{7,6},{8,9},{9,8},{10,11... | collective-permute-start | bytes 4718600 | tf_op jit(solution)/shard_map/ppermute | solution.py:27
  1.7 10.8 %collective-permute-start = (bf16[96,2048]{1,0:T(8,128)(2,1)S(1)}, bf16[96,2048]{1,0:T(8,128)(2,1)S(1)}, u32[]{:S(2)}, u32[]{:S(2)}) collective-permute-start(bf16[96,2048]{1,0:T(8,128)(2,1)S(1)} %constant_dynamic-slice_fusion), channel_id=1, source_target_pairs={{0,2},{1,3},{2,0},{3,1},{4,6},{5,7},{6,4},{7,5},{8,10},{9,11},{10,... | collective-permute-start | bytes 1179656 | tf_op jit(solution)/shard_map/ppermute | solution.py:27
  2.0 14.9 %copy-start = (s32[32,12,1]{0,2,1:T(1,128)S(1)}, s32[32,12,1]{0,2,1:T(1,128)}, u32[]{:S(2)}) copy-start(s32[32,12,1]{0,2,1:T(1,128)} %param.7) | copy-start | bytes 4612
  2.0 14.9 %copy-start.1 = (s32[32,12]{0,1:T(8,128)S(1)}, s32[32,12]{0,1:T(8,128)}, u32[]{:S(2)}) copy-start(s32[32,12]{0,1:T(8,128)} %param.8) | copy-start | bytes 4612
  2.0 14.9 %copy-start.2 = (s32[32,3]{0,1:T(4,128)S(1)}, s32[32,3]{0,1:T(4,128)}, u32[]{:S(2)}) copy-start(s32[32,3]{0,1:T(4,128)} %param.9) | copy-start | bytes 1156
  2.0 14.9 %copy-start.3 = (f32[2,3]{1,0:T(2,128)S(1)}, f32[2,3]{1,0:T(2,128)}, u32[]{:S(2)}) copy-start(f32[2,3]{1,0:T(2,128)} %refs_0_.1) | copy-start | bytes 76
  4.7 17.7 %all-to-all-start = ((bf16[32,48,128]{2,1,0:T(8,128)(2,1)}), bf16[32,48,128]{2,1,0:T(8,128)(2,1)S(1)}, u32[]{:S(2)}, u32[]{:S(2)}) async-start(bf16[32,48,128]{2,1,0:T(8,128)(2,1)} %pack_tiles.1), calls=%async_computation | async-start | bytes 786432 | tf_op jit(solution)/shard_map/all_to_all | solution.py:412
  12.5 10.0 %collective-permute-start.1 = (bf16[96,2048]{1,0:T(8,128)(2,1)S(1)}, bf16[96,2048]{1,0:T(8,128)(2,1)S(1)}, u32[]{:S(2)}, u32[]{:S(2)}) collective-permute-start(bf16[96,2048]{1,0:T(8,128)(2,1)S(1)} %collective-permute-done.rest_0_), channel_id=1, source_target_pairs={{0,1},{1,0},{2,3},{3,2},{4,5},{5,4},{6,7},{7,6},{8,9},{9,8},{10,11... | collective-permute-start | bytes 1179656 | tf_op jit(solution)/shard_map/ppermute | solution.py:27
  14.8 12.1 %collective-permute-start.8 = (bf16[96,2048]{1,0:T(8,128)(2,1)S(1)}, bf16[96,2048]{1,0:T(8,128)(2,1)S(1)}, u32[]{:S(2)}, u32[]{:S(2)}) collective-permute-start(bf16[96,2048]{1,0:T(8,128)(2,1)S(1)} %get-tuple-element.37), channel_id=1, source_target_pairs={{0,2},{1,3},{2,0},{3,1},{4,6},{5,7},{6,4},{7,5},{8,10},{9,11},{10,... | collective-permute-start | bytes 1179656 | tf_op jit(solution)/shard_map/ppermute | solution.py:27
  14.9 15.0 %collective-permute-start.6 = (bf16[96,2048]{1,0:T(8,128)(2,1)S(1)}, bf16[96,2048]{1,0:T(8,128)(2,1)S(1)}, u32[]{:S(2)}, u32[]{:S(2)}) collective-permute-start(bf16[96,2048]{1,0:T(8,128)(2,1)S(1)} %collective-permute-done.rest_0_), channel_id=1, source_target_pairs={{0,4},{1,5},{4,8},{5,9},{6,2},{7,3},{8,12},{9,13},{10,6},{11,7},{1... | collective-permute-start | bytes 1179656 | tf_op jit(solution)/shard_map/ppermute | solution.py:27
  23.2 11.1 %collective-permute-start.3 = (bf16[32,48,128]{2,1,0:T(8,128)(2,1)S(1)}, bf16[32,48,128]{2,1,0:T(8,128)(2,1)S(1)}, u32[]{:S(2)}, u32[]{:S(2)}) collective-permute-start(bf16[32,48,128]{2,1,0:T(8,128)(2,1)S(1)} %all-to-all-done.tiles_ref), channel_id=1, source_target_pairs={{0,16},{1,17},{2,18},{3,19},{4,20},{5,21},{6,22},{7,23},{8,24},{9,... | collective-permute-start | bytes 1179656 | tf_op jit(solution)/shard_map/ppermute | solution.py:27
  29.9 15.3 %collective-permute-start.10 = (bf16[96,2048]{1,0:T(8,128)(2,1)S(1)}, bf16[96,2048]{1,0:T(8,128)(2,1)S(1)}, u32[]{:S(2)}, u32[]{:S(2)}) collective-permute-start(bf16[96,2048]{1,0:T(8,128)(2,1)S(1)} %get-tuple-element.30), channel_id=1, source_target_pairs={{0,2},{1,3},{2,0},{3,1},{4,6},{5,7},{6,4},{7,5},{8,10},{9,11},{10,... | collective-permute-start | bytes 1179656 | tf_op jit(solution)/shard_map/ppermute | solution.py:27
  30.0 15.3 %collective-permute-start.9 = (bf16[96,2048]{1,0:T(8,128)(2,1)S(1)}, bf16[96,2048]{1,0:T(8,128)(2,1)S(1)}, u32[]{:S(2)}, u32[]{:S(2)}) collective-permute-start(bf16[96,2048]{1,0:T(8,128)(2,1)S(1)} %collective-permute-done.8.rest_1_), channel_id=1, source_target_pairs={{0,4},{1,5},{4,8},{5,9},{6,2},{7,3},{8,12},{9,13},{10,6},{11,7},{1... | collective-permute-start | bytes 1179656 | tf_op jit(solution)/shard_map/ppermute | solution.py:27
  35.0 20.1 %collective-permute-start.7 = (bf16[192,2048]{1,0:T(8,128)(2,1)S(1)}, bf16[192,2048]{1,0:T(8,128)(2,1)S(1)}, u32[]{:S(2)}, u32[]{:S(2)}) collective-permute-start(bf16[192,2048]{1,0:T(8,128)(2,1)S(1)} %pad_maximum_fusion), channel_id=1, source_target_pairs={{0,16},{1,17},{2,18},{3,19},{4,20},{5,21},{6,22},{7,23},{8,24},{9,... | collective-permute-start | bytes 2359304 | tf_op jit(solution)/shard_map/ppermute | solution.py:27
  36.3 7.6 %collective-permute-start.5 = (bf16[2,2,80,256]{3,2,1,0:T(8,128)(2,1)S(1)}, bf16[2,2,80,256]{3,2,1,0:T(8,128)(2,1)S(1)}, u32[]{:S(2)}, u32[]{:S(2)}) collective-permute-start(bf16[2,2,80,256]{3,2,1,0:T(8,128)(2,1)S(1)} %get-tuple-element.27), channel_id=1, source_target_pairs={{1,2},{2,1},{3,4},{4,3},{5,6},{6,5},{7,8},{8,7},{9,10},{10,9},{11,... | collective-permute-start | bytes 491528 | tf_op jit(solution)/shard_map/ppermute | solution.py:27
  39.0 6.3 %collective-permute-start.4 = (bf16[2,2,80,256]{3,2,1,0:T(8,128)(2,1)S(1)}, bf16[2,2,80,256]{3,2,1,0:T(8,128)(2,1)S(1)}, u32[]{:S(2)}, u32[]{:S(2)}) collective-permute-start(bf16[2,2,80,256]{3,2,1,0:T(8,128)(2,1)S(1)} %get-tuple-element.26), channel_id=1, source_target_pairs={{0,1},{1,0},{2,3},{3,2},{4,5},{5,4},{6,7},{7,6},{8,9},{9,8},{10,11... | collective-permute-start | bytes 491528 | tf_op jit(solution)/shard_map/ppermute | solution.py:27
  43.9 3.8 %collective-permute-start.11 = (bf16[96,2048]{1,0:T(8,128)(2,1)S(1)}, bf16[96,2048]{1,0:T(8,128)(2,1)S(1)}, u32[]{:S(2)}, u32[]{:S(2)}) collective-permute-start(bf16[96,2048]{1,0:T(8,128)(2,1)S(1)} %collective-permute-done.8.rest_1_), channel_id=1, source_target_pairs={{0,1},{1,0},{2,3},{3,2},{4,5},{5,4},{6,7},{7,6},{8,9},{9,8},{10,11... | collective-permute-start | bytes 1179656 | tf_op jit(solution)/shard_map/ppermute | solution.py:27
  45.3 2.5 %collective-permute-start.12 = (bf16[96,2048]{1,0:T(8,128)(2,1)S(1)}, bf16[96,2048]{1,0:T(8,128)(2,1)S(1)}, u32[]{:S(2)}, u32[]{:S(2)}) collective-permute-start(bf16[96,2048]{1,0:T(8,128)(2,1)S(1)} %collective-permute-done.6.rest_2_), channel_id=1, source_target_pairs={{0,1},{1,0},{2,3},{3,2},{4,5},{5,4},{6,7},{7,6},{8,9},{9,8},{10,11... | collective-permute-start | bytes 1179656 | tf_op jit(solution)/shard_map/ppermute | solution.py:27
  45.3 2.5 %collective-permute-start.13 = (bf16[96,2048]{1,0:T(8,128)(2,1)S(1)}, bf16[96,2048]{1,0:T(8,128)(2,1)S(1)}, u32[]{:S(2)}, u32[]{:S(2)}) collective-permute-start(bf16[96,2048]{1,0:T(8,128)(2,1)S(1)} %collective-permute-done.9.rest_3_), channel_id=1, source_target_pairs={{0,1},{1,0},{2,3},{3,2},{4,5},{5,4},{6,7},{7,6},{8,9},{9,8},{10,11... | collective-permute-start | bytes 1179656 | tf_op jit(solution)/shard_map/ppermute | solution.py:27
  45.8 12.6 %collective-permute-start.14 = (bf16[96,2048]{1,0:T(8,128)(2,1)S(1)}, bf16[96,2048]{1,0:T(8,128)(2,1)S(1)}, u32[]{:S(2)}, u32[]{:S(2)}) collective-permute-start(bf16[96,2048]{1,0:T(8,128)(2,1)S(1)} %collective-permute-done.10.rest_1_), channel_id=1, source_target_pairs={{0,4},{1,5},{4,8},{5,9},{6,2},{7,3},{8,12},{9,13},{10,6},{11,7},{1... | collective-permute-start | bytes 1179656 | tf_op jit(solution)/shard_map/ppermute | solution.py:27
  55.2 5.4 %collective-permute-start.15 = (bf16[192,2048]{1,0:T(8,128)(2,1)S(1)}, bf16[192,2048]{1,0:T(8,128)(2,1)S(1)}, u32[]{:S(2)}, u32[]{:S(2)}) collective-permute-start(bf16[192,2048]{1,0:T(8,128)(2,1)S(1)} %collective-permute-done.7.rest_0_.rest_2_), channel_id=1, source_target_pairs={{0,1},{1,0},{2,3},{3,2},{4,5},{5,4},{6,7},{7,6},{8,9},{9,8},{10,11... | collective-permute-start | bytes 2359304 | tf_op jit(solution)/shard_map/ppermute | solution.py:27
  55.6 3.6 %collective-permute-start.16 = (bf16[96,2048]{1,0:T(8,128)(2,1)S(1)}, bf16[96,2048]{1,0:T(8,128)(2,1)S(1)}, u32[]{:S(2)}, u32[]{:S(2)}) collective-permute-start(bf16[96,2048]{1,0:T(8,128)(2,1)S(1)} %collective-permute-done.10.rest_1_), channel_id=1, source_target_pairs={{0,1},{1,0},{2,3},{3,2},{4,5},{5,4},{6,7},{7,6},{8,9},{9,8},{10,11... | collective-permute-start | bytes 1179656 | tf_op jit(solution)/shard_map/ppermute | solution.py:27
  58.4 2.2 %collective-permute-start.17 = (bf16[96,2048]{1,0:T(8,128)(2,1)S(1)}, bf16[96,2048]{1,0:T(8,128)(2,1)S(1)}, u32[]{:S(2)}, u32[]{:S(2)}) collective-permute-start(bf16[96,2048]{1,0:T(8,128)(2,1)S(1)} %collective-permute-done.14.rest_3_), channel_id=1, source_target_pairs={{0,1},{1,0},{2,3},{3,2},{4,5},{5,4},{6,7},{7,6},{8,9},{9,8},{10,11... | collective-permute-start | bytes 1179656 | tf_op jit(solution)/shard_map/ppermute | solution.py:27

commit v6 on v5

--- a/solution.py
+++ b/solution.py
@@ -51,13 +51,14 @@
     return lax.optimization_barrier((value,) + sooner)[0]
 
 
-def pack_kernel(dest_ref, tiles_ref, packed_ref, placed, source):
-    slots = packed_ref.shape[0]
+def pack_kernel(dest_ref, tiles_ref, packed_ref, placed, source, held, arrived):
+    slots, part, _ = packed_ref.shape
     tile_count = dest_ref.shape[0]
     step_count = tiles_ref.shape[0] // tile_count
     first_vector = lax.axis_index("orb") * step_count
-    part = packed_ref.shape[1]
     rows = pl.ds(pl.multiple_of(lax.axis_index("kgrp") * part, part), part)
+    fetch = pltpu.make_async_copy(tiles_ref.at[:, rows, :], held, arrived)
+    fetch.start()
 
     def clear(slot, carry):
         source[slot] = 0
@@ -74,26 +75,33 @@
         source[dest * CAP + rank] = tile
         return carry
 
-    def fill(slot, carry):
-        packed_ref[slot] = tiles_ref[source[slot], rows, :]
-        return carry
-
     lax.fori_loop(0, slots, clear, 0, unroll=4)
     lax.fori_loop(0, slots // CAP, forget, 0, unroll=4)
     lax.fori_loop(0, step_count * tile_count, place, 0)
-    lax.fori_loop(0, slots, fill, 0, unroll=2)
+    fetch.wait()
+
+    def fill(slot, carry):
+        packed_ref[slot] = held[source[slot]]
+        return carry
+
+    lax.fori_loop(0, slots, fill, 0, unroll=4)
 
 
 def pack_tiles(tiles, dest, owners):
     slots = owners * CAP
-    rows, width = tiles.shape[1:]
-    vmem = pl.BlockSpec(memory_space=pltpu.VMEM)
+    tile_total, rows, width = tiles.shape
+    part = rows // lax.axis_size("kgrp")
     return pl.pallas_call(
         pack_kernel,
-        out_shape=jax.ShapeDtypeStruct((slots, rows // lax.axis_size("kgrp"), width), tiles.dtype),
-        in_specs=[pl.BlockSpec(memory_space=pltpu.SMEM), vmem],
-        out_specs=vmem,
-        scratch_shapes=[pltpu.SMEM((owners,), jnp.int32), pltpu.SMEM((slots,), jnp.int32)],
+        out_shape=jax.ShapeDtypeStruct((slots, part, width), tiles.dtype),
+        in_specs=[pl.BlockSpec(memory_space=pltpu.SMEM), pl.BlockSpec(memory_space=pltpu.HBM)],
+        out_specs=pl.BlockSpec(memory_space=pltpu.VMEM),
+        scratch_shapes=[
+            pltpu.SMEM((owners,), jnp.int32),
+            pltpu.SMEM((slots,), jnp.int32),
+            pltpu.VMEM((tile_total, part, width), tiles.dtype),
+            pltpu.SemaphoreType.DMA,
+        ],
         compiler_params=pltpu.CompilerParams(vmem_limit_bytes=MUCH),
         cost_estimate=pl.CostEstimate(flops=0, bytes_accessed=0, transcendentals=0),
         name="pack_tiles",

time: 68.9 us -> 69 us (level)
  no operation moved by 1% of the time
where the time goes in v6:
time: 69 us; the launch traced here: 67.9 us
  starting transfers between devices  23.1 us (33%)
  waiting for transfers between devices  22.7 us (33%)
  Pallas kernels  19.7 us (29%)
  local copies, waits for them, and re-layouts  2.2 us (3%)
    ppermute x18, waiting for transfers between devices, routed(): return lax.ppermute(value, ('kgrp', 'orb'), pairs)  18.3 us
    ppermute x18, starting transfers between devices, routed(): return lax.ppermute(value, ('kgrp', 'orb'), pairs)  16.9 us
    pallas_call x2, Pallas kernels, filter_columns(): pl.pallas_call(functools.partial(filter_kernel, places), out_shape=jax.Sh...  14.7 us
    all_to_all x1, starting transfers between devices, local(): lax.all_to_all(outgoing, 'orb', split_axis=0, concat_axis=0, tiled=True)  6.2 us
    all_to_all x1, waiting for transfers between devices, local(): lax.all_to_all(outgoing, 'orb', split_axis=0, concat_axis=0, tiled=True)  4.39 us
    pallas_call x1, Pallas kernels, pack_tiles(): pl.pallas_call(pack_kernel, out_shape=jax.ShapeDtypeStruct((slots, part,...  2.67 us
  transfers between devices with their start and end apart: 19, of which 8 were waited for; matrix products, arithmetic and copies ran while one was open for 3% of the time, Pallas kernels for 18%

profile of v6, /device:TPU:11, one launch (start us, length us, event | category | flops | bytes accessed | tf_op | source)
XLA Modules:
  0.0 67.9 jit_solution(17464146242704027366)
XLA Ops:
  0.0 0.7 collective-permute-start.2
  0.7 1.0 %constant_dynamic-slice_fusion = bf16[96,2048]{1,0:T(8,128)(2,1)S(1)} fusion(bf16[96,8192]{1,0:T(8,128)(2,1)} %own_ref.3, s32[]{:T(128)S(6)} %select_n.3), kind=kLoop, calls=%fused_computation.1 | loop fusion | bytes 786436 | tf_op jit(solution)/shard_map/dynamic_slice | solution.py:422
  1.7 0.3 collective-permute-start
  2.0 0.0 copy-start
  2.0 0.0 copy-start.1
  2.0 0.0 copy-start.2
  2.0 0.0 copy-start.3
  2.0 2.7 %pack_tiles.1 = bf16[32,48,128]{2,1,0:T(8,128)(2,1)} custom-call(s32[12,1,32]{2,1,0:T(1,128)} %bitcast.4, bf16[24,96,128]{2,1,0:T(8,128)(2,1)} %bitcast.8), custom_call_target="tpu_custom_call" | custom-call | tf_op jit(solution)/shard_map/pack_tiles/pallas_call | solution.py:94
  4.7 6.2 %all-to-all-start = ((bf16[32,48,128]{2,1,0:T(8,128)(2,1)}), bf16[32,48,128]{2,1,0:T(8,128)(2,1)S(1)}, u32[]{:S(2)}, u32[]{:S(2)}) async-start(bf16[32,48,128]{2,1,0:T(8,128)(2,1)} %pack_tiles.1), calls=%async_computation | async-start | bytes 786432 | tf_op jit(solution)/shard_map/all_to_all | solution.py:420
  10.9 1.6 %collective-permute-done.rest_0_ = bf16[96,2048]{1,0:T(8,128)(2,1)S(1)} collective-permute-done((bf16[96,2048]{1,0:T(8,128)(2,1)S(1)}, bf16[96,2048]{1,0:T(8,128)(2,1)S(1)}, u32[]{:S(2)}, u32[]{:S(2)}) %collective-permute-start) | collective-permute-done | bytes 393248 | tf_op jit(solution)/shard_map/ppermute | solution.py:27
  12.5 1.4 %collective-permute-start.1 = (bf16[96,2048]{1,0:T(8,128)(2,1)S(1)}, bf16[96,2048]{1,0:T(8,128)(2,1)S(1)}, u32[]{:S(2)}, u32[]{:S(2)}) collective-permute-start(bf16[96,2048]{1,0:T(8,128)(2,1)S(1)} %collective-permute-done.rest_0_), channel_id=1, source_target_pairs={{0,1},{1,0},{2,3},{3,2},{4,5},{5,4},{6,7},{7,6},{8,9},{9,8},{10,11... | collective-permute-start | bytes 1179656 | tf_op jit(solution)/shard_map/ppermute | solution.py:27
  13.9 1.2 %fusion = (bf16[96,2048]{1,0:T(8,128)(2,1)S(1)}, bf16[96,2048]{1,0:T(8,128)(2,1)S(1)}) fusion(bf16[96,8192]{1,0:T(8,128)(2,1)} %own_ref.3), kind=kLoop, calls=%fused_computation.2 | loop fusion | bytes 1572864 | tf_op jit(solution)/shard_map/slice | solution.py:424
  15.1 0.1 collective-permute-start.8
  15.2 1.9 %collective-permute-start.6 = (bf16[96,2048]{1,0:T(8,128)(2,1)S(1)}, bf16[96,2048]{1,0:T(8,128)(2,1)S(1)}, u32[]{:S(2)}, u32[]{:S(2)}) collective-permute-start(bf16[96,2048]{1,0:T(8,128)(2,1)S(1)} %collective-permute-done.rest_0_), channel_id=1, source_target_pairs={{0,4},{1,5},{4,8},{5,9},{6,2},{7,3},{8,12},{9,13},{10,6},{11,7},{1... | collective-permute-start | bytes 1179656 | tf_op jit(solution)/shard_map/ppermute | solution.py:27
  17.1 0.0 copy-done
  17.1 0.0 copy-done.1
  17.1 0.0 copy-done.2
  17.1 0.0 copy-done.3
  17.2 0.9 %receive_weights.1.weight_ref = f32[16,2048]{1,0:T(8,128)S(1)} custom-call(f32[2,3]{1,0:T(2,128)S(1)} %copy-done.3, s32[3,32]{1,0:T(4,128)S(1)} %bitcast.7, s32[12,1,32]{2,1,0:T(1,128)S(1)} %bitcast.5, s32[12,32]{1,0:T(8,128)S(1)} %bitcast.6), custom_call_target="tpu_custom_call" | custom-call | tf_op jit(solution)/shard_map/receive_weights/pallas_call | solution.py:164
  18.1 4.4 %all-to-all-done.tiles_ref = bf16[32,48,128]{2,1,0:T(8,128)(2,1)S(1)} async-done(((bf16[32,48,128]{2,1,0:T(8,128)(2,1)}), bf16[32,48,128]{2,1,0:T(8,128)(2,1)S(1)}, u32[]{:S(2)}, u32[]{:S(2)}) %all-to-all-start) | async-done | bytes 393248 | tf_op jit(solution)/shard_map/all_to_all | solution.py:420
  22.4 0.0 collective-permute-done.1.rest_4_
  22.4 0.0 collective-permute-done.2.sibling_ref
  22.5 0.7 %begin_bands.1.begun_ref = bf16[2,192,512]{2,1,0:T(8,128)(2,1)S(1)} custom-call(f32[16,2048]{1,0:T(8,128)S(1)} %receive_weights.1.weight_ref, bf16[32,48,128]{2,1,0:T(8,128)(2,1)S(1)} %all-to-all-done.tiles_ref), custom_call_target="tpu_custom_call" | custom-call | tf_op jit(solution)/shard_map/begin_bands/pallas_call | solution.py:235
  23.2 1.3 %collective-permute-start.3 = (bf16[32,48,128]{2,1,0:T(8,128)(2,1)S(1)}, bf16[32,48,128]{2,1,0:T(8,128)(2,1)S(1)}, u32[]{:S(2)}, u32[]{:S(2)}) collective-permute-start(bf16[32,48,128]{2,1,0:T(8,128)(2,1)S(1)} %all-to-all-done.tiles_ref), channel_id=1, source_target_pairs={{0,16},{1,17},{2,18},{3,19},{4,20},{5,21},{6,22},{7,23},{8,24},{9,... | collective-permute-start | bytes 1179656 | tf_op jit(solution)/shard_map/ppermute | solution.py:27
  24.5 2.8 %collective-permute-done.8.rest_1_ = bf16[96,2048]{1,0:T(8,128)(2,1)S(1)} collective-permute-done((bf16[96,2048]{1,0:T(8,128)(2,1)S(1)}, bf16[96,2048]{1,0:T(8,128)(2,1)S(1)}, u32[]{:S(2)}, u32[]{:S(2)}) %collective-permute-start.8) | collective-permute-done | bytes 393248 | tf_op jit(solution)/shard_map/ppermute | solution.py:27
  27.2 2.7 %collective-permute-done.6.rest_2_ = bf16[96,2048]{1,0:T(8,128)(2,1)S(1)} collective-permute-done((bf16[96,2048]{1,0:T(8,128)(2,1)S(1)}, bf16[96,2048]{1,0:T(8,128)(2,1)S(1)}, u32[]{:S(2)}, u32[]{:S(2)}) %collective-permute-start.6) | collective-permute-done | bytes 393248 | tf_op jit(solution)/shard_map/ppermute | solution.py:27
  29.9 0.0 collective-permute-start.10
  29.9 0.1 pad_maximum_fusion
  30.0 1.9 %collective-permute-start.9 = (bf16[96,2048]{1,0:T(8,128)(2,1)S(1)}, bf16[96,2048]{1,0:T(8,128)(2,1)S(1)}, u32[]{:S(2)}, u32[]{:S(2)}) collective-permute-start(bf16[96,2048]{1,0:T(8,128)(2,1)S(1)} %collective-permute-done.8.rest_1_), channel_id=1, source_target_pairs={{0,4},{1,5},{4,8},{5,9},{6,2},{7,3},{8,12},{9,13},{10,6},{11,7},{1... | collective-permute-start | bytes 1179656 | tf_op jit(solution)/shard_map/ppermute | solution.py:27
  31.9 2.3 %collective-permute-done.3.tiles_ref = bf16[32,48,128]{2,1,0:T(8,128)(2,1)S(1)} collective-permute-done((bf16[32,48,128]{2,1,0:T(8,128)(2,1)S(1)}, bf16[32,48,128]{2,1,0:T(8,128)(2,1)S(1)}, u32[]{:S(2)}, u32[]{:S(2)}) %collective-permute-start.3) | collective-permute-done | bytes 393248 | tf_op jit(solution)/shard_map/ppermute | solution.py:27
  34.3 0.7 %make_bands.1 = (bf16[2,192,512]{2,1,0:T(8,128)(2,1)S(1)}, bf16[2,2,80,256]{3,2,1,0:T(8,128)(2,1)S(1)}, bf16[2,2,80,256]{3,2,1,0:T(8,128)(2,1)S(1)}) custom-call(f32[16,2048]{1,0:T(8,128)S(1)} %receive_weights.1.weight_ref, bf16[32,48,128]{2,1,0:T(8,128)(2,1)S(1)} %collective-permute-done.3.tiles_ref, bf16[2,192,512]{2,1,0:T(8,128)(2,1)S(1)} %begin_bands.1.begun_ref), custom_call_target="tpu_custom_call" | custom-call | tf_op jit(solution)/shard_map/make_bands/pallas_call | solution.py:250
  35.0 1.3 %collective-permute-start.7 = (bf16[192,2048]{1,0:T(8,128)(2,1)S(1)}, bf16[192,2048]{1,0:T(8,128)(2,1)S(1)}, u32[]{:S(2)}, u32[]{:S(2)}) collective-permute-start(bf16[192,2048]{1,0:T(8,128)(2,1)S(1)} %pad_maximum_fusion), channel_id=1, source_target_pairs={{0,16},{1,17},{2,18},{3,19},{4,20},{5,21},{6,22},{7,23},{8,24},{9,... | collective-permute-start | bytes 2359304 | tf_op jit(solution)/shard_map/ppermute | solution.py:27
  36.3 2.7 %collective-permute-start.5 = (bf16[2,2,80,256]{3,2,1,0:T(8,128)(2,1)S(1)}, bf16[2,2,80,256]{3,2,1,0:T(8,128)(2,1)S(1)}, u32[]{:S(2)}, u32[]{:S(2)}) collective-permute-start(bf16[2,2,80,256]{3,2,1,0:T(8,128)(2,1)S(1)} %get-tuple-element.27), channel_id=1, source_target_pairs={{1,2},{2,1},{3,4},{4,3},{5,6},{6,5},{7,8},{8,7},{9,10},{10,9},{11,... | collective-permute-start | bytes 491528 | tf_op jit(solution)/shard_map/ppermute | solution.py:27
  39.0 0.1 collective-permute-start.4
  39.0 4.9 %collective-permute-done.5.chip_ref = bf16[2,2,80,256]{3,2,1,0:T(8,128)(2,1)S(1)} collective-permute-done((bf16[2,2,80,256]{3,2,1,0:T(8,128)(2,1)S(1)}, bf16[2,2,80,256]{3,2,1,0:T(8,128)(2,1)S(1)}, u32[]{:S(2)}, u32[]{:S(2)}) %collective-permute-start.5) | collective-permute-done | bytes 163872 | tf_op jit(solution)/shard_map/ppermute | solution.py:27
  43.9 1.3 %collective-permute-start.11 = (bf16[96,2048]{1,0:T(8,128)(2,1)S(1)}, bf16[96,2048]{1,0:T(8,128)(2,1)S(1)}, u32[]{:S(2)}, u32[]{:S(2)}) collective-permute-start(bf16[96,2048]{1,0:T(8,128)(2,1)S(1)} %collective-permute-done.8.rest_1_), channel_id=1, source_target_pairs={{0,1},{1,0},{2,3},{3,2},{4,5},{5,4},{6,7},{7,6},{8,9},{9,8},{10,11... | collective-permute-start | bytes 1179656 | tf_op jit(solution)/shard_map/ppermute | solution.py:27
  45.3 0.0 collective-permute-done.10.rest_1_
  45.3 0.0 collective-permute-start.12
  45.3 0.0 collective-permute-done.4.core_ref
  45.3 0.0 collective-permute-done.9.rest_3_
  45.3 0.5 collective-permute-start.13
  45.8 1.9 %collective-permute-start.14 = (bf16[96,2048]{1,0:T(8,128)(2,1)S(1)}, bf16[96,2048]{1,0:T(8,128)(2,1)S(1)}, u32[]{:S(2)}, u32[]{:S(2)}) collective-permute-start(bf16[96,2048]{1,0:T(8,128)(2,1)S(1)} %collective-permute-done.10.rest_1_), channel_id=1, source_target_pairs={{0,4},{1,5},{4,8},{5,9},{6,2},{7,3},{8,12},{9,13},{10,6},{11,7},{1... | collective-permute-start | bytes 1179656 | tf_op jit(solution)/shard_map/ppermute | solution.py:27
  47.7 0.0 collective-permute-done.11.rest_5_
  47.7 0.0 collective-permute-done.12.rest_6_
  47.7 0.0 collective-permute-done.13.rest_7_
  47.8 7.4 %filter_columns.2.rest_8_ = bf16[2,2,96,8192]{3,2,1,0:T(8,128)(2,1)} custom-call(bf16[2,192,512]{2,1,0:T(8,128)(2,1)S(1)} %get-tuple-element.25.pair_source, bf16[2,2,80,256]{3,2,1,0:T(8,128)(2,1)S(1)} %collective-permute-done.4.core_ref, bf16[2,2,80,256]{3,2,1,0:T(8,128)(2,1)S(1)} %collective-permute-done.5.chip_ref, bf16[96,8192]{1,0:T(8,128)(2,1)} %own_ref.3, ...), custom_call_target="tpu_custom_call" | custom-call | tf_op jit(solution)/shard_map/filter_columns/pallas_call | solution.py:383
  55.1 0.0 collective-permute-done.7.rest_0_.rest_2_
  55.1 0.4 collective-permute-start.15
  55.6 0.1 collective-permute-start.16
  55.7 2.6 %collective-permute-done.14.rest_3_ = bf16[96,2048]{1,0:T(8,128)(2,1)S(1)} collective-permute-done((bf16[96,2048]{1,0:T(8,128)(2,1)S(1)}, bf16[96,2048]{1,0:T(8,128)(2,1)S(1)}, u32[]{:S(2)}, u32[]{:S(2)}) %collective-permute-start.14) | collective-permute-done | bytes 393248 | tf_op jit(solution)/shard_map/ppermute | solution.py:27
  58.4 0.8 %collective-permute-start.17 = (bf16[96,2048]{1,0:T(8,128)(2,1)S(1)}, bf16[96,2048]{1,0:T(8,128)(2,1)S(1)}, u32[]{:S(2)}, u32[]{:S(2)}) collective-permute-start(bf16[96,2048]{1,0:T(8,128)(2,1)S(1)} %collective-permute-done.14.rest_3_), channel_id=1, source_target_pairs={{0,1},{1,0},{2,3},{3,2},{4,5},{5,4},{6,7},{7,6},{8,9},{9,8},{10,11... | collective-permute-start | bytes 1179656 | tf_op jit(solution)/shard_map/ppermute | solution.py:27
  59.2 0.0 collective-permute-done.16.rest_5_
  59.2 1.3 %collective-permute-done.17.rest_7_ = bf16[96,2048]{1,0:T(8,128)(2,1)S(1)} collective-permute-done((bf16[96,2048]{1,0:T(8,128)(2,1)S(1)}, bf16[96,2048]{1,0:T(8,128)(2,1)S(1)}, u32[]{:S(2)}, u32[]{:S(2)}) %collective-permute-start.17) | collective-permute-done | bytes 393248 | tf_op jit(solution)/shard_map/ppermute | solution.py:27
  60.6 0.0 collective-permute-done.15.rest_4_.rest_6_
  60.6 7.3 %filter_columns.3 = bf16[2,2,96,8192]{3,2,1,0:T(8,128)(2,1)} custom-call(bf16[2,192,512]{2,1,0:T(8,128)(2,1)S(1)} %get-tuple-element.25.pair_source, bf16[2,2,80,256]{3,2,1,0:T(8,128)(2,1)S(1)} %collective-permute-done.4.core_ref, bf16[2,2,80,256]{3,2,1,0:T(8,128)(2,1)S(1)} %collective-permute-done.5.chip_ref, ...), custom_call_target="tpu_custom_call", output_to_operand_aliasing={{}: (13, {})} | custom-call | tf_op jit(solution)/shard_map/filter_columns/pallas_call | solution.py:383
Async XLA Ops:
  0.0 22.5 %collective-permute-start.2 = (bf16[96,8192]{1,0:T(8,128)(2,1)}, bf16[96,8192]{1,0:T(8,128)(2,1)}, u32[]{:S(2)}, u32[]{:S(2)}) collective-permute-start(bf16[96,8192]{1,0:T(8,128)(2,1)} %own_ref.3), channel_id=1, source_target_pairs={{0,1},{1,0},{2,3},{3,2},{4,5},{5,4},{6,7},{7,6},{8,9},{9,8},{10,11... | collective-permute-start | bytes 4718600 | tf_op jit(solution)/shard_map/ppermute | solution.py:27
  1.7 10.8 %collective-permute-start = (bf16[96,2048]{1,0:T(8,128)(2,1)S(1)}, bf16[96,2048]{1,0:T(8,128)(2,1)S(1)}, u32[]{:S(2)}, u32[]{:S(2)}) collective-permute-start(bf16[96,2048]{1,0:T(8,128)(2,1)S(1)} %constant_dynamic-slice_fusion), channel_id=1, source_target_pairs={{0,2},{1,3},{2,0},{3,1},{4,6},{5,7},{6,4},{7,5},{8,10},{9,11},{10,... | collective-permute-start | bytes 1179656 | tf_op jit(solution)/shard_map/ppermute | solution.py:27
  2.0 15.1 %copy-start = (s32[32,12,1]{0,2,1:T(1,128)S(1)}, s32[32,12,1]{0,2,1:T(1,128)}, u32[]{:S(2)}) copy-start(s32[32,12,1]{0,2,1:T(1,128)} %param.7) | copy-start | bytes 4612
  2.0 15.1 %copy-start.1 = (s32[32,12]{0,1:T(8,128)S(1)}, s32[32,12]{0,1:T(8,128)}, u32[]{:S(2)}) copy-start(s32[32,12]{0,1:T(8,128)} %param.8) | copy-start | bytes 4612
  2.0 15.1 %copy-start.2 = (s32[32,3]{0,1:T(4,128)S(1)}, s32[32,3]{0,1:T(4,128)}, u32[]{:S(2)}) copy-start(s32[32,3]{0,1:T(4,128)} %param.9) | copy-start | bytes 1156
  2.0 15.1 %copy-start.3 = (f32[2,3]{1,0:T(2,128)S(1)}, f32[2,3]{1,0:T(2,128)}, u32[]{:S(2)}) copy-start(f32[2,3]{1,0:T(2,128)} %refs_0_.1) | copy-start | bytes 76
  4.7 17.7 %all-to-all-start = ((bf16[32,48,128]{2,1,0:T(8,128)(2,1)}), bf16[32,48,128]{2,1,0:T(8,128)(2,1)S(1)}, u32[]{:S(2)}, u32[]{:S(2)}) async-start(bf16[32,48,128]{2,1,0:T(8,128)(2,1)} %pack_tiles.1), calls=%async_computation | async-start | bytes 786432 | tf_op jit(solution)/shard_map/all_to_all | solution.py:420
  12.5 9.9 %collective-permute-start.1 = (bf16[96,2048]{1,0:T(8,128)(2,1)S(1)}, bf16[96,2048]{1,0:T(8,128)(2,1)S(1)}, u32[]{:S(2)}, u32[]{:S(2)}) collective-permute-start(bf16[96,2048]{1,0:T(8,128)(2,1)S(1)} %collective-permute-done.rest_0_), channel_id=1, source_target_pairs={{0,1},{1,0},{2,3},{3,2},{4,5},{5,4},{6,7},{7,6},{8,9},{9,8},{10,11... | collective-permute-start | bytes 1179656 | tf_op jit(solution)/shard_map/ppermute | solution.py:27
  15.1 12.1 %collective-permute-start.8 = (bf16[96,2048]{1,0:T(8,128)(2,1)S(1)}, bf16[96,2048]{1,0:T(8,128)(2,1)S(1)}, u32[]{:S(2)}, u32[]{:S(2)}) collective-permute-start(bf16[96,2048]{1,0:T(8,128)(2,1)S(1)} %get-tuple-element.37), channel_id=1, source_target_pairs={{0,2},{1,3},{2,0},{3,1},{4,6},{5,7},{6,4},{7,5},{8,10},{9,11},{10,... | collective-permute-start | bytes 1179656 | tf_op jit(solution)/shard_map/ppermute | solution.py:27
  15.2 14.7 %collective-permute-start.6 = (bf16[96,2048]{1,0:T(8,128)(2,1)S(1)}, bf16[96,2048]{1,0:T(8,128)(2,1)S(1)}, u32[]{:S(2)}, u32[]{:S(2)}) collective-permute-start(bf16[96,2048]{1,0:T(8,128)(2,1)S(1)} %collective-permute-done.rest_0_), channel_id=1, source_target_pairs={{0,4},{1,5},{4,8},{5,9},{6,2},{7,3},{8,12},{9,13},{10,6},{11,7},{1... | collective-permute-start | bytes 1179656 | tf_op jit(solution)/shard_map/ppermute | solution.py:27
  23.2 11.1 %collective-permute-start.3 = (bf16[32,48,128]{2,1,0:T(8,128)(2,1)S(1)}, bf16[32,48,128]{2,1,0:T(8,128)(2,1)S(1)}, u32[]{:S(2)}, u32[]{:S(2)}) collective-permute-start(bf16[32,48,128]{2,1,0:T(8,128)(2,1)S(1)} %all-to-all-done.tiles_ref), channel_id=1, source_target_pairs={{0,16},{1,17},{2,18},{3,19},{4,20},{5,21},{6,22},{7,23},{8,24},{9,... | collective-permute-start | bytes 1179656 | tf_op jit(solution)/shard_map/ppermute | solution.py:27
  29.9 15.3 %collective-permute-start.10 = (bf16[96,2048]{1,0:T(8,128)(2,1)S(1)}, bf16[96,2048]{1,0:T(8,128)(2,1)S(1)}, u32[]{:S(2)}, u32[]{:S(2)}) collective-permute-start(bf16[96,2048]{1,0:T(8,128)(2,1)S(1)} %get-tuple-element.30), channel_id=1, source_target_pairs={{0,2},{1,3},{2,0},{3,1},{4,6},{5,7},{6,4},{7,5},{8,10},{9,11},{10,... | collective-permute-start | bytes 1179656 | tf_op jit(solution)/shard_map/ppermute | solution.py:27
  30.0 15.3 %collective-permute-start.9 = (bf16[96,2048]{1,0:T(8,128)(2,1)S(1)}, bf16[96,2048]{1,0:T(8,128)(2,1)S(1)}, u32[]{:S(2)}, u32[]{:S(2)}) collective-permute-start(bf16[96,2048]{1,0:T(8,128)(2,1)S(1)} %collective-permute-done.8.rest_1_), channel_id=1, source_target_pairs={{0,4},{1,5},{4,8},{5,9},{6,2},{7,3},{8,12},{9,13},{10,6},{11,7},{1... | collective-permute-start | bytes 1179656 | tf_op jit(solution)/shard_map/ppermute | solution.py:27
  35.0 20.1 %collective-permute-start.7 = (bf16[192,2048]{1,0:T(8,128)(2,1)S(1)}, bf16[192,2048]{1,0:T(8,128)(2,1)S(1)}, u32[]{:S(2)}, u32[]{:S(2)}) collective-permute-start(bf16[192,2048]{1,0:T(8,128)(2,1)S(1)} %pad_maximum_fusion), channel_id=1, source_target_pairs={{0,16},{1,17},{2,18},{3,19},{4,20},{5,21},{6,22},{7,23},{8,24},{9,... | collective-permute-start | bytes 2359304 | tf_op jit(solution)/shard_map/ppermute | solution.py:27
  36.3 7.6 %collective-permute-start.5 = (bf16[2,2,80,256]{3,2,1,0:T(8,128)(2,1)S(1)}, bf16[2,2,80,256]{3,2,1,0:T(8,128)(2,1)S(1)}, u32[]{:S(2)}, u32[]{:S(2)}) collective-permute-start(bf16[2,2,80,256]{3,2,1,0:T(8,128)(2,1)S(1)} %get-tuple-element.27), channel_id=1, source_target_pairs={{1,2},{2,1},{3,4},{4,3},{5,6},{6,5},{7,8},{8,7},{9,10},{10,9},{11,... | collective-permute-start | bytes 491528 | tf_op jit(solution)/shard_map/ppermute | solution.py:27
  39.0 6.3 %collective-permute-start.4 = (bf16[2,2,80,256]{3,2,1,0:T(8,128)(2,1)S(1)}, bf16[2,2,80,256]{3,2,1,0:T(8,128)(2,1)S(1)}, u32[]{:S(2)}, u32[]{:S(2)}) collective-permute-start(bf16[2,2,80,256]{3,2,1,0:T(8,128)(2,1)S(1)} %get-tuple-element.26), channel_id=1, source_target_pairs={{0,1},{1,0},{2,3},{3,2},{4,5},{5,4},{6,7},{7,6},{8,9},{9,8},{10,11... | collective-permute-start | bytes 491528 | tf_op jit(solution)/shard_map/ppermute | solution.py:27
  43.9 3.8 %collective-permute-start.11 = (bf16[96,2048]{1,0:T(8,128)(2,1)S(1)}, bf16[96,2048]{1,0:T(8,128)(2,1)S(1)}, u32[]{:S(2)}, u32[]{:S(2)}) collective-permute-start(bf16[96,2048]{1,0:T(8,128)(2,1)S(1)} %collective-permute-done.8.rest_1_), channel_id=1, source_target_pairs={{0,1},{1,0},{2,3},{3,2},{4,5},{5,4},{6,7},{7,6},{8,9},{9,8},{10,11... | collective-permute-start | bytes 1179656 | tf_op jit(solution)/shard_map/ppermute | solution.py:27
  45.3 2.5 %collective-permute-start.12 = (bf16[96,2048]{1,0:T(8,128)(2,1)S(1)}, bf16[96,2048]{1,0:T(8,128)(2,1)S(1)}, u32[]{:S(2)}, u32[]{:S(2)}) collective-permute-start(bf16[96,2048]{1,0:T(8,128)(2,1)S(1)} %collective-permute-done.6.rest_2_), channel_id=1, source_target_pairs={{0,1},{1,0},{2,3},{3,2},{4,5},{5,4},{6,7},{7,6},{8,9},{9,8},{10,11... | collective-permute-start | bytes 1179656 | tf_op jit(solution)/shard_map/ppermute | solution.py:27
  45.3 2.5 %collective-permute-start.13 = (bf16[96,2048]{1,0:T(8,128)(2,1)S(1)}, bf16[96,2048]{1,0:T(8,128)(2,1)S(1)}, u32[]{:S(2)}, u32[]{:S(2)}) collective-permute-start(bf16[96,2048]{1,0:T(8,128)(2,1)S(1)} %collective-permute-done.9.rest_3_), channel_id=1, source_target_pairs={{0,1},{1,0},{2,3},{3,2},{4,5},{5,4},{6,7},{7,6},{8,9},{9,8},{10,11... | collective-permute-start | bytes 1179656 | tf_op jit(solution)/shard_map/ppermute | solution.py:27
  45.8 12.6 %collective-permute-start.14 = (bf16[96,2048]{1,0:T(8,128)(2,1)S(1)}, bf16[96,2048]{1,0:T(8,128)(2,1)S(1)}, u32[]{:S(2)}, u32[]{:S(2)}) collective-permute-start(bf16[96,2048]{1,0:T(8,128)(2,1)S(1)} %collective-permute-done.10.rest_1_), channel_id=1, source_target_pairs={{0,4},{1,5},{4,8},{5,9},{6,2},{7,3},{8,12},{9,13},{10,6},{11,7},{1... | collective-permute-start | bytes 1179656 | tf_op jit(solution)/shard_map/ppermute | solution.py:27
  55.1 5.4 %collective-permute-start.15 = (bf16[192,2048]{1,0:T(8,128)(2,1)S(1)}, bf16[192,2048]{1,0:T(8,128)(2,1)S(1)}, u32[]{:S(2)}, u32[]{:S(2)}) collective-permute-start(bf16[192,2048]{1,0:T(8,128)(2,1)S(1)} %collective-permute-done.7.rest_0_.rest_2_), channel_id=1, source_target_pairs={{0,1},{1,0},{2,3},{3,2},{4,5},{5,4},{6,7},{7,6},{8,9},{9,8},{10,11... | collective-permute-start | bytes 2359304 | tf_op jit(solution)/shard_map/ppermute | solution.py:27
  55.6 3.6 %collective-permute-start.16 = (bf16[96,2048]{1,0:T(8,128)(2,1)S(1)}, bf16[96,2048]{1,0:T(8,128)(2,1)S(1)}, u32[]{:S(2)}, u32[]{:S(2)}) collective-permute-start(bf16[96,2048]{1,0:T(8,128)(2,1)S(1)} %collective-permute-done.10.rest_1_), channel_id=1, source_target_pairs={{0,1},{1,0},{2,3},{3,2},{4,5},{5,4},{6,7},{7,6},{8,9},{9,8},{10,11... | collective-permute-start | bytes 1179656 | tf_op jit(solution)/shard_map/ppermute | solution.py:27
  58.4 2.2 %collective-permute-start.17 = (bf16[96,2048]{1,0:T(8,128)(2,1)S(1)}, bf16[96,2048]{1,0:T(8,128)(2,1)S(1)}, u32[]{:S(2)}, u32[]{:S(2)}) collective-permute-start(bf16[96,2048]{1,0:T(8,128)(2,1)S(1)} %collective-permute-done.14.rest_3_), channel_id=1, source_target_pairs={{0,1},{1,0},{2,3},{3,2},{4,5},{5,4},{6,7},{7,6},{8,9},{9,8},{10,11... | collective-permute-start | bytes 1179656 | tf_op jit(solution)/shard_map/ppermute | solution.py:27

commit v7 on v5

--- a/solution.py
+++ b/solution.py
@@ -290,7 +290,7 @@
                     low = places[index][2]
                     near = near_chip_refs[index].at[0:rows, piece]
                     if odd_chip == odd_core:
-                        near = near_onward_refs[index].at[low : low + rows, piece]
+                        near = near_onward_refs[index].at[0:rows, piece]
                     before, beyond = (chip_refs[index], 0), (onward_refs[index], low)
                     if odd_chip == 0:
                         before, beyond = beyond, before
@@ -448,7 +448,8 @@
         None,
     )
     other, fourth_beyond = after(other, result), after(fourth_beyond, result)
-    near_other = to_sibling(other)
+    owner = lax.axis_index("orb")
+    near_other = to_sibling(jnp.where((owner >> 1) & 1 == owner & 1, other[:row_count], other[row_count:]))
     return filtered(
         [(piece, -piece, row_count), (3 * piece, 0, 0)],
         [

time: 68.9 us -> 69.7 us (1.012)
  other arithmetic: 0.05 us -> 0.99 us
  starting transfers between devices: 22.8 us -> 23.6 us
    ppermute x18, waiting for transfers between devices: 18.3 us -> 17.1 us  [routed(): return lax.ppermute(value, ('kgrp', 'orb'), pairs)]
    concatenate x1, other arithmetic: 0.05 us -> 0.95 us  [local(): jnp.concatenate([shared, shared_beyond], axis=0)]
    all_to_all x1, waiting for transfers between devices: 4.62 us -> 5.36 us  [local(): lax.all_to_all(outgoing, 'orb', split_axis=0, concat_axis=0, tiled=True)]
  transfers between devices with their start and end apart: 19 -> 19, of which waited for: 8 -> 9; matrix products, arithmetic and copies ran while one was open for 3% -> 4% of each run, Pallas kernels for 18% -> 18%
where the time goes in v7:
time: 69.7 us; the launch traced here: 68.9 us
  starting transfers between devices  23.6 us (34%)
  waiting for transfers between devices  22.5 us (32%)
  Pallas kernels  19.7 us (28%)
  local copies, waits for them, and re-layouts  1.85 us (3%)
  other arithmetic  0.99 us (1%)
    ppermute x18, starting transfers between devices, routed(): return lax.ppermute(value, ('kgrp', 'orb'), pairs)  17.3 us
    ppermute x18, waiting for transfers between devices, routed(): return lax.ppermute(value, ('kgrp', 'orb'), pairs)  17.1 us
    pallas_call x2, Pallas kernels, filter_columns(): pl.pallas_call(functools.partial(filter_kernel, places), out_shape=jax.Sh...  14.7 us
    all_to_all x1, starting transfers between devices, local(): lax.all_to_all(outgoing, 'orb', split_axis=0, concat_axis=0, tiled=True)  6.34 us
    all_to_all x1, waiting for transfers between devices, local(): lax.all_to_all(outgoing, 'orb', split_axis=0, concat_axis=0, tiled=True)  5.36 us
    pallas_call x1, Pallas kernels, pack_tiles(): pl.pallas_call(pack_kernel, out_shape=jax.ShapeDtypeStruct((slots, rows /...  2.71 us
  transfers between devices with their start and end apart: 19, of which 9 were waited for; matrix products, arithmetic and copies ran while one was open for 4% of the time, Pallas kernels for 18%

profile of v7, /device:TPU:11, one launch (start us, length us, event | category | flops | bytes accessed | tf_op | source)
XLA Modules:
  0.0 68.9 jit_solution(4739066754192936755)
XLA Ops:
  0.0 0.0 copy-start
  0.0 0.7 collective-permute-start.2
  0.7 1.0 %constant_dynamic-slice_fusion = bf16[96,2048]{1,0:T(8,128)(2,1)S(1)} fusion(bf16[96,8192]{1,0:T(8,128)(2,1)} %own_ref.3, s32[]{:T(128)S(6)} %select_n.11), kind=kLoop, calls=%fused_computation.2 | loop fusion | bytes 786436 | tf_op jit(solution)/shard_map/dynamic_slice | solution.py:414
  1.7 0.3 collective-permute-start
  2.0 0.0 copy-start.2
  2.0 0.0 copy-start.3
  2.0 0.0 copy-start.4
  2.0 0.0 copy-start.5
  2.0 2.7 %pack_tiles.1 = bf16[32,48,128]{2,1,0:T(8,128)(2,1)} custom-call(s32[12,1,32]{2,1,0:T(1,128)} %bitcast.4, bf16[24,96,128]{2,1,0:T(8,128)(2,1)} %bitcast.8), custom_call_target="tpu_custom_call" | custom-call | tf_op jit(solution)/shard_map/pack_tiles/pallas_call | solution.py:91
  4.7 6.3 %all-to-all-start = ((bf16[32,48,128]{2,1,0:T(8,128)(2,1)}), bf16[32,48,128]{2,1,0:T(8,128)(2,1)S(1)}, u32[]{:S(2)}, u32[]{:S(2)}) async-start(bf16[32,48,128]{2,1,0:T(8,128)(2,1)} %pack_tiles.1), calls=%async_computation | async-start | bytes 786432 | tf_op jit(solution)/shard_map/all_to_all | solution.py:412
  11.1 1.3 %collective-permute-done.rest_0_ = bf16[96,2048]{1,0:T(8,128)(2,1)S(1)} collective-permute-done((bf16[96,2048]{1,0:T(8,128)(2,1)S(1)}, bf16[96,2048]{1,0:T(8,128)(2,1)S(1)}, u32[]{:S(2)}, u32[]{:S(2)}) %collective-permute-start) | collective-permute-done | bytes 393248 | tf_op jit(solution)/shard_map/ppermute | solution.py:27
  12.3 1.0 %collective-permute-start.1 = (bf16[96,2048]{1,0:T(8,128)(2,1)S(1)}, bf16[96,2048]{1,0:T(8,128)(2,1)S(1)}, u32[]{:S(2)}, u32[]{:S(2)}) collective-permute-start(bf16[96,2048]{1,0:T(8,128)(2,1)S(1)} %collective-permute-done.rest_0_), channel_id=1, source_target_pairs={{0,1},{1,0},{2,3},{3,2},{4,5},{5,4},{6,7},{7,6},{8,9},{9,8},{10,11... | collective-permute-start | bytes 1179656 | tf_op jit(solution)/shard_map/ppermute | solution.py:27
  13.3 0.0 copy-done
  13.3 0.8 %fusion = (bf16[96,2048]{1,0:T(8,128)(2,1)S(1)}, bf16[96,2048]{1,0:T(8,128)(2,1)}) fusion(bf16[96,8192]{1,0:T(8,128)(2,1)S(1)} %copy-done), kind=kLoop, calls=%fused_computation.3 | loop fusion | bytes 1572864 | tf_op jit(solution)/shard_map/slice | solution.py:416
  14.1 0.2 collective-permute-start.8
  14.4 1.9 %collective-permute-start.6 = (bf16[96,2048]{1,0:T(8,128)(2,1)S(1)}, bf16[96,2048]{1,0:T(8,128)(2,1)S(1)}, u32[]{:S(2)}, u32[]{:S(2)}) collective-permute-start(bf16[96,2048]{1,0:T(8,128)(2,1)S(1)} %collective-permute-done.rest_0_), channel_id=1, source_target_pairs={{0,4},{1,5},{4,8},{5,9},{6,2},{7,3},{8,12},{9,13},{10,6},{11,7},{1... | collective-permute-start | bytes 1179656 | tf_op jit(solution)/shard_map/ppermute | solution.py:27
  16.3 0.0 copy-done.2
  16.3 0.0 copy-done.3
  16.3 0.0 copy-done.4
  16.3 0.0 copy-done.5
  16.3 0.9 %receive_weights.1.weight_ref = f32[16,2048]{1,0:T(8,128)S(1)} custom-call(f32[2,3]{1,0:T(2,128)S(1)} %copy-done.5, s32[3,32]{1,0:T(4,128)S(1)} %bitcast.7, s32[12,1,32]{2,1,0:T(1,128)S(1)} %bitcast.5, s32[12,32]{1,0:T(8,128)S(1)} %bitcast.6), custom_call_target="tpu_custom_call" | custom-call | tf_op jit(solution)/shard_map/receive_weights/pallas_call | solution.py:156
  17.2 5.4 %all-to-all-done.tiles_ref = bf16[32,48,128]{2,1,0:T(8,128)(2,1)S(1)} async-done(((bf16[32,48,128]{2,1,0:T(8,128)(2,1)}), bf16[32,48,128]{2,1,0:T(8,128)(2,1)S(1)}, u32[]{:S(2)}, u32[]{:S(2)}) %all-to-all-start) | async-done | bytes 393248 | tf_op jit(solution)/shard_map/all_to_all | solution.py:412
  22.6 0.0 collective-permute-done.1.rest_4_
  22.6 0.0 collective-permute-done.2.sibling_ref
  22.6 0.7 %begin_bands.1.begun_ref = bf16[2,192,512]{2,1,0:T(8,128)(2,1)S(1)} custom-call(f32[16,2048]{1,0:T(8,128)S(1)} %receive_weights.1.weight_ref, bf16[32,48,128]{2,1,0:T(8,128)(2,1)S(1)} %all-to-all-done.tiles_ref), custom_call_target="tpu_custom_call" | custom-call | tf_op jit(solution)/shard_map/begin_bands/pallas_call | solution.py:227
  23.3 1.3 %collective-permute-start.3 = (bf16[32,48,128]{2,1,0:T(8,128)(2,1)S(1)}, bf16[32,48,128]{2,1,0:T(8,128)(2,1)S(1)}, u32[]{:S(2)}, u32[]{:S(2)}) collective-permute-start(bf16[32,48,128]{2,1,0:T(8,128)(2,1)S(1)} %all-to-all-done.tiles_ref), channel_id=1, source_target_pairs={{0,16},{1,17},{2,18},{3,19},{4,20},{5,21},{6,22},{7,23},{8,24},{9,... | collective-permute-start | bytes 1179656 | tf_op jit(solution)/shard_map/ppermute | solution.py:27
  24.6 2.5 %collective-permute-done.8.rest_1_ = bf16[96,2048]{1,0:T(8,128)(2,1)S(1)} collective-permute-done((bf16[96,2048]{1,0:T(8,128)(2,1)S(1)}, bf16[96,2048]{1,0:T(8,128)(2,1)S(1)}, u32[]{:S(2)}, u32[]{:S(2)}) %collective-permute-start.8) | collective-permute-done | bytes 393248 | tf_op jit(solution)/shard_map/ppermute | solution.py:27
  27.1 2.1 %collective-permute-start.9 = (bf16[96,2048]{1,0:T(8,128)(2,1)S(1)}, bf16[96,2048]{1,0:T(8,128)(2,1)S(1)}, u32[]{:S(2)}, u32[]{:S(2)}) collective-permute-start(bf16[96,2048]{1,0:T(8,128)(2,1)S(1)} %collective-permute-done.8.rest_1_), channel_id=1, source_target_pairs={{0,4},{1,5},{4,8},{5,9},{6,2},{7,3},{8,12},{9,13},{10,6},{11,7},{1... | collective-permute-start | bytes 1179656 | tf_op jit(solution)/shard_map/ppermute | solution.py:27
  29.2 0.9 %collective-permute-done.6.rest_2_ = bf16[96,2048]{1,0:T(8,128)(2,1)S(1)} collective-permute-done((bf16[96,2048]{1,0:T(8,128)(2,1)S(1)}, bf16[96,2048]{1,0:T(8,128)(2,1)S(1)}, u32[]{:S(2)}, u32[]{:S(2)}) %collective-permute-start.6) | collective-permute-done | bytes 393248 | tf_op jit(solution)/shard_map/ppermute | solution.py:27
  30.1 0.8 %collective-permute-start.10 = (bf16[96,2048]{1,0:T(8,128)(2,1)}, bf16[96,2048]{1,0:T(8,128)(2,1)}, u32[]{:S(2)}, u32[]{:S(2)}) collective-permute-start(bf16[96,2048]{1,0:T(8,128)(2,1)} %get-tuple-element.30), channel_id=1, source_target_pairs={{0,2},{1,3},{2,0},{3,1},{4,6},{5,7},{6,4},{7,5},{8,10},{9,11},{10,... | collective-permute-start | bytes 1179656 | tf_op jit(solution)/shard_map/ppermute | solution.py:27
  30.9 0.9 %pad_maximum_fusion = bf16[192,2048]{1,0:T(8,128)(2,1)} fusion(bf16[96,2048]{1,0:T(8,128)(2,1)S(1)} %collective-permute-done.6.rest_2_, bf16[96,2048]{1,0:T(8,128)(2,1)S(1)} %collective-permute-done.rest_0_), kind=kLoop, calls=%fused_computation | loop fusion | flops 1572864 | bytes 1572864 | tf_op jit(solution)/shard_map/concatenate | solution.py:430
  31.9 2.6 %collective-permute-done.3.tiles_ref = bf16[32,48,128]{2,1,0:T(8,128)(2,1)S(1)} collective-permute-done((bf16[32,48,128]{2,1,0:T(8,128)(2,1)S(1)}, bf16[32,48,128]{2,1,0:T(8,128)(2,1)S(1)}, u32[]{:S(2)}, u32[]{:S(2)}) %collective-permute-start.3) | collective-permute-done | bytes 393248 | tf_op jit(solution)/shard_map/ppermute | solution.py:27
  34.5 0.7 %make_bands.1 = (bf16[2,192,512]{2,1,0:T(8,128)(2,1)S(1)}, bf16[2,2,80,256]{3,2,1,0:T(8,128)(2,1)S(1)}, bf16[2,2,80,256]{3,2,1,0:T(8,128)(2,1)S(1)}) custom-call(f32[16,2048]{1,0:T(8,128)S(1)} %receive_weights.1.weight_ref, bf16[32,48,128]{2,1,0:T(8,128)(2,1)S(1)} %collective-permute-done.3.tiles_ref, bf16[2,192,512]{2,1,0:T(8,128)(2,1)S(1)} %begin_bands.1.begun_ref), custom_call_target="tpu_custom_call" | custom-call | tf_op jit(solution)/shard_map/make_bands/pallas_call | solution.py:242
  35.2 1.3 %collective-permute-start.7 = (bf16[192,2048]{1,0:T(8,128)(2,1)}, bf16[192,2048]{1,0:T(8,128)(2,1)S(1)}, u32[]{:S(2)}, u32[]{:S(2)}) collective-permute-start(bf16[192,2048]{1,0:T(8,128)(2,1)} %pad_maximum_fusion), channel_id=1, source_target_pairs={{0,16},{1,17},{2,18},{3,19},{4,20},{5,21},{6,22},{7,23},{8,24},{9,... | collective-permute-start | bytes 2359304 | tf_op jit(solution)/shard_map/ppermute | solution.py:27
  36.6 2.6 %collective-permute-start.5 = (bf16[2,2,80,256]{3,2,1,0:T(8,128)(2,1)S(1)}, bf16[2,2,80,256]{3,2,1,0:T(8,128)(2,1)S(1)}, u32[]{:S(2)}, u32[]{:S(2)}) collective-permute-start(bf16[2,2,80,256]{3,2,1,0:T(8,128)(2,1)S(1)} %get-tuple-element.27), channel_id=1, source_target_pairs={{1,2},{2,1},{3,4},{4,3},{5,6},{6,5},{7,8},{8,7},{9,10},{10,9},{11,... | collective-permute-start | bytes 491528 | tf_op jit(solution)/shard_map/ppermute | solution.py:27
  39.1 0.1 collective-permute-start.4
  39.2 5.0 %collective-permute-done.5.chip_ref = bf16[2,2,80,256]{3,2,1,0:T(8,128)(2,1)S(1)} collective-permute-done((bf16[2,2,80,256]{3,2,1,0:T(8,128)(2,1)S(1)}, bf16[2,2,80,256]{3,2,1,0:T(8,128)(2,1)S(1)}, u32[]{:S(2)}, u32[]{:S(2)}) %collective-permute-start.5) | collective-permute-done | bytes 163872 | tf_op jit(solution)/shard_map/ppermute | solution.py:27
  44.2 1.2 %collective-permute-start.11 = (bf16[96,2048]{1,0:T(8,128)(2,1)S(1)}, bf16[96,2048]{1,0:T(8,128)(2,1)}, u32[]{:S(2)}, u32[]{:S(2)}) collective-permute-start(bf16[96,2048]{1,0:T(8,128)(2,1)S(1)} %collective-permute-done.8.rest_1_), channel_id=1, source_target_pairs={{0,1},{1,0},{2,3},{3,2},{4,5},{5,4},{6,7},{7,6},{8,9},{9,8},{10,11... | collective-permute-start | bytes 1179656 | tf_op jit(solution)/shard_map/ppermute | solution.py:27
  45.4 0.0 collective-permute-done.10.rest_1_
  45.4 0.0 collective-permute-start.12
  45.4 0.0 collective-permute-done.4.core_ref
  45.4 0.0 collective-permute-done.9.rest_3_
  45.4 0.5 collective-permute-start.13
  45.9 1.9 %collective-permute-start.14 = (bf16[96,2048]{1,0:T(8,128)(2,1)}, bf16[96,2048]{1,0:T(8,128)(2,1)}, u32[]{:S(2)}, u32[]{:S(2)}) collective-permute-start(bf16[96,2048]{1,0:T(8,128)(2,1)} %collective-permute-done.10.rest_1_), channel_id=1, source_target_pairs={{0,4},{1,5},{4,8},{5,9},{6,2},{7,3},{8,12},{9,13},{10,6},{11,7},{1... | collective-permute-start | bytes 1179656 | tf_op jit(solution)/shard_map/ppermute | solution.py:27
  47.9 0.0 collective-permute-done.11.rest_5_
  47.9 0.4 collective-permute-start.16
  48.3 0.0 collective-permute-done.12.rest_6_
  48.3 0.0 collective-permute-done.13.rest_7_
  48.3 0.0 copy-start.1
  48.3 7.5 %filter_columns.2.rest_8_ = bf16[2,2,96,8192]{3,2,1,0:T(8,128)(2,1)} custom-call(bf16[2,192,512]{2,1,0:T(8,128)(2,1)S(1)} %get-tuple-element.25.pair_source, bf16[2,2,80,256]{3,2,1,0:T(8,128)(2,1)S(1)} %collective-permute-done.4.core_ref, bf16[2,2,80,256]{3,2,1,0:T(8,128)(2,1)S(1)} %collective-permute-done.5.chip_ref, bf16[96,8192]{1,0:T(8,128)(2,1)} %own_ref.3, ...), custom_call_target="tpu_custom_call" | custom-call | tf_op jit(solution)/shard_map/filter_columns/pallas_call | solution.py:375
  55.8 3.0 %collective-permute-done.14.rest_3_ = bf16[96,2048]{1,0:T(8,128)(2,1)} collective-permute-done((bf16[96,2048]{1,0:T(8,128)(2,1)}, bf16[96,2048]{1,0:T(8,128)(2,1)}, u32[]{:S(2)}, u32[]{:S(2)}) %collective-permute-start.14) | collective-permute-done | bytes 393248 | tf_op jit(solution)/shard_map/ppermute | solution.py:27
  58.8 0.8 %collective-permute-start.17 = (bf16[96,2048]{1,0:T(8,128)(2,1)}, bf16[96,2048]{1,0:T(8,128)(2,1)S(1)}, u32[]{:S(2)}, u32[]{:S(2)}) collective-permute-start(bf16[96,2048]{1,0:T(8,128)(2,1)} %collective-permute-done.14.rest_3_), channel_id=1, source_target_pairs={{0,1},{1,0},{2,3},{3,2},{4,5},{5,4},{6,7},{7,6},{8,9},{9,8},{10,11... | collective-permute-start | bytes 1179656 | tf_op jit(solution)/shard_map/ppermute | solution.py:27
  59.7 0.0 collective-permute-done.7.rest_0_.rest_2_
  59.7 0.1 collective-permute-start.15
  59.8 0.0 collective-permute-done.16.rest_5_
  59.8 1.4 %collective-permute-done.17.rest_7_ = bf16[96,2048]{1,0:T(8,128)(2,1)S(1)} collective-permute-done((bf16[96,2048]{1,0:T(8,128)(2,1)}, bf16[96,2048]{1,0:T(8,128)(2,1)S(1)}, u32[]{:S(2)}, u32[]{:S(2)}) %collective-permute-start.17) | collective-permute-done | bytes 393248 | tf_op jit(solution)/shard_map/ppermute | solution.py:27
  61.2 0.4 collective-permute-done.15.rest_4_.rest_6_
  61.6 0.0 copy-done.1
  61.6 7.3 %filter_columns.3 = bf16[2,2,96,8192]{3,2,1,0:T(8,128)(2,1)} custom-call(bf16[2,192,512]{2,1,0:T(8,128)(2,1)S(1)} %get-tuple-element.25.pair_source, bf16[2,2,80,256]{3,2,1,0:T(8,128)(2,1)S(1)} %collective-permute-done.4.core_ref, bf16[2,2,80,256]{3,2,1,0:T(8,128)(2,1)S(1)} %collective-permute-done.5.chip_ref, ...), custom_call_target="tpu_custom_call", output_to_operand_aliasing={{}: (13, {})} | custom-call | tf_op jit(solution)/shard_map/filter_columns/pallas_call | solution.py:375
  (1 shorter events, 0.0 us)
Async XLA Ops:
  0.0 13.3 %copy-start = (bf16[96,8192]{1,0:T(8,128)(2,1)S(1)}, bf16[96,8192]{1,0:T(8,128)(2,1)}, u32[]{:S(2)}) copy-start(bf16[96,8192]{1,0:T(8,128)(2,1)} %own_ref.3) | copy-start | bytes 4718596
  0.0 22.6 %collective-permute-start.2 = (bf16[96,8192]{1,0:T(8,128)(2,1)}, bf16[96,8192]{1,0:T(8,128)(2,1)}, u32[]{:S(2)}, u32[]{:S(2)}) collective-permute-start(bf16[96,8192]{1,0:T(8,128)(2,1)} %own_ref.3), channel_id=1, source_target_pairs={{0,1},{1,0},{2,3},{3,2},{4,5},{5,4},{6,7},{7,6},{8,9},{9,8},{10,11... | collective-permute-start | bytes 4718600 | tf_op jit(solution)/shard_map/ppermute | solution.py:27
  1.7 10.6 %collective-permute-start = (bf16[96,2048]{1,0:T(8,128)(2,1)S(1)}, bf16[96,2048]{1,0:T(8,128)(2,1)S(1)}, u32[]{:S(2)}, u32[]{:S(2)}) collective-permute-start(bf16[96,2048]{1,0:T(8,128)(2,1)S(1)} %constant_dynamic-slice_fusion), channel_id=1, source_target_pairs={{0,2},{1,3},{2,0},{3,1},{4,6},{5,7},{6,4},{7,5},{8,10},{9,11},{10,... | collective-permute-start | bytes 1179656 | tf_op jit(solution)/shard_map/ppermute | solution.py:27
  2.0 14.3 %copy-start.2 = (s32[32,12,1]{0,2,1:T(1,128)S(1)}, s32[32,12,1]{0,2,1:T(1,128)}, u32[]{:S(2)}) copy-start(s32[32,12,1]{0,2,1:T(1,128)} %param.7) | copy-start | bytes 4612
  2.0 14.3 %copy-start.3 = (s32[32,12]{0,1:T(8,128)S(1)}, s32[32,12]{0,1:T(8,128)}, u32[]{:S(2)}) copy-start(s32[32,12]{0,1:T(8,128)} %param.8) | copy-start | bytes 4612
  2.0 14.3 %copy-start.4 = (s32[32,3]{0,1:T(4,128)S(1)}, s32[32,3]{0,1:T(4,128)}, u32[]{:S(2)}) copy-start(s32[32,3]{0,1:T(4,128)} %param.9) | copy-start | bytes 1156
  2.0 14.3 %copy-start.5 = (f32[2,3]{1,0:T(2,128)S(1)}, f32[2,3]{1,0:T(2,128)}, u32[]{:S(2)}) copy-start(f32[2,3]{1,0:T(2,128)} %refs_0_.1) | copy-start | bytes 76
  4.7 17.9 %all-to-all-start = ((bf16[32,48,128]{2,1,0:T(8,128)(2,1)}), bf16[32,48,128]{2,1,0:T(8,128)(2,1)S(1)}, u32[]{:S(2)}, u32[]{:S(2)}) async-start(bf16[32,48,128]{2,1,0:T(8,128)(2,1)} %pack_tiles.1), calls=%async_computation | async-start | bytes 786432 | tf_op jit(solution)/shard_map/all_to_all | solution.py:412
  12.3 10.3 %collective-permute-start.1 = (bf16[96,2048]{1,0:T(8,128)(2,1)S(1)}, bf16[96,2048]{1,0:T(8,128)(2,1)S(1)}, u32[]{:S(2)}, u32[]{:S(2)}) collective-permute-start(bf16[96,2048]{1,0:T(8,128)(2,1)S(1)} %collective-permute-done.rest_0_), channel_id=1, source_target_pairs={{0,1},{1,0},{2,3},{3,2},{4,5},{5,4},{6,7},{7,6},{8,9},{9,8},{10,11... | collective-permute-start | bytes 1179656 | tf_op jit(solution)/shard_map/ppermute | solution.py:27
  14.1 13.0 %collective-permute-start.8 = (bf16[96,2048]{1,0:T(8,128)(2,1)S(1)}, bf16[96,2048]{1,0:T(8,128)(2,1)S(1)}, u32[]{:S(2)}, u32[]{:S(2)}) collective-permute-start(bf16[96,2048]{1,0:T(8,128)(2,1)S(1)} %get-tuple-element.37), channel_id=1, source_target_pairs={{0,2},{1,3},{2,0},{3,1},{4,6},{5,7},{6,4},{7,5},{8,10},{9,11},{10,... | collective-permute-start | bytes 1179656 | tf_op jit(solution)/shard_map/ppermute | solution.py:27
  14.4 15.7 %collective-permute-start.6 = (bf16[96,2048]{1,0:T(8,128)(2,1)S(1)}, bf16[96,2048]{1,0:T(8,128)(2,1)S(1)}, u32[]{:S(2)}, u32[]{:S(2)}) collective-permute-start(bf16[96,2048]{1,0:T(8,128)(2,1)S(1)} %collective-permute-done.rest_0_), channel_id=1, source_target_pairs={{0,4},{1,5},{4,8},{5,9},{6,2},{7,3},{8,12},{9,13},{10,6},{11,7},{1... | collective-permute-start | bytes 1179656 | tf_op jit(solution)/shard_map/ppermute | solution.py:27
  23.3 11.2 %collective-permute-start.3 = (bf16[32,48,128]{2,1,0:T(8,128)(2,1)S(1)}, bf16[32,48,128]{2,1,0:T(8,128)(2,1)S(1)}, u32[]{:S(2)}, u32[]{:S(2)}) collective-permute-start(bf16[32,48,128]{2,1,0:T(8,128)(2,1)S(1)} %all-to-all-done.tiles_ref), channel_id=1, source_target_pairs={{0,16},{1,17},{2,18},{3,19},{4,20},{5,21},{6,22},{7,23},{8,24},{9,... | collective-permute-start | bytes 1179656 | tf_op jit(solution)/shard_map/ppermute | solution.py:27
  27.1 18.3 %collective-permute-start.9 = (bf16[96,2048]{1,0:T(8,128)(2,1)S(1)}, bf16[96,2048]{1,0:T(8,128)(2,1)S(1)}, u32[]{:S(2)}, u32[]{:S(2)}) collective-permute-start(bf16[96,2048]{1,0:T(8,128)(2,1)S(1)} %collective-permute-done.8.rest_1_), channel_id=1, source_target_pairs={{0,4},{1,5},{4,8},{5,9},{6,2},{7,3},{8,12},{9,13},{10,6},{11,7},{1... | collective-permute-start | bytes 1179656 | tf_op jit(solution)/shard_map/ppermute | solution.py:27
  30.1 15.3 %collective-permute-start.10 = (bf16[96,2048]{1,0:T(8,128)(2,1)}, bf16[96,2048]{1,0:T(8,128)(2,1)}, u32[]{:S(2)}, u32[]{:S(2)}) collective-permute-start(bf16[96,2048]{1,0:T(8,128)(2,1)} %get-tuple-element.30), channel_id=1, source_target_pairs={{0,2},{1,3},{2,0},{3,1},{4,6},{5,7},{6,4},{7,5},{8,10},{9,11},{10,... | collective-permute-start | bytes 1179656 | tf_op jit(solution)/shard_map/ppermute | solution.py:27
  35.2 24.4 %collective-permute-start.7 = (bf16[192,2048]{1,0:T(8,128)(2,1)}, bf16[192,2048]{1,0:T(8,128)(2,1)S(1)}, u32[]{:S(2)}, u32[]{:S(2)}) collective-permute-start(bf16[192,2048]{1,0:T(8,128)(2,1)} %pad_maximum_fusion), channel_id=1, source_target_pairs={{0,16},{1,17},{2,18},{3,19},{4,20},{5,21},{6,22},{7,23},{8,24},{9,... | collective-permute-start | bytes 2359304 | tf_op jit(solution)/shard_map/ppermute | solution.py:27
  36.6 7.6 %collective-permute-start.5 = (bf16[2,2,80,256]{3,2,1,0:T(8,128)(2,1)S(1)}, bf16[2,2,80,256]{3,2,1,0:T(8,128)(2,1)S(1)}, u32[]{:S(2)}, u32[]{:S(2)}) collective-permute-start(bf16[2,2,80,256]{3,2,1,0:T(8,128)(2,1)S(1)} %get-tuple-element.27), channel_id=1, source_target_pairs={{1,2},{2,1},{3,4},{4,3},{5,6},{6,5},{7,8},{8,7},{9,10},{10,9},{11,... | collective-permute-start | bytes 491528 | tf_op jit(solution)/shard_map/ppermute | solution.py:27
  39.1 6.3 %collective-permute-start.4 = (bf16[2,2,80,256]{3,2,1,0:T(8,128)(2,1)S(1)}, bf16[2,2,80,256]{3,2,1,0:T(8,128)(2,1)S(1)}, u32[]{:S(2)}, u32[]{:S(2)}) collective-permute-start(bf16[2,2,80,256]{3,2,1,0:T(8,128)(2,1)S(1)} %get-tuple-element.26), channel_id=1, source_target_pairs={{0,1},{1,0},{2,3},{3,2},{4,5},{5,4},{6,7},{7,6},{8,9},{9,8},{10,11... | collective-permute-start | bytes 491528 | tf_op jit(solution)/shard_map/ppermute | solution.py:27
  44.2 3.7 %collective-permute-start.11 = (bf16[96,2048]{1,0:T(8,128)(2,1)S(1)}, bf16[96,2048]{1,0:T(8,128)(2,1)}, u32[]{:S(2)}, u32[]{:S(2)}) collective-permute-start(bf16[96,2048]{1,0:T(8,128)(2,1)S(1)} %collective-permute-done.8.rest_1_), channel_id=1, source_target_pairs={{0,1},{1,0},{2,3},{3,2},{4,5},{5,4},{6,7},{7,6},{8,9},{9,8},{10,11... | collective-permute-start | bytes 1179656 | tf_op jit(solution)/shard_map/ppermute | solution.py:27
  45.4 2.9 %collective-permute-start.12 = (bf16[96,2048]{1,0:T(8,128)(2,1)S(1)}, bf16[96,2048]{1,0:T(8,128)(2,1)}, u32[]{:S(2)}, u32[]{:S(2)}) collective-permute-start(bf16[96,2048]{1,0:T(8,128)(2,1)S(1)} %collective-permute-done.6.rest_2_), channel_id=1, source_target_pairs={{0,1},{1,0},{2,3},{3,2},{4,5},{5,4},{6,7},{7,6},{8,9},{9,8},{10,11... | collective-permute-start | bytes 1179656 | tf_op jit(solution)/shard_map/ppermute | solution.py:27
  45.4 2.9 %collective-permute-start.13 = (bf16[96,2048]{1,0:T(8,128)(2,1)S(1)}, bf16[96,2048]{1,0:T(8,128)(2,1)}, u32[]{:S(2)}, u32[]{:S(2)}) collective-permute-start(bf16[96,2048]{1,0:T(8,128)(2,1)S(1)} %collective-permute-done.9.rest_3_), channel_id=1, source_target_pairs={{0,1},{1,0},{2,3},{3,2},{4,5},{5,4},{6,7},{7,6},{8,9},{9,8},{10,11... | collective-permute-start | bytes 1179656 | tf_op jit(solution)/shard_map/ppermute | solution.py:27
  45.9 12.9 %collective-permute-start.14 = (bf16[96,2048]{1,0:T(8,128)(2,1)}, bf16[96,2048]{1,0:T(8,128)(2,1)}, u32[]{:S(2)}, u32[]{:S(2)}) collective-permute-start(bf16[96,2048]{1,0:T(8,128)(2,1)} %collective-permute-done.10.rest_1_), channel_id=1, source_target_pairs={{0,4},{1,5},{4,8},{5,9},{6,2},{7,3},{8,12},{9,13},{10,6},{11,7},{1... | collective-permute-start | bytes 1179656 | tf_op jit(solution)/shard_map/ppermute | solution.py:27
  47.9 11.9 %collective-permute-start.16 = (bf16[96,2048]{1,0:T(8,128)(2,1)}, bf16[96,2048]{1,0:T(8,128)(2,1)S(1)}, u32[]{:S(2)}, u32[]{:S(2)}) collective-permute-start(bf16[96,2048]{1,0:T(8,128)(2,1)} %collective-permute-done.10.rest_1_), channel_id=1, source_target_pairs={{0,1},{1,0},{2,3},{3,2},{4,5},{5,4},{6,7},{7,6},{8,9},{9,8},{10,11... | collective-permute-start | bytes 1179656 | tf_op jit(solution)/shard_map/ppermute | solution.py:27
  48.3 13.3 %copy-start.1 = (bf16[96,8192]{1,0:T(8,128)(2,1)S(1)}, bf16[96,8192]{1,0:T(8,128)(2,1)}, u32[]{:S(2)}) copy-start(bf16[96,8192]{1,0:T(8,128)(2,1)} %own_ref.3) | copy-start | bytes 4718596
  58.8 2.4 %collective-permute-start.17 = (bf16[96,2048]{1,0:T(8,128)(2,1)}, bf16[96,2048]{1,0:T(8,128)(2,1)S(1)}, u32[]{:S(2)}, u32[]{:S(2)}) collective-permute-start(bf16[96,2048]{1,0:T(8,128)(2,1)} %collective-permute-done.14.rest_3_), channel_id=1, source_target_pairs={{0,1},{1,0},{2,3},{3,2},{4,5},{5,4},{6,7},{7,6},{8,9},{9,8},{10,11... | collective-permute-start | bytes 1179656 | tf_op jit(solution)/shard_map/ppermute | solution.py:27
  59.7 1.9 %collective-permute-start.15 = (bf16[96,2048]{1,0:T(8,128)(2,1)S(1)}, bf16[96,2048]{1,0:T(8,128)(2,1)S(1)}, u32[]{:S(2)}, u32[]{:S(2)}) collective-permute-start(bf16[96,2048]{1,0:T(8,128)(2,1)S(1)} %slice_select_fusion), channel_id=1, source_target_pairs={{0,1},{1,0},{2,3},{3,2},{4,5},{5,4},{6,7},{7,6},{8,9},{9,8},{10,11... | collective-permute-start | bytes 1179656 | tf_op jit(solution)/shard_map/ppermute | solution.py:27
